TPU v7x, 32 devices: a whole 2x2x4 slice. The times are simulated.
32 devices in a mesh: cuts: 2 (over y), wide: 8 (over z, x), narrow: 2 (over core).
Axes of the slice: x: 2, y: 2, z: 4, core: 2. Of those that a mesh axis runs over, the one named last changes fastest.
Arguments:
- stem_tensor: float32 [2, 4194304], P(None, ('cuts', 'wide', 'narrow')), parts along dimension 1, may hold values from -6 to 6
- sub_branches: bfloat16 [3, 2, 2, 512, 512], P(None, 'narrow', None, 'wide'), may hold values from -0.1875 to 0.1875
- branch_bits: int32 [3, 9], replicated, may hold values from 7 to 20, as said below
Outputs:
- amplitudes: float32 [2, 4194304], P(None, ('cuts', 'wide', 'narrow')), parts along dimension 1
There are 2 independent parts, one for each index of `cuts`. A program takes and returns all parts, laid end to end along the dimension named above; an argument that names none is the same for every part. Nothing has to cross between parts.
Inputs may be any that keep to these rules, and one draw needn't show every extreme that they name: `branch_bits`: no bit below 7 is ever named. Row 0 holds 9 distinct bits of 7 to 16, bit 7 among them. Row 1 holds the 3 bits 17 + 1 to 20 and 6 distinct bits of 7 to 12. Row 2 holds bit 17 and 8 distinct bits of 7 to 12 and 18 to 20. Each row in any order.
All inputs are finite; a program needn't handle non-finite values.
Results may differ from a plain program's by a relative error of at most 0.005.
Values may be sent and summed in bfloat16 or wider, within the bound.
No kernel may reach another device: no remote copies, remote signals or barrier semaphores. Data moves between devices by JAX's collectives and lax.ppermute only.
A program may use at most 64 MiB of HBM per device.

v0:
```python
import jax
import jax.numpy as jnp
from jax import lax
from jax.sharding import PartitionSpec as P

LBITS = 17
BBITS = 9
BRANCHES = 3


lane_bits = 7


def partner(value, axis, stride):
    mask = 2**stride
    pairs = [(source, source ^ mask) for source in range(lax.axis_size(axis))]
    return lax.ppermute(value, axis, pairs)


def bit_tables(chosen_bits, total_bits, width_bits):
    places = jnp.arange(total_bits, dtype=jnp.int32)
    orders = jnp.arange(width_bits, dtype=jnp.int32)
    matches = places[:, None] == chosen_bits[None, :]
    chosen = jnp.any(matches, axis=1)
    ranking = jnp.sum(jnp.where(matches, orders[None, :], 0), axis=1)
    unchosen = 1 - chosen.astype(jnp.int32)
    free_rank = jnp.cumsum(unchosen) - unchosen
    unit_ones = jnp.ones((total_bits,), jnp.int32)
    weight = jnp.where(
        chosen,
        jnp.left_shift(unit_ones, width_bits - 1 - ranking),
        jnp.left_shift(unit_ones, width_bits + free_rank),
    )
    low_bits = total_bits // 2

    def partial_table(count, first_place, last_place):
        values = jnp.arange(count, dtype=jnp.int32)
        running = jnp.zeros((count,), jnp.int32)
        for position in range(first_place, last_place):
            running = (
                running
                + jnp.bitwise_and(jnp.right_shift(values, position - first_place), 1)
                * weight[position]
            )
        return running

    inverse = (
        partial_table(2 ** (total_bits - low_bits), low_bits, total_bits)[:, None]
        + partial_table(2**low_bits, 0, low_bits)[None, :]
    ).reshape(-1)
    columns = jnp.arange(2**width_bits, dtype=jnp.int32)
    col_part = jnp.zeros((2**width_bits,), jnp.int32)
    for slot_no in range(width_bits):
        col_part = col_part + jnp.left_shift(
            jnp.bitwise_and(jnp.right_shift(columns, width_bits - 1 - slot_no), 1),
            chosen_bits[slot_no],
        )
    row_ids = jnp.arange(2 ** (total_bits - width_bits), dtype=jnp.int32)
    row_part = jnp.zeros((2 ** (total_bits - width_bits),), jnp.int32)
    for position in range(total_bits):
        bit_value = jnp.bitwise_and(jnp.right_shift(row_ids, free_rank[position]), 1) * 2**position
        row_part = row_part + jnp.where(chosen[position], 0, bit_value)
    gather_index = row_part[:, None] + col_part[None, :]
    return (gather_index, inverse)


def half_product(first_matrix, second_matrix):
    return jnp.dot(first_matrix, second_matrix, preferred_element_type=jnp.float32)


def merge_branch(left_factor, right_factor):
    real_part = half_product(left_factor[0], right_factor[0]) - half_product(
        left_factor[1], right_factor[1]
    )
    imag_part = half_product(left_factor[0], right_factor[1]) + half_product(
        left_factor[1], right_factor[0]
    )
    return jnp.stack([real_part, imag_part]).astype(jnp.bfloat16)


def contract_blocks(amplitude, branch, gather_index, inverse):
    lanes = 2**lane_bits
    blocks = amplitude.reshape(2, -1, lanes)
    picked = jnp.take(blocks, gather_index, axis=1)
    widened = branch.astype(jnp.float32)

    def real_product(data, matrix):
        return jnp.einsum(
            "rul,cu->rcl",
            data,
            matrix,
            precision=lax.Precision.HIGHEST,
            preferred_element_type=jnp.float32,
        )

    real_part = real_product(picked[0], widened[0]) - real_product(picked[1], widened[1])
    imag_part = real_product(picked[0], widened[1]) + real_product(picked[1], widened[0])
    merged = jnp.stack([real_part, imag_part]).reshape(2, -1, lanes)
    return jnp.take(merged, inverse, axis=1).reshape(2, -1)


def shards(stem_tensor, sub_branches, branch_bits):
    wide_count = lax.axis_size("wide")
    wide_log = wide_count.bit_length() - 1
    local_bits = LBITS
    block_shape = (2, wide_count, 2, stem_tensor.shape[1] // (2 * wide_count))
    leading = lax.axis_index("narrow") == 0

    def move_wide(amplitude):
        return lax.all_to_all(
            amplitude.reshape(block_shape), "wide", split_axis=1, concat_axis=1, tiled=True
        ).reshape(2, -1)

    def move_narrow(amplitude):
        return lax.all_to_all(
            amplitude.reshape(block_shape), "narrow", split_axis=2, concat_axis=2, tiled=True
        ).reshape(2, -1)

    def working_places(which):
        chosen_bits = branch_bits[which]
        if which == 0:
            return chosen_bits - lane_bits
        shifted = jnp.where(chosen_bits == local_bits, local_bits - wide_log - 1, chosen_bits)
        placed = jnp.where(chosen_bits > local_bits, chosen_bits - wide_log - 1, shifted)
        return placed - lane_bits

    amplitude = stem_tensor
    for which in range(BRANCHES):
        own_rows = sub_branches[which, 0]
        own_whole = lax.all_gather(own_rows, "wide", axis=1, tiled=True)
        partner_whole = partner(own_whole, "narrow", 0)
        branch = merge_branch(
            jnp.where(leading, own_whole, partner_whole),
            jnp.where(leading, partner_whole, own_whole),
        )
        if which == 1:
            amplitude = move_wide(amplitude)
        if which == 2:
            amplitude = move_narrow(amplitude)
        gather_index, inverse = bit_tables(working_places(which), local_bits - lane_bits, BBITS)
        amplitude = contract_blocks(amplitude, branch, gather_index, inverse)
    amplitude = move_narrow(amplitude)
    amplitude = move_wide(amplitude)
    return amplitude


def solution(mesh):
    in_specs = (P(None, ("cuts", "wide", "narrow")), P(None, "narrow", None, "wide", None), P())
    out_specs = P(None, ("cuts", "wide", "narrow"))
    return jax.shard_map(shards, mesh=mesh, in_specs=in_specs, out_specs=out_specs, check_vma=False)
```

profile of v0, /device:TPU:0, one launch (start us, length us, event | category | flops | bytes accessed | tf_op | source)
XLA Modules:
  0.0 283.7 jit_solution(12411207935728170080)
XLA Ops:
  6.5 1.9 fusion.70
  8.5 0.7 all-gather.11.cloned.1.call-update
  12.4 5.5 %shift-left_add_fusion.2 = s32[512]{0:T(512)S(1)} fusion(s32[]{:T(128)} %bitcast.145, s32[]{:T(128)} %bitcast.144, s32[]{:T(128)} %bitcast.143, s32[]{:T(128)} %bitcast.142, s32[]{:T(128)} %bitcast.141, s32[]{:T(128)} %bitcast.140, s32[]{:T(128)} %bitcast.139, s32[]{:T(128)} %bitcast.138, s32[]{:T(128)} %bitcast.137), kind=kLoop, calls=%fused_computation.114 | loop fusion | flops 17920 | bytes 2084 | tf_op jit(solution)/shard_map/add | solution.py:54
  17.9 12.4 %fusion.41 = s32[2]{0:T(128)S(1)} fusion(pred[]{:T(512)} %bitcast.131, pred[]{:T(512)} %bitcast.133, pred[]{:T(512)} %bitcast.135, pred[]{:T(512)} %bitcast.129, pred[]{:T(512)} %bitcast.127, pred[]{:T(512)} %bitcast.125, pred[]{:T(512)} %bitcast.123, pred[]{:T(512)} %bitcast.121, pred[]{:T(512)} %bitcast.119, pred[]{:T(512)} %bitcast.117, s32[]{:T(128)} %bitcast.136, ...), kind=kLoop, calls=%fused_computation.166 | loop fusion | flops 96 | bytes 58 | tf_op jit(solution)/shard_map/add | solution.py:62
  31.2 6.2 %multiply_add_fusion.4 = (s32[32]{0:T(128)S(1)}, s32[32]{0:T(128)S(1)}) fusion(s32[]{:T(128)} %bitcast.110, s32[]{:T(128)} %bitcast.109, s32[]{:T(128)} %bitcast.108, s32[]{:T(128)} %bitcast.107, s32[]{:T(128)} %bitcast.106, s32[]{:T(128)} %bitcast.105, s32[]{:T(128)} %bitcast.104, s32[]{:T(128)} %bitcast.103, s32[]{:T(128)} %bitcast.102, s32[]{:T(128)} %bitcast.101), kind=kLoop, calls=%fused_computation.204 | loop fusion | flops 896 | bytes 296 | tf_op jit(solution)/shard_map/add | solution.py:41
  37.8 0.7 fusion.77
  40.7 3.1 %multiply_add_fusion.2 = s32[32]{0:T(128)S(1)} fusion(s32[]{:T(128)} %bitcast.61, s32[]{:T(128)} %bitcast.60, s32[]{:T(128)} %bitcast.59, s32[]{:T(128)} %bitcast.58, s32[]{:T(128)} %bitcast.57), kind=kLoop, calls=%fused_computation.199 | loop fusion | flops 608 | bytes 148 | tf_op jit(solution)/shard_map/add | solution.py:41
  43.8 3.1 %multiply_add_fusion.3 = s32[32]{0:T(128)S(1)} fusion(s32[]{:T(128)} %bitcast.56, s32[]{:T(128)} %bitcast.55, s32[]{:T(128)} %bitcast.54, s32[]{:T(128)} %bitcast.53, s32[]{:T(128)} %bitcast.52), kind=kLoop, calls=%fused_computation.200 | loop fusion | flops 608 | bytes 148 | tf_op jit(solution)/shard_map/add | solution.py:41
  48.7 3.1 %multiply_add_fusion = s32[32]{0:T(128)S(1)} fusion(s32[]{:T(128)} %bitcast.12, s32[]{:T(128)} %bitcast.11, s32[]{:T(128)} %bitcast.10, s32[]{:T(128)} %bitcast.9, s32[]{:T(128)} %bitcast.8), kind=kLoop, calls=%fused_computation.194 | loop fusion | flops 608 | bytes 148 | tf_op jit(solution)/shard_map/add | solution.py:41
  51.8 3.1 %multiply_add_fusion.1 = s32[32]{0:T(128)S(1)} fusion(s32[]{:T(128)} %bitcast.7, s32[]{:T(128)} %bitcast.6, s32[]{:T(128)} %bitcast.5, s32[]{:T(128)} %bitcast.4, s32[]{:T(128)} %bitcast.3), kind=kLoop, calls=%fused_computation.195 | loop fusion | flops 608 | bytes 148 | tf_op jit(solution)/shard_map/add | solution.py:41
  55.0 0.7 fusion.74
  55.8 5.7 %shift-left_add_fusion.1 = s32[512]{0:T(512)S(1)} fusion(s32[]{:T(128)} %bitcast.97, s32[]{:T(128)} %bitcast.96, s32[]{:T(128)} %bitcast.95, s32[]{:T(128)} %bitcast.94, s32[]{:T(128)} %bitcast.93, s32[]{:T(128)} %bitcast.92, s32[]{:T(128)} %bitcast.91, s32[]{:T(128)} %bitcast.90, s32[]{:T(128)} %bitcast.89), kind=kLoop, calls=%fused_computation.113 | loop fusion | flops 17920 | bytes 2084 | tf_op jit(solution)/shard_map/add | solution.py:54
  61.5 12.4 %fusion.50 = s32[2]{0:T(128)S(1)} fusion(pred[]{:T(512)} %bitcast.82, pred[]{:T(512)} %bitcast.84, pred[]{:T(512)} %bitcast.86, pred[]{:T(512)} %bitcast.80, pred[]{:T(512)} %bitcast.78, pred[]{:T(512)} %bitcast.76, pred[]{:T(512)} %bitcast.74, pred[]{:T(512)} %bitcast.72, pred[]{:T(512)} %bitcast.70, pred[]{:T(512)} %bitcast.68, s32[]{:T(128)} %bitcast.87, ...), kind=kLoop, calls=%fused_computation.175 | loop fusion | flops 96 | bytes 58 | tf_op jit(solution)/shard_map/add | solution.py:62
  73.9 5.6 %shift-left_add_fusion = s32[512]{0:T(512)S(1)} fusion(s32[]{:T(128)} %bitcast.48, s32[]{:T(128)} %bitcast.47, s32[]{:T(128)} %bitcast.46, s32[]{:T(128)} %bitcast.45, s32[]{:T(128)} %bitcast.44, s32[]{:T(128)} %bitcast.43, s32[]{:T(128)} %bitcast.42, s32[]{:T(128)} %bitcast.41, s32[]{:T(128)} %bitcast.40), kind=kLoop, calls=%fused_computation.112 | loop fusion | flops 17920 | bytes 2084 | tf_op jit(solution)/shard_map/add | solution.py:54
  79.6 12.4 %fusion.59 = s32[2]{0:T(128)S(1)} fusion(pred[]{:T(512)} %bitcast.33, pred[]{:T(512)} %bitcast.35, pred[]{:T(512)} %bitcast.37, pred[]{:T(512)} %bitcast.31, pred[]{:T(512)} %bitcast.29, pred[]{:T(512)} %bitcast.27, pred[]{:T(512)} %bitcast.25, pred[]{:T(512)} %bitcast.23, pred[]{:T(512)} %bitcast.21, pred[]{:T(512)} %bitcast.19, s32[]{:T(128)} %bitcast.38, ...), kind=kLoop, calls=%fused_computation.184 | loop fusion | flops 96 | bytes 58 | tf_op jit(solution)/shard_map/add | solution.py:62
  92.7 1.0 all-gather.11.cloned.1.call-done
  93.8 3.5 %gather_fusion = f32[1024,2,128]{2,1,0:T(2,128)S(1)} fusion(f32[2,1024,128]{2,0,1:T(2,128)S(1)} %bitcast.311, s32[1024]{0:T(1024)S(1)} %broadcast_clamp_fusion.2), kind=kCustom, calls=%fused_computation.clone | custom fusion | bytes 2101248 | tf_op jit(solution)/shard_map/jit(_take)/gather | solution.py:84
  97.7 37.2 %all-gather.7.cloned.1.call-done = bf16[1,1,2,512,512]{4,3,2,1,0:T(8,128)(2,1)} async-done(((bf16[1,1,2,64,512]{4,3,2,1,0:T(8,128)(2,1)}), bf16[1,1,2,512,512]{4,3,2,1,0:T(8,128)(2,1)}) %all-gather.7.cloned.1.call-update) | async-done | bytes 1048592 | tf_op jit(solution)/shard_map/all_gather | solution.py:130
  134.9 2.5 broadcast_select_fusion.1
  141.7 0.9 pad_maximum_fusion
  142.7 7.5 %gather_fusion.1 = f32[1024,2,128]{2,1,0:T(2,128)} fusion(f32[2,1024,128]{2,0,1:T(2,128)S(1)} %pad_maximum_fusion, s32[1024]{0:T(1024)S(1)} %fusion.27), kind=kCustom, calls=%fused_computation.1.clone | custom fusion | bytes 2101248 | tf_op jit(solution)/shard_map/jit(_take)/gather | solution.py:99
  150.2 5.3 %select_bitcast_fusion.4 = f32[2,1024,128]{2,0,1:T(2,128)S(1)} fusion(f32[1024,2,128]{2,1,0:T(2,128)} %gather_fusion.1, pred[1024]{0:T(1024)(128)(4,1)S(1)} %compare_and_fusion.5), kind=kLoop, calls=%fused_computation.37 | loop fusion | flops 262144 | bytes 2098176 | tf_op jit(solution)/shard_map/jit(_take)/select_n | solution.py:99
  155.6 1.6 reshape_reshape.15
  157.2 2.3 copy.72
  159.4 4.4 %all-to-all-start = ((f32[2,8,2,8192]{3,2,0,1:T(2,128)}), f32[2,8,2,8192]{3,2,0,1:T(2,128)}, u32[]{:S(2)}, u32[]{:S(2)}) async-start(f32[2,8,2,8192]{3,2,0,1:T(2,128)} %copy.72), calls=%async_computation | async-start | bytes 2097152 | tf_op jit(solution)/shard_map/all_to_all | solution.py:110
  165.7 0.8 copy-done.2
  166.4 1.4 broadcast_select_fusion.5
  169.6 20.9 %all-to-all-done = f32[2,8,2,8192]{3,2,0,1:T(2,128)} async-done(((f32[2,8,2,8192]{3,2,0,1:T(2,128)}), f32[2,8,2,8192]{3,2,0,1:T(2,128)}, u32[]{:S(2)}, u32[]{:S(2)}) %all-to-all-start) | async-done | bytes 1048608 | tf_op jit(solution)/shard_map/all_to_all | solution.py:110
  190.4 1.3 copy.73
  191.7 1.9 reshape_reshape.16
  193.6 2.0 copy.74
  195.6 7.5 %gather_fusion.2 = f32[1024,2,128]{2,1,0:T(2,128)} fusion(f32[2,1024,128]{2,0,1:T(2,128)S(1)} %copy.74, s32[1024]{0:T(1024)S(1)} %broadcast_clamp_fusion.1), kind=kCustom, calls=%fused_computation.2.clone | custom fusion | bytes 2101248 | tf_op jit(solution)/shard_map/jit(_take)/gather | solution.py:84
  203.1 1.3 copy.75
  207.3 0.9 pad_maximum_fusion.1
  208.2 3.5 %gather_fusion.3 = f32[1024,2,128]{2,1,0:T(2,128)S(1)} fusion(f32[2,1024,128]{2,0,1:T(2,128)S(1)} %pad_maximum_fusion.1, s32[1024]{0:T(1024)S(1)} %fusion.28), kind=kCustom, calls=%fused_computation.4.clone | custom fusion | bytes 2101248 | tf_op jit(solution)/shard_map/jit(_take)/gather | solution.py:99
  211.8 3.7 %select_bitcast_fusion.2 = f32[2,1024,128]{2,0,1:T(2,128)S(1)} fusion(f32[1024,2,128]{2,1,0:T(2,128)S(1)} %gather_fusion.3, pred[1024]{0:T(1024)(128)(4,1)S(1)} %compare_and_fusion.4), kind=kLoop, calls=%fused_computation.35 | loop fusion | flops 262144 | bytes 2098176 | tf_op jit(solution)/shard_map/jit(_take)/select_n | solution.py:99
  216.8 4.6 %all_to_all.20 = f32[2,8,2,8192]{3,1,0,2:T(8,128)S(1)} all-to-all(f32[2,8,2,8192]{3,1,0,2:T(8,128)S(1)} %copy.79), channel_id=1, replica_groups=mesh['cuts'=2,'wide'=8,'narrow'=2] {'narrow'}, dimensions={2} | all-to-all | bytes 2097152 | tf_op jit(solution)/shard_map/all_to_all | solution.py:115
  221.4 0.8 copy.80
  222.2 0.9 reshape_reshape.18
  223.1 0.8 copy.81
  223.9 3.6 %gather_fusion.4 = f32[1024,2,128]{2,1,0:T(2,128)S(1)} fusion(f32[2,1024,128]{2,0,1:T(2,128)S(1)} %copy.81, s32[1024]{0:T(1024)S(1)} %broadcast_clamp_fusion), kind=kCustom, calls=%fused_computation.3.clone | custom fusion | bytes 2101248 | tf_op jit(solution)/shard_map/jit(_take)/gather | solution.py:84
  230.4 0.9 pad_maximum_fusion.2
  231.4 3.6 %gather_fusion.5 = f32[1024,2,128]{2,1,0:T(2,128)S(1)} fusion(f32[2,1024,128]{2,0,1:T(2,128)S(1)} %pad_maximum_fusion.2, s32[1024]{0:T(1024)S(1)} %fusion.29), kind=kCustom, calls=%fused_computation.5.clone | custom fusion | bytes 2101248 | tf_op jit(solution)/shard_map/jit(_take)/gather | solution.py:99
  234.9 3.7 %select_bitcast_fusion = f32[2,1024,128]{2,0,1:T(2,128)S(1)} fusion(f32[1024,2,128]{2,1,0:T(2,128)S(1)} %gather_fusion.5, pred[1024]{0:T(1024)(128)(4,1)S(1)} %compare_and_fusion.3), kind=kLoop, calls=%fused_computation.33 | loop fusion | flops 262144 | bytes 2098176 | tf_op jit(solution)/shard_map/jit(_take)/select_n | solution.py:99
  240.0 4.6 %all_to_all.21 = f32[2,8,2,8192]{3,1,0,2:T(8,128)S(1)} all-to-all(f32[2,8,2,8192]{3,1,0,2:T(8,128)S(1)} %copy.86), channel_id=1, replica_groups=mesh['cuts'=2,'wide'=8,'narrow'=2] {'narrow'}, dimensions={2} | all-to-all | bytes 2097152 | tf_op jit(solution)/shard_map/all_to_all | solution.py:115
  244.5 0.8 copy.87
  245.4 29.4 %all_to_all.22 = f32[2,8,2,8192]{3,2,0,1:T(2,128)S(1)} all-to-all(f32[2,8,2,8192]{3,2,0,1:T(2,128)S(1)} %copy.87), channel_id=1, replica_groups=mesh['cuts'=2,'wide'=8,'narrow'=2] {'wide'}, dimensions={1} | all-to-all | bytes 2097152 | tf_op jit(solution)/shard_map/all_to_all | solution.py:110
  274.9 2.2 reshape.532
  (104 shorter events, 26.0 us)
Async XLA Ops:
  6.5 87.2 %copy-start = (f32[2,131072]{1,0:T(2,128)S(1)}, f32[2,131072]{1,0:T(2,128)}, u32[]{:S(2)}) copy-start(f32[2,131072]{1,0:T(2,128)} %param.7) | copy-start | bytes 3145732
  6.5 85.6 %all-gather.9.cloned.1.call-start = ((), (), s32[]{:S(2)}) async-start(), calls=%async_computation.5 | async-start | bytes 1179648 | tf_op jit(solution)/shard_map/all_gather | solution.py:130
  8.4 85.3 %all-gather.11.cloned.1.call-start = ((), (), s32[]{:S(2)}) async-start(), calls=%async_computation.6 | async-start | bytes 1179648 | tf_op jit(solution)/shard_map/all_gather | solution.py:130
  9.2 125.7 %all-gather.7.cloned.1.call-start = ((), (), s32[]{:S(2)}) async-start(), calls=%async_computation.4 | async-start | bytes 1179648 | tf_op jit(solution)/shard_map/all_gather | solution.py:130
  9.2 0.7 copy-start.3
  92.2 42.7 %collective-permute-start.1 = (bf16[2,512,512]{2,1,0:T(8,128)(2,1)}, bf16[2,512,512]{2,1,0:T(8,128)(2,1)}, u32[]{:S(2)}, u32[]{:S(2)}) collective-permute-start(bf16[2,512,512]{2,1,0:T(8,128)(2,1)} %bitcast.322), channel_id=1, source_target_pairs={{0,1},{1,0},{2,3},{3,2},{4,5},{5,4},{6,7},{7,6},{8,9},{9,8},{10,11... | collective-permute-start | bytes 3145736 | tf_op jit(solution)/shard_map/ppermute | solution.py:17
  93.7 41.2 %collective-permute-start.2 = (bf16[2,512,512]{2,1,0:T(8,128)(2,1)}, bf16[2,512,512]{2,1,0:T(8,128)(2,1)}, u32[]{:S(2)}, u32[]{:S(2)}) collective-permute-start(bf16[2,512,512]{2,1,0:T(8,128)(2,1)} %bitcast.323), channel_id=1, source_target_pairs={{0,1},{1,0},{2,3},{3,2},{4,5},{5,4},{6,7},{7,6},{8,9},{9,8},{10,11... | collective-permute-start | bytes 3145736 | tf_op jit(solution)/shard_map/ppermute | solution.py:17
  134.9 30.8 %collective-permute-start = (bf16[2,512,512]{2,1,0:T(8,128)(2,1)}, bf16[2,512,512]{2,1,0:T(8,128)(2,1)}, u32[]{:S(2)}, u32[]{:S(2)}) collective-permute-start(bf16[2,512,512]{2,1,0:T(8,128)(2,1)} %bitcast.321), channel_id=1, source_target_pairs={{0,1},{1,0},{2,3},{3,2},{4,5},{5,4},{6,7},{7,6},{8,9},{9,8},{10,11... | collective-permute-start | bytes 3145736 | tf_op jit(solution)/shard_map/ppermute | solution.py:17
  159.4 31.0 %all-to-all-start = ((f32[2,8,2,8192]{3,2,0,1:T(2,128)}), f32[2,8,2,8192]{3,2,0,1:T(2,128)}, u32[]{:S(2)}, u32[]{:S(2)}) async-start(f32[2,8,2,8192]{3,2,0,1:T(2,128)} %copy.72), calls=%async_computation | async-start | bytes 2097152 | tf_op jit(solution)/shard_map/all_to_all | solution.py:110
  165.2 1.2 copy-start.2
  274.8 2.3 copy-start.1
Sparse Core Ops, SparseCore 0:
  9.5 42.8 all-gather.8
  54.7 38.9 all-gather.10
  95.9 38.9 all-gather.6
where the time goes:
time: 285 us; the launch traced here: 284 us
  other arithmetic  94.5 us (33%)
  waiting for transfers between devices  60.4 us (21%)
  local copies, waits for them, and re-layouts  58.4 us (20%)
  blocking collectives  38.6 us (14%)
  between operations  13.7 us (5%)
  matrix products  13 us (5%)
  starting transfers between devices  5.02 us (2%)
    all_gather x3, waiting for transfers between devices, shards(): own_whole = lax.all_gather(own_rows, 'wide', axis=1, tiled=True)  38.2 us
    add x3, other arithmetic, bit_tables(): row_part = row_part + jnp.where(chosen[position], 0, bit_value)  37.2 us
    all_to_all x1, blocking collectives, move_wide(): lax.all_to_all(amplitude.reshape(block_shape), 'wide', split_axis=1, conc...  29.4 us
    all_to_all x1, waiting for transfers between devices, move_wide(): lax.all_to_all(amplitude.reshape(block_shape), 'wide', split_axis=1, conc...  20.9 us
    add x5, other arithmetic, partial_table(): running + jnp.bitwise_and(jnp.right_shift(values, position - first_place)...  18.6 us
    add x3, other arithmetic, bit_tables(): col_part + jnp.left_shift(jnp.bitwise_and(jnp.right_shift(columns, width_...  16.9 us
    gather x6, local copies, waits for them, and re-layouts, contract_blocks(): picked = jnp.take(blocks, gather_index, axis=1)  16.1 us
    gather x3, local copies, waits for them, and re-layouts, contract_blocks(): return jnp.take(merged, inverse, axis=1).reshape(2, -1)  14.6 us
  transfers between devices with their start and end apart: 7, of which 3 were waited for; matrix products, arithmetic and copies ran while one was open for 41% of the time, Pallas kernels for 0%

commit v1 on v0

v1 whole, which is shorter than its diff:
```python
import functools

import jax
import jax.numpy as jnp
from jax import lax
from jax.experimental import pallas as pl
from jax.experimental.pallas import tpu as pltpu
from jax.sharding import PartitionSpec as P

lane_bits = 7
lanes = 2**lane_bits
vmem_budget = 48 * 2**20


def log2(size):
    return size.bit_length() - 1


def exchange(value, axis, mask):
    pairs = [(source, source ^ mask) for source in range(lax.axis_size(axis))]
    return lax.ppermute(value, axis, pairs)


def on_vmem():
    return pl.BlockSpec(memory_space=pltpu.VMEM)


def on_smem():
    return pl.BlockSpec(memory_space=pltpu.SMEM)


def params():
    return pltpu.CompilerParams(vmem_limit_bytes=vmem_budget)


def merge_kernel(blocks, block_rows, place_ref, own_ref, other_ref, branch_ref, factors):
    width = own_ref.shape[1]
    wide, cuts, narrow = place_ref[0], place_ref[1], place_ref[2]
    for source, slot in ((own_ref, narrow), (other_ref, 1 - narrow)):
        for number, (wide_mask, part_mask) in enumerate(blocks):
            if wide_mask is None:
                start = (slot * 2 + part_mask) * width
            else:
                part = jnp.bitwise_xor(cuts, part_mask)
                start = (slot * 2 + part) * width + jnp.bitwise_xor(wide, wide_mask) * block_rows
            start = pl.multiple_of(start, block_rows)
            factors[pl.ds(start, block_rows), :] = source[
                number * block_rows : (number + 1) * block_rows, :
            ]
    chunk = min(256, width)

    def dot(left, right):
        return jnp.dot(left, right, preferred_element_type=jnp.float32)

    second_real = factors[2 * width : 3 * width, :]
    second_imag = factors[3 * width : 4 * width, :]
    for row in range(0, width, chunk):
        first_real = factors[row : row + chunk, :]
        first_imag = factors[width + row : width + row + chunk, :]
        real = dot(first_real, second_real) - dot(first_imag, second_imag)
        imag = dot(first_real, second_imag) + dot(first_imag, second_real)
        branch_ref[row : row + chunk, :] = real.astype(jnp.bfloat16)
        branch_ref[width + row : width + row + chunk, :] = imag.astype(jnp.bfloat16)


def merge(place, own, other, blocks, block_rows):
    width = own.shape[1]
    return pl.pallas_call(
        functools.partial(merge_kernel, blocks, block_rows),
        out_shape=jax.ShapeDtypeStruct((2 * width, width), jnp.bfloat16),
        in_specs=[on_smem(), on_vmem(), on_vmem()],
        out_specs=on_vmem(),
        scratch_shapes=[pltpu.VMEM((4 * width, width), jnp.bfloat16)],
        compiler_params=params(),
        cost_estimate=pl.CostEstimate(
            flops=8 * width**3, bytes_accessed=12 * width**2, transcendentals=0
        ),
        name="merge",
    )(place, own, other)


def bit_of(values, position):
    return jnp.bitwise_and(jnp.right_shift(values, position), 1)


def apply_kernel(interleaved, bits_ref, amplitude_ref, branch_ref, out_ref, sorted_ref, product_ref):
    width = branch_ref.shape[1]
    rows = 2 * width
    order = log2(width)
    chosen = [bits_ref[k] for k in range(order)]
    free = order * (order + 1) // 2 - sum(chosen)
    index = lax.broadcasted_iota(jnp.int32, (1, rows), 1)
    to_sorted = jnp.left_shift(bit_of(index, free), order)
    to_plain = jnp.left_shift(bit_of(index, order), free)
    for k in range(order):
        to_sorted += jnp.left_shift(bit_of(index, chosen[k]), order - 1 - k)
        to_plain += jnp.left_shift(bit_of(index, order - 1 - k), chosen[k])

    if interleaved:
        amplitude = jnp.concatenate(
            [
                amplitude_ref[pl.ds(0, rows, stride=2), :].astype(jnp.bfloat16),
                amplitude_ref[pl.ds(1, rows, stride=2), :].astype(jnp.bfloat16),
            ],
            axis=1,
        )
    else:
        amplitude = amplitude_ref[...]

    def dot(left, right):
        return jnp.dot(left, right, preferred_element_type=jnp.float32)

    def selector(target, first, count):
        row = lax.broadcasted_iota(jnp.int32, (count, rows), 0) + first
        return jnp.where(row == target, 1.0, 0.0).astype(jnp.bfloat16)

    chunk = 256
    for first in range(0, rows, chunk):
        picked = dot(selector(to_sorted, first, chunk), amplitude).astype(jnp.bfloat16)
        half, row = divmod(first, width)
        sorted_ref[row : row + chunk, half * 2 * lanes : (half + 1) * 2 * lanes] = picked
    for row in range(0, width, chunk):
        by_real = dot(branch_ref[row : row + chunk, :], sorted_ref[...])
        by_imag = dot(branch_ref[width + row : width + row + chunk, :], sorted_ref[...])
        for half in range(2):
            at = half * 2 * lanes
            real = by_real[:, at : at + lanes] - by_imag[:, at + lanes : at + 2 * lanes]
            imag = by_real[:, at + lanes : at + 2 * lanes] + by_imag[:, at : at + lanes]
            to = half * width + row
            product_ref[to : to + chunk, :lanes] = real.astype(jnp.bfloat16)
            product_ref[to : to + chunk, lanes:] = imag.astype(jnp.bfloat16)
    for first in range(0, rows, chunk):
        out_ref[first : first + chunk, :] = dot(
            selector(to_plain, first, chunk), product_ref[...]
        ).astype(jnp.bfloat16)


def apply(bits, amplitude, branch, interleaved):
    width = branch.shape[1]
    rows = 2 * width
    return pl.pallas_call(
        functools.partial(apply_kernel, interleaved),
        out_shape=jax.ShapeDtypeStruct((rows, 2 * lanes), jnp.bfloat16),
        in_specs=[on_smem(), on_vmem(), on_vmem()],
        out_specs=on_vmem(),
        scratch_shapes=[
            pltpu.VMEM((width, 4 * lanes), jnp.bfloat16),
            pltpu.VMEM((rows, 2 * lanes), jnp.bfloat16),
        ],
        compiler_params=params(),
        cost_estimate=pl.CostEstimate(
            flops=6 * rows * rows * 2 * lanes, bytes_accessed=2**22, transcendentals=0
        ),
        name="contract",
    )(bits, amplitude, branch)


def widen_kernel(amplitude_ref, out_ref):
    rows = amplitude_ref.shape[0]
    wide = amplitude_ref[...].astype(jnp.float32)
    out_ref[pl.ds(0, rows, stride=2), :] = wide[:, :lanes]
    out_ref[pl.ds(1, rows, stride=2), :] = wide[:, lanes:]


def widen(amplitude):
    rows = amplitude.shape[0]
    return pl.pallas_call(
        widen_kernel,
        out_shape=jax.ShapeDtypeStruct((2 * rows, lanes), jnp.float32),
        in_specs=[on_vmem()],
        out_specs=on_vmem(),
        compiler_params=params(),
        name="widen",
    )(amplitude)


def gather_factors(sub_branch):
    rows = sub_branch.shape[1]
    if rows % 16 or lax.axis_size("cuts") != 2 or lax.axis_size("wide") < 4:
        own = lax.all_gather(sub_branch, "wide", axis=1, tiled=True)
        own = own.reshape(-1, own.shape[-1])
        return own, exchange(own, "narrow", 1), [(None, 0), (None, 1)], own.shape[0] // 2
    part = lax.axis_index("cuts")
    mine = lax.dynamic_index_in_dim(sub_branch, part, axis=0, keepdims=False)
    masks = [0]
    for bit in reversed(range(1, log2(lax.axis_size("wide")))):
        mine = jnp.concatenate([mine, exchange(mine, "wide", 2**bit)])
        masks = masks + [mask ^ 2**bit for mask in masks]
    half = mine.shape[0] // 2
    first, second = mine[:half], mine[half:]
    first_masks, second_masks = masks[: len(masks) // 2], masks[len(masks) // 2 :]
    first = jnp.concatenate([first, exchange(first, "wide", 1)])
    second = jnp.concatenate([second, exchange(second, "cuts", 1)])
    first_blocks = [(mask, 0) for mask in first_masks] + [(mask ^ 1, 0) for mask in first_masks]
    second_blocks = [(mask, 0) for mask in second_masks] + [(mask, 1) for mask in second_masks]
    own = jnp.concatenate(
        [first, exchange(first, "cuts", 1), second, exchange(second, "wide", 1)]
    )
    blocks = (
        first_blocks
        + [(mask, part ^ 1) for mask, part in first_blocks]
        + second_blocks
        + [(mask ^ 1, part) for mask, part in second_blocks]
    )
    return own, exchange(own, "narrow", 1), blocks, rows


def shards(stem_tensor, sub_branches, branch_bits):
    wide_count, narrow_count = lax.axis_size("wide"), lax.axis_size("narrow")
    local_bits = log2(stem_tensor.shape[1])
    branches, width = sub_branches.shape[0], sub_branches.shape[-1]
    rows = stem_tensor.shape[1] // lanes
    devices = wide_count * narrow_count
    low_bits = log2(rows // devices)
    place = jnp.stack([lax.axis_index(axis) for axis in ("wide", "cuts", "narrow")]).astype(
        jnp.int32
    )
    swapped = jnp.where(
        branch_bits < local_bits, branch_bits - lane_bits, branch_bits - local_bits + low_bits
    )
    positions = [branch_bits[0] - lane_bits] + [swapped[which] for which in range(1, branches)]

    def swap(amplitude):
        blocks = amplitude.reshape(devices, rows // devices, 2 * lanes)
        return lax.all_to_all(blocks, ("wide", "narrow"), 0, 0, tiled=True).reshape(rows, 2 * lanes)

    amplitude = (
        stem_tensor.reshape(2, rows, lanes).transpose(1, 0, 2).reshape(2 * rows, lanes)
    )
    for which in range(branches):
        own, other, blocks, block_rows = gather_factors(sub_branches[which, 0])
        branch = merge(place, own, other, blocks, block_rows)
        amplitude = apply(positions[which], amplitude, branch, which == 0)
        if which == 0:
            amplitude = swap(amplitude)
    amplitude = widen(swap(amplitude))
    return amplitude.reshape(rows, 2, lanes).transpose(1, 0, 2).reshape(2, rows * lanes)


def solution(mesh):
    in_specs = (P(None, ("cuts", "wide", "narrow")), P(None, "narrow", None, "wide", None), P())
    out_specs = P(None, ("cuts", "wide", "narrow"))
    return jax.shard_map(shards, mesh=mesh, in_specs=in_specs, out_specs=out_specs, check_vma=False)
```

time: 285 us -> 108 us (0.38)
  other arithmetic: 94.5 us -> 0.22 us
  local copies, waits for them, and re-layouts: 58.4 us -> 3.95 us
  starting transfers between devices: 5.02 us -> 34.4 us
  waiting for transfers between devices: 60.4 us -> 33.5 us
  blocking collectives: 38.6 us -> 18.4 us
  Pallas kernels: 0 us -> 16.9 us
  between operations: 13.7 us -> 0.39 us
  matrix products: 13 us -> 0 us
    add x14 -> x0, other arithmetic: 72.9 us -> none  [the longest x3 37.2 us: bit_tables(): row_part = row_part + jnp.where(chosen[position], 0, bit_value)]
    all_gather x3 -> x0, waiting for transfers between devices: 38.2 us -> none  [shards(): own_whole = lax.all_gather(own_rows, 'wide', axis=1, tiled=True)]
    gather x9 -> x0, local copies, waits for them, and re-layouts: 30.7 us -> none  [the longest x6 16.1 us: contract_blocks(): picked = jnp.take(blocks, gather_index, axis=1)]
    ppermute x3 -> x21, starting transfers between devices: 0.52 us -> 27.8 us  [exchange(): return lax.ppermute(value, axis, pairs)]
    ppermute x3 -> x21, waiting for transfers between devices: 0.01 us -> 26.4 us  [exchange(): return lax.ppermute(value, axis, pairs)]
    all_to_all x3 -> x1, blocking collectives: 38.6 us -> 18.4 us  [swap(): lax.all_to_all(blocks, ('wide', 'narrow'), 0, 0, tiled=True)]
    select_n x11 -> x1, other arithmetic: 17.2 us -> 0.01 us  [shards(): jnp.where(branch_bits < local_bits, branch_bits - lane_bits, branch_bits...]
    pallas_call x0 -> x7, Pallas kernels: none -> 16.9 us  [the longest x3 8.56 us: apply(): pl.pallas_call(functools.partial(apply_kernel, interleaved), out_shape=ja...]
  transfers between devices with their start and end apart: 7 -> 22, of which waited for: 3 -> 8; matrix products, arithmetic and copies ran while one was open for 41% -> 0% of each run, Pallas kernels for 0% -> 10%
where the time goes in v1:
time: 108 us
  starting transfers between devices  34.4 us (32%)
  waiting for transfers between devices  33.5 us (31%)
  blocking collectives  18.4 us (17%)
  Pallas kernels  16.9 us (16%)
  local copies, waits for them, and re-layouts  3.95 us (4%)
    ppermute x21, starting transfers between devices, exchange(): return lax.ppermute(value, axis, pairs)  27.8 us
    ppermute x21, waiting for transfers between devices, exchange(): return lax.ppermute(value, axis, pairs)  26.4 us
    all_to_all x1, blocking collectives, swap(): lax.all_to_all(blocks, ('wide', 'narrow'), 0, 0, tiled=True)  18.4 us
    pallas_call x3, Pallas kernels, apply(): pl.pallas_call(functools.partial(apply_kernel, interleaved), out_shape=ja...  8.56 us
    pallas_call x3, Pallas kernels, merge(): pl.pallas_call(functools.partial(merge_kernel, blocks, block_rows), out_s...  7.26 us
    all_to_all x1, waiting for transfers between devices, swap(): lax.all_to_all(blocks, ('wide', 'narrow'), 0, 0, tiled=True)  7.12 us
    all_to_all x1, starting transfers between devices, swap(): lax.all_to_all(blocks, ('wide', 'narrow'), 0, 0, tiled=True)  6.65 us
    unnamed x32, local copies, waits for them, and re-layouts  2.17 us
  transfers between devices with their start and end apart: 22, of which 8 were waited for; matrix products, arithmetic and copies ran while one was open for 0% of the time, Pallas kernels for 10%

profile of v1, /device:TPU:0, one launch (start us, length us, event | category | flops | bytes accessed | tf_op | source)
XLA Modules:
  0.0 107.7 jit_solution(13745757375926420937)
XLA Ops:
  0.0 1.7 %fusion = (bf16[1,1,2,64,512]{4,3,2,1,0:T(8,128)(2,1)}, bf16[1,1,2,64,512]{4,3,2,1,0:T(8,128)(2,1)S(1)}, bf16[1,1,2,64,512]{4,3,2,1,0:T(8,128)(2,1)S(1)}) fusion(bf16[3,1,2,64,512]{4,3,2,1,0:T(8,128)(2,1)} %param.4), kind=kLoop, calls=%fused_computation.38 | loop fusion | bytes 786432 | tf_op jit(solution)/shard_map/slice | solution.py:231
  1.7 0.0 copy-start.5
  1.7 4.1 %collective-permute-start = (bf16[64,512]{1,0:T(8,128)(2,1)S(1)}, bf16[64,512]{1,0:T(8,128)(2,1)S(1)}, u32[]{:S(2)}, u32[]{:S(2)}) collective-permute-start(bf16[64,512]{1,0:T(8,128)(2,1)S(1)} %get-tuple-element.10), channel_id=1, source_target_pairs={{0,8},{2,10},{4,12},{6,14},{8,0},{10,2},{12,4},{14,6},{1,9},{3,11}... | collective-permute-start | bytes 196616 | tf_op jit(solution)/shard_map/ppermute | solution.py:21
  5.9 0.1 collective-permute-start.7
  6.0 0.0 copy-start.6
  6.0 3.0 %collective-permute-start.14 = (bf16[64,512]{1,0:T(8,128)(2,1)S(1)}, bf16[64,512]{1,0:T(8,128)(2,1)S(1)}, u32[]{:S(2)}, u32[]{:S(2)}) collective-permute-start(bf16[64,512]{1,0:T(8,128)(2,1)S(1)} %get-tuple-element.6), channel_id=1, source_target_pairs={{0,8},{2,10},{4,12},{6,14},{8,0},{10,2},{12,4},{14,6},{1,9},{3,11}... | collective-permute-start | bytes 196616 | tf_op jit(solution)/shard_map/ppermute | solution.py:21
  8.9 0.1 pad_add_fusion.place_ref
  9.0 0.5 collective-permute-done
  9.5 2.0 %collective-permute-start.1 = (bf16[128,512]{1,0:T(8,128)(2,1)S(1)}, bf16[128,512]{1,0:T(8,128)(2,1)S(1)}, u32[]{:S(2)}, u32[]{:S(2)}) collective-permute-start(bf16[128,512]{1,0:T(8,128)(2,1)S(1)} %pad_maximum_fusion.6), channel_id=1, source_target_pairs={{0,2},{2,0},{4,6},{6,4},{8,10},{10,8},{12,14},{14,12},{1,3},{3,1},... | collective-permute-start | bytes 393224 | tf_op jit(solution)/shard_map/ppermute | solution.py:21
  11.5 3.0 %collective-permute-start.3 = (bf16[128,512]{1,0:T(8,128)(2,1)S(1)}, bf16[128,512]{1,0:T(8,128)(2,1)S(1)}, u32[]{:S(2)}, u32[]{:S(2)}) collective-permute-start(bf16[128,512]{1,0:T(8,128)(2,1)S(1)} %pad_maximum_fusion.6), channel_id=1, source_target_pairs={{0,4},{2,6},{4,0},{6,2},{8,12},{10,14},{12,8},{14,10},{1,5},{3,7},... | collective-permute-start | bytes 393224 | tf_op jit(solution)/shard_map/ppermute | solution.py:21
  14.5 0.0 collective-permute-done.7
  14.5 1.5 %collective-permute-start.8 = (bf16[128,512]{1,0:T(8,128)(2,1)S(1)}, bf16[128,512]{1,0:T(8,128)(2,1)S(1)}, u32[]{:S(2)}, u32[]{:S(2)}) collective-permute-start(bf16[128,512]{1,0:T(8,128)(2,1)S(1)} %pad_maximum_fusion.7), channel_id=1, source_target_pairs={{0,2},{2,0},{4,6},{6,4},{8,10},{10,8},{12,14},{14,12},{1,3},{3,1},... | collective-permute-start | bytes 393224 | tf_op jit(solution)/shard_map/ppermute | solution.py:21
  16.0 1.0 collective-permute-start.15
  17.0 0.0 collective-permute-done.1
  17.0 2.3 %collective-permute-start.17 = (bf16[128,512]{1,0:T(8,128)(2,1)S(1)}, bf16[128,512]{1,0:T(8,128)(2,1)S(1)}, u32[]{:S(2)}, u32[]{:S(2)}) collective-permute-start(bf16[128,512]{1,0:T(8,128)(2,1)S(1)} %pad_maximum_fusion.8), channel_id=1, source_target_pairs={{0,4},{2,6},{4,0},{6,2},{8,12},{10,14},{12,8},{14,10},{1,5},{3,7},... | collective-permute-start | bytes 393224 | tf_op jit(solution)/shard_map/ppermute | solution.py:21
  19.4 1.4 %collective-permute-done.8 = bf16[128,512]{1,0:T(8,128)(2,1)S(1)} collective-permute-done((bf16[128,512]{1,0:T(8,128)(2,1)S(1)}, bf16[128,512]{1,0:T(8,128)(2,1)S(1)}, u32[]{:S(2)}, u32[]{:S(2)}) %collective-permute-start.8) | collective-permute-done | bytes 131104 | tf_op jit(solution)/shard_map/ppermute | solution.py:21
  20.8 1.5 %collective-permute-start.2 = (bf16[256,512]{1,0:T(8,128)(2,1)S(1)}, bf16[256,512]{1,0:T(8,128)(2,1)S(1)}, u32[]{:S(2)}, u32[]{:S(2)}) collective-permute-start(bf16[256,512]{1,0:T(8,128)(2,1)S(1)} %pad_maximum_fusion), channel_id=1, source_target_pairs={{0,16},{16,0},{1,17},{17,1},{2,18},{18,2},{3,19},{19,3},{4,20},{20... | collective-permute-start | bytes 786440 | tf_op jit(solution)/shard_map/ppermute | solution.py:21
  22.3 0.0 collective-permute-done.3
  22.3 0.6 collective-permute-start.9
  22.9 1.5 %collective-permute-start.4 = (bf16[128,512]{1,0:T(8,128)(2,1)S(1)}, bf16[128,512]{1,0:T(8,128)(2,1)S(1)}, u32[]{:S(2)}, u32[]{:S(2)}) collective-permute-start(bf16[128,512]{1,0:T(8,128)(2,1)S(1)} %collective-permute-done.3), channel_id=1, source_target_pairs={{0,16},{16,0},{1,17},{17,1},{2,18},{18,2},{3,19},{19,3},{4,20},{20... | collective-permute-start | bytes 393224 | tf_op jit(solution)/shard_map/ppermute | solution.py:21
  24.5 0.6 collective-permute-start.11
  25.1 1.6 %collective-permute-start.16 = (bf16[256,512]{1,0:T(8,128)(2,1)S(1)}, bf16[256,512]{1,0:T(8,128)(2,1)S(1)}, u32[]{:S(2)}, u32[]{:S(2)}) collective-permute-start(bf16[256,512]{1,0:T(8,128)(2,1)S(1)} %pad_maximum_fusion.4), channel_id=1, source_target_pairs={{0,16},{16,0},{1,17},{17,1},{2,18},{18,2},{3,19},{19,3},{4,20},{20... | collective-permute-start | bytes 786440 | tf_op jit(solution)/shard_map/ppermute | solution.py:21
  26.7 11.8 %collective-permute-done.4 = bf16[128,512]{1,0:T(8,128)(2,1)S(1)} collective-permute-done((bf16[128,512]{1,0:T(8,128)(2,1)S(1)}, bf16[128,512]{1,0:T(8,128)(2,1)S(1)}, u32[]{:S(2)}, u32[]{:S(2)}) %collective-permute-start.4) | collective-permute-done | bytes 131104 | tf_op jit(solution)/shard_map/ppermute | solution.py:21
  38.5 1.5 %collective-permute-start.18 = (bf16[128,512]{1,0:T(8,128)(2,1)S(1)}, bf16[128,512]{1,0:T(8,128)(2,1)S(1)}, u32[]{:S(2)}, u32[]{:S(2)}) collective-permute-start(bf16[128,512]{1,0:T(8,128)(2,1)S(1)} %collective-permute-done.17), channel_id=1, source_target_pairs={{0,16},{16,0},{1,17},{17,1},{2,18},{18,2},{3,19},{19,3},{4,20},{20... | collective-permute-start | bytes 393224 | tf_op jit(solution)/shard_map/ppermute | solution.py:21
  40.0 1.3 %collective-permute-done.11 = bf16[128,512]{1,0:T(8,128)(2,1)S(1)} collective-permute-done((bf16[128,512]{1,0:T(8,128)(2,1)S(1)}, bf16[128,512]{1,0:T(8,128)(2,1)S(1)}, u32[]{:S(2)}, u32[]{:S(2)}) %collective-permute-start.11) | collective-permute-done | bytes 131104 | tf_op jit(solution)/shard_map/ppermute | solution.py:21
  41.3 1.2 %collective-permute-start.5 = (bf16[256,512]{1,0:T(8,128)(2,1)S(1)}, bf16[256,512]{1,0:T(8,128)(2,1)S(1)}, u32[]{:S(2)}, u32[]{:S(2)}) collective-permute-start(bf16[256,512]{1,0:T(8,128)(2,1)S(1)} %pad_maximum_fusion.1), channel_id=1, source_target_pairs={{0,2},{2,0},{4,6},{6,4},{8,10},{10,8},{12,14},{14,12},{1,3},{3,1},... | collective-permute-start | bytes 786440 | tf_op jit(solution)/shard_map/ppermute | solution.py:21
  42.5 0.9 collective-permute-start.12
  43.4 4.2 %collective-permute-done.5 = bf16[256,512]{1,0:T(8,128)(2,1)S(1)} collective-permute-done((bf16[256,512]{1,0:T(8,128)(2,1)S(1)}, bf16[256,512]{1,0:T(8,128)(2,1)S(1)}, u32[]{:S(2)}, u32[]{:S(2)}) %collective-permute-start.5) | collective-permute-done | bytes 262176 | tf_op jit(solution)/shard_map/ppermute | solution.py:21
  47.7 0.1 collective-permute-start.6
  47.8 1.2 %collective-permute-start.19 = (bf16[256,512]{1,0:T(8,128)(2,1)S(1)}, bf16[256,512]{1,0:T(8,128)(2,1)S(1)}, u32[]{:S(2)}, u32[]{:S(2)}) collective-permute-start(bf16[256,512]{1,0:T(8,128)(2,1)S(1)} %pad_maximum_fusion.5), channel_id=1, source_target_pairs={{0,2},{2,0},{4,6},{6,4},{8,10},{10,8},{12,14},{14,12},{1,3},{3,1},... | collective-permute-start | bytes 786440 | tf_op jit(solution)/shard_map/ppermute | solution.py:21
  49.2 1.3 %collective-permute-done.12 = bf16[256,512]{1,0:T(8,128)(2,1)S(1)} collective-permute-done((bf16[256,512]{1,0:T(8,128)(2,1)S(1)}, bf16[256,512]{1,0:T(8,128)(2,1)S(1)}, u32[]{:S(2)}, u32[]{:S(2)}) %collective-permute-start.12) | collective-permute-done | bytes 262176 | tf_op jit(solution)/shard_map/ppermute | solution.py:21
  50.5 0.1 collective-permute-start.13
  50.5 6.0 %collective-permute-done.19 = bf16[256,512]{1,0:T(8,128)(2,1)S(1)} collective-permute-done((bf16[256,512]{1,0:T(8,128)(2,1)S(1)}, bf16[256,512]{1,0:T(8,128)(2,1)S(1)}, u32[]{:S(2)}, u32[]{:S(2)}) %collective-permute-start.19) | collective-permute-done | bytes 262176 | tf_op jit(solution)/shard_map/ppermute | solution.py:21
  56.6 0.0 copy-start
  56.6 0.1 collective-permute-start.20
  56.7 1.9 %merge.3.branch_ref = bf16[1024,512]{1,0:T(8,128)(2,1)S(1)} custom-call(s32[3]{0:T(128)S(1)} %pad_add_fusion.place_ref, bf16[1024,512]{1,0:T(8,128)(2,1)S(1)} %constant_dynamic-update-slice_fusion.own_ref, bf16[1024,512]{1,0:T(8,128)(2,1)S(1)} %collective-permute-done.6.other_ref), custom_call_target="tpu_custom_call" | custom-call | flops 1073741824 | bytes 3145728 | tf_op jit(solution)/shard_map/merge/pallas_call | solution.py:68
  58.6 3.4 %contract.3 = bf16[1024,256]{1,0:T(8,128)(2,1)} custom-call(s32[9]{0:T(128)S(1)} %add_bitcast_fusion.bits_ref, f32[2048,128]{1,0:T(8,128)S(1)} %bitcast.35, bf16[1024,512]{1,0:T(8,128)(2,1)S(1)} %merge.3.branch_ref), custom_call_target="tpu_custom_call" | custom-call | flops 1610612736 | bytes 4194304 | tf_op jit(solution)/shard_map/contract/pallas_call | solution.py:141
  62.0 6.6 %all-to-all-start = ((bf16[16,64,256]{2,1,0:T(8,128)(2,1)}), bf16[16,64,256]{2,1,0:T(8,128)(2,1)S(1)}, u32[]{:S(2)}, u32[]{:S(2)}) async-start(bf16[16,64,256]{2,1,0:T(8,128)(2,1)} %bitcast.10), calls=%async_computation | async-start | bytes 1048576 | tf_op jit(solution)/shard_map/all_to_all | solution.py:225
  68.7 2.6 %merge.4.branch_ref = bf16[1024,512]{1,0:T(8,128)(2,1)S(1)} custom-call(s32[3]{0:T(128)S(1)} %pad_add_fusion.place_ref, bf16[1024,512]{1,0:T(8,128)(2,1)S(1)} %constant_dynamic-update-slice_fusion.7.own_ref, bf16[1024,512]{1,0:T(8,128)(2,1)} %collective-permute-done.13.other_ref), custom_call_target="tpu_custom_call" | custom-call | flops 1073741824 | bytes 3145728 | tf_op jit(solution)/shard_map/merge/pallas_call | solution.py:68
  71.3 0.0 copy-start.1
  71.3 1.0 copy-done.1
  72.3 2.7 %merge.5.branch_ref = bf16[1024,512]{1,0:T(8,128)(2,1)S(1)} custom-call(s32[3]{0:T(128)S(1)} %pad_add_fusion.place_ref, bf16[1024,512]{1,0:T(8,128)(2,1)S(1)} %constant_dynamic-update-slice_fusion.14.own_ref, bf16[1024,512]{1,0:T(8,128)(2,1)} %collective-permute-done.20.other_ref), custom_call_target="tpu_custom_call" | custom-call | flops 1073741824 | bytes 3145728 | tf_op jit(solution)/shard_map/merge/pallas_call | solution.py:68
  75.0 1.0 copy-done.3
  76.0 7.1 %all-to-all-done = bf16[16,64,256]{2,1,0:T(8,128)(2,1)S(1)} async-done(((bf16[16,64,256]{2,1,0:T(8,128)(2,1)}), bf16[16,64,256]{2,1,0:T(8,128)(2,1)S(1)}, u32[]{:S(2)}, u32[]{:S(2)}) %all-to-all-start) | async-done | bytes 524320 | tf_op jit(solution)/shard_map/all_to_all | solution.py:225
  83.1 2.6 %contract.4.amplitude_ref = bf16[1024,256]{1,0:T(8,128)(2,1)S(1)} custom-call(s32[9]{0:T(128)S(1)} %get-tuple-element.14.bits_ref, bf16[1024,256]{1,0:T(8,128)(2,1)S(1)} %bitcast.33, bf16[1024,512]{1,0:T(8,128)(2,1)S(1)} %copy-done.2), custom_call_target="tpu_custom_call" | custom-call | flops 1610612736 | bytes 4194304 | tf_op jit(solution)/shard_map/contract/pallas_call | solution.py:141
  85.7 2.6 %contract.5 = bf16[1024,256]{1,0:T(8,128)(2,1)S(1)} custom-call(s32[9]{0:T(128)S(1)} %get-tuple-element.15.bits_ref, bf16[1024,256]{1,0:T(8,128)(2,1)S(1)} %contract.4.amplitude_ref, bf16[1024,512]{1,0:T(8,128)(2,1)S(1)} %copy-done.4), custom_call_target="tpu_custom_call" | custom-call | flops 1610612736 | bytes 4194304 | tf_op jit(solution)/shard_map/contract/pallas_call | solution.py:141
  88.3 18.4 %all_to_all.10 = bf16[16,64,256]{2,1,0:T(8,128)(2,1)S(1)} all-to-all(bf16[16,64,256]{2,1,0:T(8,128)(2,1)S(1)} %bitcast.34), channel_id=1, replica_groups=mesh['cuts'=2,'wide'=8,'narrow'=2] {'wide','narrow'}, dimensions={0} | all-to-all | bytes 1048576 | tf_op jit(solution)/shard_map/all_to_all | solution.py:225
  106.7 1.0 widen.1
  (53 shorter events, 0.5 us)
Async XLA Ops:
  1.7 4.2 %copy-start.5 = (bf16[1,1,2,64,512]{4,3,2,1,0:T(8,128)(2,1)S(1)}, bf16[1,1,2,64,512]{4,3,2,1,0:T(8,128)(2,1)}, u32[]{:S(2)}) copy-start(bf16[1,1,2,64,512]{4,3,2,1,0:T(8,128)(2,1)} %get-tuple-element.11) | copy-start | bytes 393220
  1.7 7.8 %collective-permute-start = (bf16[64,512]{1,0:T(8,128)(2,1)S(1)}, bf16[64,512]{1,0:T(8,128)(2,1)S(1)}, u32[]{:S(2)}, u32[]{:S(2)}) collective-permute-start(bf16[64,512]{1,0:T(8,128)(2,1)S(1)} %get-tuple-element.10), channel_id=1, source_target_pairs={{0,8},{2,10},{4,12},{6,14},{8,0},{10,2},{12,4},{14,6},{1,9},{3,11}... | collective-permute-start | bytes 196616 | tf_op jit(solution)/shard_map/ppermute | solution.py:21
  5.9 8.6 %collective-permute-start.7 = (bf16[64,512]{1,0:T(8,128)(2,1)S(1)}, bf16[64,512]{1,0:T(8,128)(2,1)S(1)}, u32[]{:S(2)}, u32[]{:S(2)}) collective-permute-start(bf16[64,512]{1,0:T(8,128)(2,1)S(1)} %get-tuple-element.8), channel_id=1, source_target_pairs={{0,8},{2,10},{4,12},{6,14},{8,0},{10,2},{12,4},{14,6},{1,9},{3,11}... | collective-permute-start | bytes 196616 | tf_op jit(solution)/shard_map/ppermute | solution.py:21
  6.0 3.0 %copy-start.6 = (s32[3,9]{1,0:T(4,128)S(1)}, s32[3,9]{1,0:T(4,128)}, u32[]{:S(2)}) copy-start(s32[3,9]{1,0:T(4,128)} %param.5) | copy-start | bytes 328
  6.0 10.0 %collective-permute-start.14 = (bf16[64,512]{1,0:T(8,128)(2,1)S(1)}, bf16[64,512]{1,0:T(8,128)(2,1)S(1)}, u32[]{:S(2)}, u32[]{:S(2)}) collective-permute-start(bf16[64,512]{1,0:T(8,128)(2,1)S(1)} %get-tuple-element.6), channel_id=1, source_target_pairs={{0,8},{2,10},{4,12},{6,14},{8,0},{10,2},{12,4},{14,6},{1,9},{3,11}... | collective-permute-start | bytes 196616 | tf_op jit(solution)/shard_map/ppermute | solution.py:21
  9.5 7.5 %collective-permute-start.1 = (bf16[128,512]{1,0:T(8,128)(2,1)S(1)}, bf16[128,512]{1,0:T(8,128)(2,1)S(1)}, u32[]{:S(2)}, u32[]{:S(2)}) collective-permute-start(bf16[128,512]{1,0:T(8,128)(2,1)S(1)} %pad_maximum_fusion.6), channel_id=1, source_target_pairs={{0,2},{2,0},{4,6},{6,4},{8,10},{10,8},{12,14},{14,12},{1,3},{3,1},... | collective-permute-start | bytes 393224 | tf_op jit(solution)/shard_map/ppermute | solution.py:21
  11.5 10.8 %collective-permute-start.3 = (bf16[128,512]{1,0:T(8,128)(2,1)S(1)}, bf16[128,512]{1,0:T(8,128)(2,1)S(1)}, u32[]{:S(2)}, u32[]{:S(2)}) collective-permute-start(bf16[128,512]{1,0:T(8,128)(2,1)S(1)} %pad_maximum_fusion.6), channel_id=1, source_target_pairs={{0,4},{2,6},{4,0},{6,2},{8,12},{10,14},{12,8},{14,10},{1,5},{3,7},... | collective-permute-start | bytes 393224 | tf_op jit(solution)/shard_map/ppermute | solution.py:21
  14.5 6.3 %collective-permute-start.8 = (bf16[128,512]{1,0:T(8,128)(2,1)S(1)}, bf16[128,512]{1,0:T(8,128)(2,1)S(1)}, u32[]{:S(2)}, u32[]{:S(2)}) collective-permute-start(bf16[128,512]{1,0:T(8,128)(2,1)S(1)} %pad_maximum_fusion.7), channel_id=1, source_target_pairs={{0,2},{2,0},{4,6},{6,4},{8,10},{10,8},{12,14},{14,12},{1,3},{3,1},... | collective-permute-start | bytes 393224 | tf_op jit(solution)/shard_map/ppermute | solution.py:21
  16.0 8.5 %collective-permute-start.10 = (bf16[128,512]{1,0:T(8,128)(2,1)S(1)}, bf16[128,512]{1,0:T(8,128)(2,1)S(1)}, u32[]{:S(2)}, u32[]{:S(2)}) collective-permute-start(bf16[128,512]{1,0:T(8,128)(2,1)S(1)} %pad_maximum_fusion.7), channel_id=1, source_target_pairs={{0,4},{2,6},{4,0},{6,2},{8,12},{10,14},{12,8},{14,10},{1,5},{3,7},... | collective-permute-start | bytes 393224 | tf_op jit(solution)/shard_map/ppermute | solution.py:21
  16.0 6.9 %collective-permute-start.15 = (bf16[128,512]{1,0:T(8,128)(2,1)S(1)}, bf16[128,512]{1,0:T(8,128)(2,1)S(1)}, u32[]{:S(2)}, u32[]{:S(2)}) collective-permute-start(bf16[128,512]{1,0:T(8,128)(2,1)S(1)} %pad_maximum_fusion.8), channel_id=1, source_target_pairs={{0,2},{2,0},{4,6},{6,4},{8,10},{10,8},{12,14},{14,12},{1,3},{3,1},... | collective-permute-start | bytes 393224 | tf_op jit(solution)/shard_map/ppermute | solution.py:21
  17.0 8.1 %collective-permute-start.17 = (bf16[128,512]{1,0:T(8,128)(2,1)S(1)}, bf16[128,512]{1,0:T(8,128)(2,1)S(1)}, u32[]{:S(2)}, u32[]{:S(2)}) collective-permute-start(bf16[128,512]{1,0:T(8,128)(2,1)S(1)} %pad_maximum_fusion.8), channel_id=1, source_target_pairs={{0,4},{2,6},{4,0},{6,2},{8,12},{10,14},{12,8},{14,10},{1,5},{3,7},... | collective-permute-start | bytes 393224 | tf_op jit(solution)/shard_map/ppermute | solution.py:21
  20.8 21.7 %collective-permute-start.2 = (bf16[256,512]{1,0:T(8,128)(2,1)S(1)}, bf16[256,512]{1,0:T(8,128)(2,1)S(1)}, u32[]{:S(2)}, u32[]{:S(2)}) collective-permute-start(bf16[256,512]{1,0:T(8,128)(2,1)S(1)} %pad_maximum_fusion), channel_id=1, source_target_pairs={{0,16},{16,0},{1,17},{17,1},{2,18},{18,2},{3,19},{19,3},{4,20},{20... | collective-permute-start | bytes 786440 | tf_op jit(solution)/shard_map/ppermute | solution.py:21
  22.3 26.7 %collective-permute-start.9 = (bf16[256,512]{1,0:T(8,128)(2,1)S(1)}, bf16[256,512]{1,0:T(8,128)(2,1)S(1)}, u32[]{:S(2)}, u32[]{:S(2)}) collective-permute-start(bf16[256,512]{1,0:T(8,128)(2,1)S(1)} %pad_maximum_fusion.2), channel_id=1, source_target_pairs={{0,16},{16,0},{1,17},{17,1},{2,18},{18,2},{3,19},{19,3},{4,20},{20... | collective-permute-start | bytes 786440 | tf_op jit(solution)/shard_map/ppermute | solution.py:21
  22.9 15.5 %collective-permute-start.4 = (bf16[128,512]{1,0:T(8,128)(2,1)S(1)}, bf16[128,512]{1,0:T(8,128)(2,1)S(1)}, u32[]{:S(2)}, u32[]{:S(2)}) collective-permute-start(bf16[128,512]{1,0:T(8,128)(2,1)S(1)} %collective-permute-done.3), channel_id=1, source_target_pairs={{0,16},{16,0},{1,17},{17,1},{2,18},{18,2},{3,19},{19,3},{4,20},{20... | collective-permute-start | bytes 393224 | tf_op jit(solution)/shard_map/ppermute | solution.py:21
  24.5 16.8 %collective-permute-start.11 = (bf16[128,512]{1,0:T(8,128)(2,1)S(1)}, bf16[128,512]{1,0:T(8,128)(2,1)S(1)}, u32[]{:S(2)}, u32[]{:S(2)}) collective-permute-start(bf16[128,512]{1,0:T(8,128)(2,1)S(1)} %collective-permute-done.10), channel_id=1, source_target_pairs={{0,16},{16,0},{1,17},{17,1},{2,18},{18,2},{3,19},{19,3},{4,20},{20... | collective-permute-start | bytes 393224 | tf_op jit(solution)/shard_map/ppermute | solution.py:21
  25.1 24.0 %collective-permute-start.16 = (bf16[256,512]{1,0:T(8,128)(2,1)S(1)}, bf16[256,512]{1,0:T(8,128)(2,1)S(1)}, u32[]{:S(2)}, u32[]{:S(2)}) collective-permute-start(bf16[256,512]{1,0:T(8,128)(2,1)S(1)} %pad_maximum_fusion.4), channel_id=1, source_target_pairs={{0,16},{16,0},{1,17},{17,1},{2,18},{18,2},{3,19},{19,3},{4,20},{20... | collective-permute-start | bytes 786440 | tf_op jit(solution)/shard_map/ppermute | solution.py:21
  38.5 9.3 %collective-permute-start.18 = (bf16[128,512]{1,0:T(8,128)(2,1)S(1)}, bf16[128,512]{1,0:T(8,128)(2,1)S(1)}, u32[]{:S(2)}, u32[]{:S(2)}) collective-permute-start(bf16[128,512]{1,0:T(8,128)(2,1)S(1)} %collective-permute-done.17), channel_id=1, source_target_pairs={{0,16},{16,0},{1,17},{17,1},{2,18},{18,2},{3,19},{19,3},{4,20},{20... | collective-permute-start | bytes 393224 | tf_op jit(solution)/shard_map/ppermute | solution.py:21
  41.3 6.4 %collective-permute-start.5 = (bf16[256,512]{1,0:T(8,128)(2,1)S(1)}, bf16[256,512]{1,0:T(8,128)(2,1)S(1)}, u32[]{:S(2)}, u32[]{:S(2)}) collective-permute-start(bf16[256,512]{1,0:T(8,128)(2,1)S(1)} %pad_maximum_fusion.1), channel_id=1, source_target_pairs={{0,2},{2,0},{4,6},{6,4},{8,10},{10,8},{12,14},{14,12},{1,3},{3,1},... | collective-permute-start | bytes 786440 | tf_op jit(solution)/shard_map/ppermute | solution.py:21
  42.5 8.0 %collective-permute-start.12 = (bf16[256,512]{1,0:T(8,128)(2,1)S(1)}, bf16[256,512]{1,0:T(8,128)(2,1)S(1)}, u32[]{:S(2)}, u32[]{:S(2)}) collective-permute-start(bf16[256,512]{1,0:T(8,128)(2,1)S(1)} %pad_maximum_fusion.3), channel_id=1, source_target_pairs={{0,2},{2,0},{4,6},{6,4},{8,10},{10,8},{12,14},{14,12},{1,3},{3,1},... | collective-permute-start | bytes 786440 | tf_op jit(solution)/shard_map/ppermute | solution.py:21
  47.7 9.0 %collective-permute-start.6 = (bf16[1024,512]{1,0:T(8,128)(2,1)S(1)}, bf16[1024,512]{1,0:T(8,128)(2,1)S(1)}, u32[]{:S(2)}, u32[]{:S(2)}) collective-permute-start(bf16[1024,512]{1,0:T(8,128)(2,1)S(1)} %constant_dynamic-update-slice_fusion.own_ref), channel_id=1, source_target_pairs={{0,1},{1,0},{2,3},{3,2},{4,5},{5,4},{6,7},{7,6},{8,9},{9,8},{10,11... | collective-permute-start | bytes 3145736 | tf_op jit(solution)/shard_map/ppermute | solution.py:21
  47.8 8.8 %collective-permute-start.19 = (bf16[256,512]{1,0:T(8,128)(2,1)S(1)}, bf16[256,512]{1,0:T(8,128)(2,1)S(1)}, u32[]{:S(2)}, u32[]{:S(2)}) collective-permute-start(bf16[256,512]{1,0:T(8,128)(2,1)S(1)} %pad_maximum_fusion.5), channel_id=1, source_target_pairs={{0,2},{2,0},{4,6},{6,4},{8,10},{10,8},{12,14},{14,12},{1,3},{3,1},... | collective-permute-start | bytes 786440 | tf_op jit(solution)/shard_map/ppermute | solution.py:21
  50.5 18.2 %collective-permute-start.13 = (bf16[1024,512]{1,0:T(8,128)(2,1)S(1)}, bf16[1024,512]{1,0:T(8,128)(2,1)}, u32[]{:S(2)}, u32[]{:S(2)}) collective-permute-start(bf16[1024,512]{1,0:T(8,128)(2,1)S(1)} %constant_dynamic-update-slice_fusion.7.own_ref), channel_id=1, source_target_pairs={{0,1},{1,0},{2,3},{3,2},{4,5},{5,4},{6,7},{7,6},{8,9},{9,8},{10,11... | collective-permute-start | bytes 3145736 | tf_op jit(solution)/shard_map/ppermute | solution.py:21
  56.6 2.0 %copy-start = (f32[2,131072]{1,0:T(2,128)S(1)}, f32[2,131072]{1,0:T(2,128)}, u32[]{:S(2)}) copy-start(f32[2,131072]{1,0:T(2,128)} %param.3) | copy-start | bytes 3145732
  56.6 15.7 %collective-permute-start.20 = (bf16[1024,512]{1,0:T(8,128)(2,1)S(1)}, bf16[1024,512]{1,0:T(8,128)(2,1)}, u32[]{:S(2)}, u32[]{:S(2)}) collective-permute-start(bf16[1024,512]{1,0:T(8,128)(2,1)S(1)} %constant_dynamic-update-slice_fusion.14.own_ref), channel_id=1, source_target_pairs={{0,1},{1,0},{2,3},{3,2},{4,5},{5,4},{6,7},{7,6},{8,9},{9,8},{10,11... | collective-permute-start | bytes 3145736 | tf_op jit(solution)/shard_map/ppermute | solution.py:21
  62.0 21.1 %all-to-all-start = ((bf16[16,64,256]{2,1,0:T(8,128)(2,1)}), bf16[16,64,256]{2,1,0:T(8,128)(2,1)S(1)}, u32[]{:S(2)}, u32[]{:S(2)}) async-start(bf16[16,64,256]{2,1,0:T(8,128)(2,1)} %bitcast.10), calls=%async_computation | async-start | bytes 1048576 | tf_op jit(solution)/shard_map/all_to_all | solution.py:225
  71.3 1.0 copy-start.1
  72.3 10.8 %copy-start.2 = (bf16[1024,512]{1,0:T(8,128)(2,1)S(1)}, bf16[1024,512]{1,0:T(8,128)(2,1)}, u32[]{:S(2)}) copy-start(bf16[1024,512]{1,0:T(8,128)(2,1)} %copy-done.1) | copy-start | bytes 3145732
  75.0 1.0 copy-start.3
  83.1 2.6 %copy-start.4 = (bf16[1024,512]{1,0:T(8,128)(2,1)S(1)}, bf16[1024,512]{1,0:T(8,128)(2,1)}, u32[]{:S(2)}) copy-start(bf16[1024,512]{1,0:T(8,128)(2,1)} %copy-done.3) | copy-start | bytes 3145732

commit v2 on v1

v2 whole, which is shorter than its diff:
```python
import functools

import jax
import jax.numpy as jnp
from jax import lax
from jax.experimental import pallas as pl
from jax.experimental.pallas import tpu as pltpu
from jax.sharding import PartitionSpec as P

lane_bits = 7
lanes = 2**lane_bits
vmem_budget = 24 * 2**20
permute_swaps = (False, False)


def log2(size):
    return size.bit_length() - 1


def exchange(value, axis, mask):
    count = lax.axis_size(axis)
    pairs = [(source, source ^ mask) for source in range(count)]
    return lax.ppermute(value, axis, pairs)


def on_vmem():
    return pl.BlockSpec(memory_space=pltpu.VMEM)


def on_smem():
    return pl.BlockSpec(memory_space=pltpu.SMEM)


def params():
    return pltpu.CompilerParams(vmem_limit_bytes=vmem_budget)


def merge_kernel(layout, block_rows, place_ref, *refs):
    count = len(layout)
    own_refs, other_refs = refs[:count], refs[count : 2 * count]
    branch_ref, factors = refs[2 * count :]
    width = branch_ref.shape[1]
    wide, cuts, narrow = place_ref[0], place_ref[1], place_ref[2]
    for sources, slot in ((own_refs, narrow), (other_refs, 1 - narrow)):
        for source, blocks in zip(sources, layout):
            for number, (wide_mask, part_mask) in enumerate(blocks):
                if wide_mask is None:
                    start = (slot * 2 + part_mask) * width
                else:
                    part = jnp.bitwise_xor(cuts, part_mask)
                    block = jnp.bitwise_xor(wide, wide_mask)
                    start = (slot * 2 + part) * width + block * block_rows
                factors[pl.ds(pl.multiple_of(start, block_rows), block_rows), :] = source[
                    number * block_rows : (number + 1) * block_rows, :
                ]
    chunk = min(256, width)

    second_real = factors[2 * width : 3 * width, :]
    second_imag = factors[3 * width : 4 * width, :]
    for row in range(0, width, chunk):
        first_real = factors[row : row + chunk, :]
        first_imag = factors[width + row : width + row + chunk, :]
        real = dot(first_real, second_real) - dot(first_imag, second_imag)
        imag = dot(first_real, second_imag) + dot(first_imag, second_real)
        branch_ref[row : row + chunk, :] = real.astype(jnp.bfloat16)
        branch_ref[width + row : width + row + chunk, :] = imag.astype(jnp.bfloat16)


def merge(place, own, other, layout, block_rows):
    width = own[0].shape[1]
    return pl.pallas_call(
        functools.partial(merge_kernel, layout, block_rows),
        out_shape=jax.ShapeDtypeStruct((2 * width, width), jnp.bfloat16),
        in_specs=[on_smem()] + [on_vmem()] * (2 * len(own)),
        out_specs=on_vmem(),
        scratch_shapes=[pltpu.VMEM((4 * width, width), jnp.bfloat16)],
        compiler_params=params(),
        cost_estimate=pl.CostEstimate(
            flops=8 * width**3, bytes_accessed=12 * width**2, transcendentals=0
        ),
        name="merge",
    )(place, *own, *other)


def dot(left, right):
    return jnp.dot(left, right, preferred_element_type=jnp.float32)


def bit_of(values, position):
    return jnp.bitwise_and(jnp.right_shift(values, position), 1)


def to_sorted(values, chosen, free):
    order = len(chosen)
    result = jnp.left_shift(bit_of(values, free), order)
    for k in range(order):
        result += jnp.left_shift(bit_of(values, chosen[k]), order - 1 - k)
    return result


def to_plain(values, chosen, free):
    order = len(chosen)
    result = jnp.left_shift(bit_of(values, order), free)
    for k in range(order):
        result += jnp.left_shift(bit_of(values, order - 1 - k), chosen[k])
    return result


def selector(target, first, count):
    row = lax.broadcasted_iota(jnp.int32, (count, target.shape[1]), 0) + first
    return jnp.where(row == target, 1.0, 0.0).astype(jnp.bfloat16)


select_rows = 512
branch_rows = 256


def outgoing(plain, place_ref, order):
    if order is None:
        return plain
    low, cores = order
    block = jnp.bitwise_xor(jnp.right_shift(plain, low), place_ref[0] * cores + place_ref[2])
    blocks = plain.shape[1] >> low
    core, wide = jnp.bitwise_and(block, cores - 1), jnp.right_shift(block, log2(cores))
    position = core * (blocks // cores) + wide
    return jnp.left_shift(position, low) + jnp.bitwise_and(plain, 2**low - 1)


def incoming(number, place_ref, order):
    if order is None:
        return number
    low, cores = order
    return jnp.bitwise_xor(number, jnp.left_shift(place_ref[0] * cores + place_ref[2], low))


def order_of(bits_ref, which):
    count = bits_ref.shape[1]
    chosen = [bits_ref[which, k] for k in range(count)]
    return chosen, count * (count + 1) // 2 - sum(chosen)


def row_numbers(rows):
    return lax.broadcasted_iota(jnp.int32, (1, rows), 1)


def permute_into(sorted_ref, target, source):
    rows = target.shape[1]
    for first in range(0, rows, select_rows):
        half, row = divmod(first, rows // 2)
        sorted_ref[row : row + select_rows, half * 2 * lanes : (half + 1) * 2 * lanes] = dot(
            selector(target, first, select_rows), source
        ).astype(jnp.bfloat16)


def multiply_into(product_ref, branch_ref, sorted_ref):
    width = branch_ref.shape[1]
    for row in range(0, width, branch_rows):
        by_real = dot(branch_ref[row : row + branch_rows, :], sorted_ref[...])
        by_imag = dot(branch_ref[width + row : width + row + branch_rows, :], sorted_ref[...])
        for half in range(2):
            at = half * 2 * lanes
            real = by_real[:, at : at + lanes] - by_imag[:, at + lanes : at + 2 * lanes]
            imag = by_real[:, at + lanes : at + 2 * lanes] + by_imag[:, at : at + lanes]
            to = half * width + row
            product_ref[to : to + branch_rows, :lanes] = real.astype(jnp.bfloat16)
            product_ref[to : to + branch_rows, lanes:] = imag.astype(jnp.bfloat16)


def restore_into(out_ref, target, product_ref):
    for first in range(0, target.shape[1], select_rows):
        out_ref[first : first + select_rows, :] = dot(
            selector(target, first, select_rows), product_ref[...]
        ).astype(jnp.bfloat16)


def prepare_kernel(bits_ref, place_ref, stem_ref, sorted_ref):
    rows = stem_ref.shape[0] // 2
    stem = jnp.concatenate(
        [stem_ref[pl.ds(part, rows, stride=2), :].astype(jnp.bfloat16) for part in range(2)],
        axis=1,
    )
    permute_into(sorted_ref, to_sorted(row_numbers(rows), *order_of(bits_ref, 0)), stem)


def first_kernel(order, bits_ref, place_ref, sorted_ref, branch_ref, result_ref, product_ref):
    multiply_into(product_ref, branch_ref, sorted_ref)
    target = to_plain(row_numbers(result_ref.shape[0]), *order_of(bits_ref, 0))
    restore_into(result_ref, outgoing(target, place_ref, order), product_ref)


def rest_kernel(
    orders,
    bits_ref,
    place_ref,
    amplitude_ref,
    branch1_ref,
    branch2_ref,
    result_ref,
    sorted_ref,
    product_ref,
):
    numbers = row_numbers(result_ref.shape[0])
    second, third = order_of(bits_ref, 1), order_of(bits_ref, 2)
    target = to_sorted(incoming(numbers, place_ref, orders[0]), *second)
    permute_into(sorted_ref, target, amplitude_ref[...])
    multiply_into(product_ref, branch1_ref, sorted_ref)
    between = to_sorted(to_plain(numbers, *second), *third)
    permute_into(sorted_ref, between, product_ref[...])
    multiply_into(product_ref, branch2_ref, sorted_ref)
    target = outgoing(to_plain(numbers, *third), place_ref, orders[1])
    restore_into(result_ref, target, product_ref)


def contract(kernel, bits, place, operands, rows, shape, scratch, products, name):
    shapes = [
        pltpu.VMEM((rows // 2, 4 * lanes), jnp.bfloat16),
        pltpu.VMEM((rows, 2 * lanes), jnp.bfloat16),
    ]
    return pl.pallas_call(
        kernel,
        out_shape=jax.ShapeDtypeStruct(shape, jnp.bfloat16),
        in_specs=[on_smem()] * 2 + [on_vmem()] * len(operands),
        out_specs=on_vmem(),
        scratch_shapes=shapes[2 - scratch :],
        compiler_params=params(),
        cost_estimate=pl.CostEstimate(
            flops=4 * products * rows * rows * 2 * lanes, bytes_accessed=2**20, transcendentals=0
        ),
        name=name,
    )(bits, place, *operands)


def widen_kernel(order, place_ref, amplitude_ref, out_ref):
    rows = amplitude_ref.shape[0]
    low = log2(rows) if order is None else order[0]
    size = 2**low
    for block in range(rows // size):
        start = 0 if order is None else incoming(block * size, place_ref, order)
        values = amplitude_ref[block * size : (block + 1) * size, :].astype(jnp.float32)
        start = pl.multiple_of(2 * start, 2 * size)
        out_ref[pl.ds(start, size, stride=2), :] = values[:, :lanes]
        out_ref[pl.ds(start + 1, size, stride=2), :] = values[:, lanes:]


def widen(place, amplitude, order):
    rows = amplitude.shape[0]
    return pl.pallas_call(
        functools.partial(widen_kernel, order),
        out_shape=jax.ShapeDtypeStruct((2 * rows, lanes), jnp.float32),
        in_specs=[on_smem(), on_vmem()],
        out_specs=on_vmem(),
        compiler_params=params(),
        name="widen",
    )(place, amplitude)


def gather_plain(sub_branch):
    own = lax.all_gather(sub_branch, "wide", axis=1, tiled=True)
    own = own.reshape(-1, own.shape[-1])
    return [own], [exchange(own, "narrow", 1)], [[(None, 0), (None, 1)]], own.shape[0] // 2


def from_other_core(pieces):
    return [exchange(piece, "narrow", 1) for piece in pieces]


def after(value, *others):
    return lax.optimization_barrier((value,) + others)[0]


def gather_shared(sub_branches, ready):
    wide_count = lax.axis_size("wide")
    block_rows = sub_branches.shape[-2]
    even = list(range(0, wide_count, 2))
    part = lax.axis_index("cuts")

    def along(value):
        return jnp.concatenate(
            [value] + [exchange(value, "wide", mask) for mask in even[1:]], axis=-2
        )

    def mine(first, last):
        own = sub_branches[first:last, 0]
        return jnp.where(part == 0, own[:, 0], own[:, 1])

    def blocks(masks, wide_mask, part_mask):
        return [(mask ^ wide_mask, part_mask) for mask in masks]

    sides = [(0, 0), (1, 0), (0, 1), (1, 1)]
    layout = [blocks(even, *side) for side in sides]
    near0 = after(along(mine(0, 1)[0]), ready)
    near0_other = from_other_core([near0])
    x0, y0 = exchange(near0, "wide", 1), exchange(near0, "cuts", 1)
    half = near0.shape[0] // 2
    late = [x0, y0, exchange(x0[:half], "cuts", 1), exchange(y0[half:], "wide", 1)]
    cut = len(even) // 2
    layout0 = layout[:3] + [blocks(even[:cut], 1, 1), blocks(even[cut:], 1, 1)]
    first = ([near0] + late, near0_other + from_other_core(late), layout0, block_rows)
    near1, near2 = after(along(after(mine(1, 3), near0_other[0])), x0, y0)
    x1, y2 = exchange(near1, "wide", 1), exchange(near2, "cuts", 1)
    own1 = [near1, x1, exchange(near1, "cuts", 1), exchange(x1, "cuts", 1)]
    own2 = [near2, exchange(near2, "wide", 1), y2, exchange(y2, "wide", 1)]
    second = (own1, from_other_core(own1), layout, block_rows)
    third = (own2, from_other_core(own2), layout, block_rows)
    return [first, second, third], (x1, y2)


def gather_factors(sub_branches, ready):
    shared = (
        sub_branches.shape[-2] % 16 == 0
        and lax.axis_size("cuts") == 2
        and lax.axis_size("wide") >= 4
        and sub_branches.shape[0] == 3
    )
    if shared:
        return gather_shared(sub_branches, ready)
    count = sub_branches.shape[0]
    return [gather_plain(sub_branches[which, 0]) for which in range(count)], ()


def shards(stem_tensor, sub_branches, branch_bits):
    wide_count, narrow_count = lax.axis_size("wide"), lax.axis_size("narrow")
    local_bits = log2(stem_tensor.shape[1])
    rows = stem_tensor.shape[1] // lanes
    devices = wide_count * narrow_count
    low_bits = log2(rows // devices)
    place = jnp.stack([lax.axis_index(axis) for axis in ("wide", "cuts", "narrow")]).astype(
        jnp.int32
    )
    positions = jnp.where(
        branch_bits < local_bits, branch_bits - lane_bits, branch_bits - local_bits + low_bits
    )

    small = rows // devices >= 16 and wide_count <= 8 and narrow_count == 2
    permuted = (low_bits, narrow_count)
    orders = [permuted if small and use else None for use in permute_swaps]

    def swap(amplitude, order):
        if order is None:
            blocks = amplitude.reshape(devices, rows // devices, 2 * lanes)
            blocks = lax.all_to_all(blocks, ("wide", "narrow"), 0, 0, tiled=True)
            return blocks.reshape(rows, 2 * lanes)
        size, half = 2**low_bits, rows // 2
        other = exchange(amplitude[half:], "narrow", 1)
        pairs = [
            jnp.concatenate([amplitude[at : at + size], other[at : at + size]])
            for at in range(0, half, size)
        ]
        pairs = [pair if mask == 0 else exchange(pair, "wide", mask) for mask, pair in enumerate(pairs)]
        return jnp.concatenate(pairs)

    stem = stem_tensor.reshape(2, rows, lanes).transpose(1, 0, 2).reshape(2 * rows, lanes)
    width = sub_branches.shape[-1]
    plain = (rows, 2 * lanes)
    run = functools.partial(contract, bits=positions, place=place, rows=rows)
    ordered = run(
        prepare_kernel,
        operands=[stem],
        shape=(width, 4 * lanes),
        scratch=0,
        products=1,
        name="prepare",
    )
    factors, sent = gather_factors(sub_branches, ordered)
    branch0, branch1, branch2 = [merge(place, *each) for each in factors]
    amplitude = run(
        functools.partial(first_kernel, orders[0]),
        operands=[ordered, branch0],
        shape=plain,
        scratch=1,
        products=2,
        name="first",
    )
    amplitude = swap(amplitude, orders[0])
    amplitude = run(
        functools.partial(rest_kernel, orders),
        operands=[amplitude, branch1, branch2],
        shape=plain,
        scratch=2,
        products=5,
        name="rest",
    )
    amplitude = widen(place, swap(amplitude, orders[1]), orders[1])
    return amplitude.reshape(rows, 2, lanes).transpose(1, 0, 2).reshape(2, rows * lanes)


def solution(mesh):
    in_specs = (P(None, ("cuts", "wide", "narrow")), P(None, "narrow", None, "wide", None), P())
    out_specs = P(None, ("cuts", "wide", "narrow"))
    return jax.shard_map(shards, mesh=mesh, in_specs=in_specs, out_specs=out_specs, check_vma=False)
```

time: 108 us -> 91 us (0.84)
  waiting for transfers between devices: 33.5 us -> 22.9 us
  starting transfers between devices: 34.4 us -> 29.5 us
  Pallas kernels: 16.9 us -> 15.1 us
  blocking collectives: 18.4 us -> 19.9 us
    all_to_all x1, waiting for transfers between devices: 7.12 us -> 0.01 us  [swap(): blocks = lax.all_to_all(blocks, ('wide', 'narrow'), 0, 0, tiled=True)]
    ppermute x21 -> x29, waiting for transfers between devices: 26.4 us -> 22.9 us  [exchange(): return lax.ppermute(value, axis, pairs)]
    all_to_all x1, starting transfers between devices: 6.65 us -> 3.68 us  [swap(): blocks = lax.all_to_all(blocks, ('wide', 'narrow'), 0, 0, tiled=True)]
    ppermute x21 -> x29, starting transfers between devices: 27.8 us -> 25.8 us  [exchange(): return lax.ppermute(value, axis, pairs)]
    pallas_call x7, Pallas kernels: 16.9 us -> 15.1 us  [the longest x3 7.7 us: contract(): pl.pallas_call(kernel, out_shape=jax.ShapeDtypeStruct(shape, jnp.bfloat16...]
    slice x1 -> x2, local copies, waits for them, and re-layouts: 1.72 us -> 0.02 us  [the longest x1 0.01 us: gather_shared(): x0[:half]]
    all_to_all x1, blocking collectives: 18.4 us -> 19.9 us  [swap(): blocks = lax.all_to_all(blocks, ('wide', 'narrow'), 0, 0, tiled=True)]
    unnamed x32 -> x6, local copies, waits for them, and re-layouts: 2.17 us -> 1.91 us
  transfers between devices with their start and end apart: 22 -> 30, of which waited for: 8 -> 10; matrix products, arithmetic and copies ran while one was open for 0% -> 0% of each run, Pallas kernels for 10% -> 11%
where the time goes in v2:
time: 91 us; the launch traced here: 90.7 us
  starting transfers between devices  29.5 us (32%)
  waiting for transfers between devices  22.9 us (25%)
  blocking collectives  19.9 us (22%)
  Pallas kernels  15.1 us (17%)
  local copies, waits for them, and re-layouts  2.9 us (3%)
    ppermute x29, starting transfers between devices, exchange(): return lax.ppermute(value, axis, pairs)  25.8 us
    ppermute x29, waiting for transfers between devices, exchange(): return lax.ppermute(value, axis, pairs)  22.9 us
    all_to_all x1, blocking collectives, swap(): blocks = lax.all_to_all(blocks, ('wide', 'narrow'), 0, 0, tiled=True)  19.9 us
    pallas_call x3, Pallas kernels, contract(): pl.pallas_call(kernel, out_shape=jax.ShapeDtypeStruct(shape, jnp.bfloat16...  7.7 us
    pallas_call x3, Pallas kernels, merge(): pl.pallas_call(functools.partial(merge_kernel, layout, block_rows), out_s...  5.79 us
    all_to_all x1, starting transfers between devices, swap(): blocks = lax.all_to_all(blocks, ('wide', 'narrow'), 0, 0, tiled=True)  3.68 us
    unnamed x6, local copies, waits for them, and re-layouts  1.91 us
  transfers between devices with their start and end apart: 30, of which 10 were waited for; matrix products, arithmetic and copies ran while one was open for 0% of the time, Pallas kernels for 11%

profile of v2, /device:TPU:0, one launch (start us, length us, event | category | flops | bytes accessed | tf_op | source)
XLA Modules:
  0.0 90.7 jit_solution(8875554414558133245)
XLA Ops:
  0.0 0.9 %slice_bitcast_fusion.2 = bf16[1,2,64,512]{3,2,1,0:T(8,128)(2,1)S(1)} fusion(bf16[3,1,2,64,512]{4,3,2,1,0:T(8,128)(2,1)} %param.4), kind=kLoop, calls=%fused_computation.7 | loop fusion | bytes 262144 | tf_op jit(solution)/shard_map/squeeze | solution.py:283
  0.9 5.1 %collective-permute-start.2 = (bf16[64,512]{1,0:T(8,128)(2,1)S(1)}, bf16[64,512]{1,0:T(8,128)(2,1)S(1)}, u32[]{:S(2)}, u32[]{:S(2)}) collective-permute-start(bf16[64,512]{1,0:T(8,128)(2,1)S(1)} %fusion.1), channel_id=1, source_target_pairs={{0,12},{2,14},{4,8},{6,10},{8,4},{10,6},{12,0},{14,2},{1,13},{3,15... | collective-permute-start | bytes 196616 | tf_op jit(solution)/shard_map/ppermute | solution.py:23
  6.1 0.6 collective-permute-start
  6.7 0.7 copy-done.2
  7.4 0.1 pad_add_fusion.place_ref
  7.5 1.2 %copy-done = f32[2,131072]{1,0:T(2,128)S(1)} copy-done((f32[2,131072]{1,0:T(2,128)S(1)}, f32[2,131072]{1,0:T(2,128)}, u32[]{:S(2)}) %copy-start) | copy-done | bytes 1048600
  8.7 1.3 %prepare.1.sorted_ref = bf16[512,512]{1,0:T(8,128)(2,1)S(1)} custom-call(s32[3,9]{1,0:T(4,128)S(1)} %add_select_fusion.bits_ref, s32[3]{0:T(128)S(1)} %pad_add_fusion.place_ref, f32[2048,128]{1,0:T(8,128)S(1)} %bitcast.32), custom_call_target="tpu_custom_call" | custom-call | flops 1073741824 | bytes 1048576 | tf_op jit(solution)/shard_map/prepare/pallas_call | solution.py:219
  10.0 0.0 copy-start.1
  10.0 0.0 collective-permute-done.2
  10.0 1.6 %collective-permute-done.1 = bf16[64,512]{1,0:T(8,128)(2,1)S(1)} collective-permute-done((bf16[64,512]{1,0:T(8,128)(2,1)S(1)}, bf16[64,512]{1,0:T(8,128)(2,1)S(1)}, u32[]{:S(2)}, u32[]{:S(2)}) %collective-permute-start.1) | collective-permute-done | bytes 65568 | tf_op jit(solution)/shard_map/ppermute | solution.py:23
  11.7 0.1 collective-permute-start.7
  11.8 1.6 %collective-permute-start.3 = (bf16[256,512]{1,0:T(8,128)(2,1)S(1)}, bf16[256,512]{1,0:T(8,128)(2,1)S(1)}, u32[]{:S(2)}, u32[]{:S(2)}) collective-permute-start(bf16[256,512]{1,0:T(8,128)(2,1)S(1)} %pad_maximum_fusion.1.refs_0_), channel_id=1, source_target_pairs={{0,2},{2,0},{4,6},{6,4},{8,10},{10,8},{12,14},{14,12},{1,3},{3,1},... | collective-permute-start | bytes 786440 | tf_op jit(solution)/shard_map/ppermute | solution.py:23
  13.4 1.5 %collective-permute-start.4 = (bf16[256,512]{1,0:T(8,128)(2,1)S(1)}, bf16[256,512]{1,0:T(8,128)(2,1)S(1)}, u32[]{:S(2)}, u32[]{:S(2)}) collective-permute-start(bf16[256,512]{1,0:T(8,128)(2,1)S(1)} %pad_maximum_fusion.1.refs_0_), channel_id=1, source_target_pairs={{0,16},{16,0},{1,17},{17,1},{2,18},{18,2},{3,19},{19,3},{4,20},{20... | collective-permute-start | bytes 786440 | tf_op jit(solution)/shard_map/ppermute | solution.py:23
  14.9 3.0 %collective-permute-start.14 = (bf16[2,64,512]{2,1,0:T(8,128)(2,1)S(1)}, bf16[2,64,512]{2,1,0:T(8,128)(2,1)S(1)}, u32[]{:S(2)}, u32[]{:S(2)}) collective-permute-start(bf16[2,64,512]{2,1,0:T(8,128)(2,1)S(1)} %fusion), channel_id=1, source_target_pairs={{0,12},{2,14},{4,8},{6,10},{8,4},{10,6},{12,0},{14,2},{1,13},{3,15... | collective-permute-start | bytes 393224 | tf_op jit(solution)/shard_map/ppermute | solution.py:23
  17.9 0.0 collective-permute-start.13
  17.9 1.4 %collective-permute-start.12 = (bf16[2,64,512]{2,1,0:T(8,128)(2,1)S(1)}, bf16[2,64,512]{2,1,0:T(8,128)(2,1)S(1)}, u32[]{:S(2)}, u32[]{:S(2)}) collective-permute-start(bf16[2,64,512]{2,1,0:T(8,128)(2,1)S(1)} %fusion), channel_id=1, source_target_pairs={{0,4},{2,6},{4,0},{6,2},{8,12},{10,14},{12,8},{14,10},{1,5},{3,7},... | collective-permute-start | bytes 393224 | tf_op jit(solution)/shard_map/ppermute | solution.py:23
  19.4 1.2 %collective-permute-done.3.refs_1_ = bf16[256,512]{1,0:T(8,128)(2,1)S(1)} collective-permute-done((bf16[256,512]{1,0:T(8,128)(2,1)S(1)}, bf16[256,512]{1,0:T(8,128)(2,1)S(1)}, u32[]{:S(2)}, u32[]{:S(2)}) %collective-permute-start.3) | collective-permute-done | bytes 262176 | tf_op jit(solution)/shard_map/ppermute | solution.py:23
  20.6 1.6 %collective-permute-start.5 = (bf16[128,512]{1,0:T(8,128)(2,1)S(1)}, bf16[128,512]{1,0:T(8,128)(2,1)S(1)}, u32[]{:S(2)}, u32[]{:S(2)}) collective-permute-start(bf16[128,512]{1,0:T(8,128)(2,1)S(1)} %slice.34), channel_id=1, source_target_pairs={{0,16},{16,0},{1,17},{17,1},{2,18},{18,2},{3,19},{19,3},{4,20},{20... | collective-permute-start | bytes 393224 | tf_op jit(solution)/shard_map/ppermute | solution.py:23
  22.2 1.6 %collective-permute-start.6 = (bf16[128,512]{1,0:T(8,128)(2,1)S(1)}, bf16[128,512]{1,0:T(8,128)(2,1)S(1)}, u32[]{:S(2)}, u32[]{:S(2)}) collective-permute-start(bf16[128,512]{1,0:T(8,128)(2,1)S(1)} %slice.35), channel_id=1, source_target_pairs={{0,2},{2,0},{4,6},{6,4},{8,10},{10,8},{12,14},{14,12},{1,3},{3,1},... | collective-permute-start | bytes 393224 | tf_op jit(solution)/shard_map/ppermute | solution.py:23
  23.7 5.5 %collective-permute-done.13 = bf16[2,64,512]{2,1,0:T(8,128)(2,1)S(1)} collective-permute-done((bf16[2,64,512]{2,1,0:T(8,128)(2,1)S(1)}, bf16[2,64,512]{2,1,0:T(8,128)(2,1)S(1)}, u32[]{:S(2)}, u32[]{:S(2)}) %collective-permute-start.13) | collective-permute-done | bytes 131104 | tf_op jit(solution)/shard_map/ppermute | solution.py:23
  29.3 0.6 collective-permute-start.10
  29.9 0.1 collective-permute-start.11
  30.0 0.6 collective-permute-start.15
  30.6 0.2 collective-permute-done.9.refs_7_
  30.8 0.2 collective-permute-done.10.refs_8_
  31.0 0.3 collective-permute-done.11.refs_9_
  31.2 1.9 %merge.3.branch_ref = bf16[1024,512]{1,0:T(8,128)(2,1)S(1)} custom-call(s32[3]{0:T(128)S(1)} %pad_add_fusion.place_ref, bf16[256,512]{1,0:T(8,128)(2,1)S(1)} %pad_maximum_fusion.1.refs_0_, bf16[256,512]{1,0:T(8,128)(2,1)S(1)} %collective-permute-done.3.refs_1_, bf16[256,512]{1,0:T(8,128)(2,1)S(1)} %collective-permute-done.4.refs_2_, ...), custom_call_target="tpu_custom_call" | custom-call | flops 1073741824 | bytes 3145728 | tf_op jit(solution)/shard_map/merge/pallas_call | solution.py:71
  33.2 2.7 %first.1 = bf16[1024,256]{1,0:T(8,128)(2,1)} custom-call(s32[3,9]{1,0:T(4,128)S(1)} %add_select_fusion.bits_ref, s32[3]{0:T(128)S(1)} %pad_add_fusion.place_ref, bf16[512,512]{1,0:T(8,128)(2,1)S(1)} %prepare.1.sorted_ref, bf16[1024,512]{1,0:T(8,128)(2,1)S(1)} %merge.3.branch_ref), custom_call_target="tpu_custom_call" | custom-call | flops 2147483648 | bytes 1048576 | tf_op jit(solution)/shard_map/first/pallas_call | solution.py:219
  35.8 3.7 %all-to-all-start = ((bf16[16,64,256]{2,1,0:T(8,128)(2,1)}), bf16[16,64,256]{2,1,0:T(8,128)(2,1)S(1)}, u32[]{:S(2)}, u32[]{:S(2)}) async-start(bf16[16,64,256]{2,1,0:T(8,128)(2,1)} %bitcast.8), calls=%async_computation | async-start | bytes 1048576 | tf_op jit(solution)/shard_map/all_to_all | solution.py:341
  39.5 0.7 collective-permute-start.16
  40.2 0.1 collective-permute-start.18
  40.3 1.3 %collective-permute-start.23 = (bf16[256,512]{1,0:T(8,128)(2,1)S(1)}, bf16[256,512]{1,0:T(8,128)(2,1)S(1)}, u32[]{:S(2)}, u32[]{:S(2)}) collective-permute-start(bf16[256,512]{1,0:T(8,128)(2,1)S(1)} %get-tuple-element.11.refs_0_), channel_id=1, source_target_pairs={{0,16},{16,0},{1,17},{17,1},{2,18},{18,2},{3,19},{19,3},{4,20},{20... | collective-permute-start | bytes 786440 | tf_op jit(solution)/shard_map/ppermute | solution.py:23
  41.7 0.7 collective-permute-start.17
  42.3 1.8 %collective-permute-start.22 = (bf16[256,512]{1,0:T(8,128)(2,1)S(1)}, bf16[256,512]{1,0:T(8,128)(2,1)S(1)}, u32[]{:S(2)}, u32[]{:S(2)}) collective-permute-start(bf16[256,512]{1,0:T(8,128)(2,1)S(1)} %get-tuple-element.11.refs_0_), channel_id=1, source_target_pairs={{0,2},{2,0},{4,6},{6,4},{8,10},{10,8},{12,14},{14,12},{1,3},{3,1},... | collective-permute-start | bytes 786440 | tf_op jit(solution)/shard_map/ppermute | solution.py:23
  44.1 4.5 %collective-permute-done.16.refs_2_ = bf16[256,512]{1,0:T(8,128)(2,1)S(1)} collective-permute-done((bf16[256,512]{1,0:T(8,128)(2,1)S(1)}, bf16[256,512]{1,0:T(8,128)(2,1)S(1)}, u32[]{:S(2)}, u32[]{:S(2)}) %collective-permute-start.16) | collective-permute-done | bytes 262176 | tf_op jit(solution)/shard_map/ppermute | solution.py:23
  48.7 0.5 collective-permute-start.20
  49.2 5.1 %collective-permute-done.23.refs_2_ = bf16[256,512]{1,0:T(8,128)(2,1)S(1)} collective-permute-done((bf16[256,512]{1,0:T(8,128)(2,1)S(1)}, bf16[256,512]{1,0:T(8,128)(2,1)S(1)}, u32[]{:S(2)}, u32[]{:S(2)}) %collective-permute-start.23) | collective-permute-done | bytes 262176 | tf_op jit(solution)/shard_map/ppermute | solution.py:23
  54.3 1.9 %collective-permute-start.24 = (bf16[256,512]{1,0:T(8,128)(2,1)S(1)}, bf16[256,512]{1,0:T(8,128)(2,1)S(1)}, u32[]{:S(2)}, u32[]{:S(2)}) collective-permute-start(bf16[256,512]{1,0:T(8,128)(2,1)S(1)} %collective-permute-done.23.refs_2_), channel_id=1, source_target_pairs={{0,2},{2,0},{4,6},{6,4},{8,10},{10,8},{12,14},{14,12},{1,3},{3,1},... | collective-permute-start | bytes 786440 | tf_op jit(solution)/shard_map/ppermute | solution.py:23
  56.2 3.2 %collective-permute-done.17.refs_3_ = bf16[256,512]{1,0:T(8,128)(2,1)S(1)} collective-permute-done((bf16[256,512]{1,0:T(8,128)(2,1)S(1)}, bf16[256,512]{1,0:T(8,128)(2,1)S(1)}, u32[]{:S(2)}, u32[]{:S(2)}) %collective-permute-start.17) | collective-permute-done | bytes 262176 | tf_op jit(solution)/shard_map/ppermute | solution.py:23
  59.4 0.5 collective-permute-start.25
  59.9 0.1 collective-permute-start.27
  59.9 0.4 collective-permute-start.26
  60.4 1.1 %collective-permute-done.24.refs_3_ = bf16[256,512]{1,0:T(8,128)(2,1)S(1)} collective-permute-done((bf16[256,512]{1,0:T(8,128)(2,1)S(1)}, bf16[256,512]{1,0:T(8,128)(2,1)S(1)}, u32[]{:S(2)}, u32[]{:S(2)}) %collective-permute-start.24) | collective-permute-done | bytes 262176 | tf_op jit(solution)/shard_map/ppermute | solution.py:23
  61.5 1.9 %merge.4.branch1_ref = bf16[1024,512]{1,0:T(8,128)(2,1)S(1)} custom-call(s32[3]{0:T(128)S(1)} %pad_add_fusion.place_ref, bf16[256,512]{1,0:T(8,128)(2,1)S(1)} %get-tuple-element.12.refs_0_, bf16[256,512]{1,0:T(8,128)(2,1)S(1)} %collective-permute-done.15.refs_1_, bf16[256,512]{1,0:T(8,128)(2,1)S(1)} %collective-permute-done.16.refs_2_, ...), custom_call_target="tpu_custom_call" | custom-call | flops 1073741824 | bytes 3145728 | tf_op jit(solution)/shard_map/merge/pallas_call | solution.py:71
  63.5 1.9 %merge.5.branch2_ref = bf16[1024,512]{1,0:T(8,128)(2,1)S(1)} custom-call(s32[3]{0:T(128)S(1)} %pad_add_fusion.place_ref, bf16[256,512]{1,0:T(8,128)(2,1)S(1)} %get-tuple-element.11.refs_0_, bf16[256,512]{1,0:T(8,128)(2,1)S(1)} %collective-permute-done.22.refs_1_, bf16[256,512]{1,0:T(8,128)(2,1)S(1)} %collective-permute-done.23.refs_2_, ...), custom_call_target="tpu_custom_call" | custom-call | flops 1073741824 | bytes 3145728 | tf_op jit(solution)/shard_map/merge/pallas_call | solution.py:71
  65.4 3.7 %rest.1 = bf16[1024,256]{1,0:T(8,128)(2,1)S(1)} custom-call(s32[3,9]{1,0:T(4,128)S(1)} %add_select_fusion.bits_ref, s32[3]{0:T(128)S(1)} %pad_add_fusion.place_ref, bf16[1024,256]{1,0:T(8,128)(2,1)S(1)} %bitcast.30, bf16[1024,512]{1,0:T(8,128)(2,1)S(1)} %merge.4.branch1_ref, bf16[1024,512]{1,0:T(8,128)(2,1)S(1)} %merge.5.branch2_ref), custom_call_target="tpu_custom_call" | custom-call | flops 5368709120 | bytes 1048576 | tf_op jit(solution)/shard_map/rest/pallas_call | solution.py:219
  69.2 19.9 %all_to_all.10 = bf16[16,64,256]{2,1,0:T(8,128)(2,1)S(1)} all-to-all(bf16[16,64,256]{2,1,0:T(8,128)(2,1)S(1)} %bitcast.31), channel_id=1, replica_groups=mesh['cuts'=2,'wide'=8,'narrow'=2] {'wide','narrow'}, dimensions={0} | all-to-all | bytes 1048576 | tf_op jit(solution)/shard_map/all_to_all | solution.py:341
  89.1 1.6 %widen.1 = f32[2048,128]{1,0:T(8,128)} custom-call(s32[3]{0:T(128)S(1)} %pad_add_fusion.place_ref, bf16[1024,256]{1,0:T(8,128)(2,1)S(1)} %bitcast.29), custom_call_target="tpu_custom_call" | custom-call | tf_op jit(solution)/shard_map/widen/pallas_call | solution.py:247
  (37 shorter events, 0.2 us)
Async XLA Ops:
  0.9 9.1 %collective-permute-start.2 = (bf16[64,512]{1,0:T(8,128)(2,1)S(1)}, bf16[64,512]{1,0:T(8,128)(2,1)S(1)}, u32[]{:S(2)}, u32[]{:S(2)}) collective-permute-start(bf16[64,512]{1,0:T(8,128)(2,1)S(1)} %fusion.1), channel_id=1, source_target_pairs={{0,12},{2,14},{4,8},{6,10},{8,4},{10,6},{12,0},{14,2},{1,13},{3,15... | collective-permute-start | bytes 196616 | tf_op jit(solution)/shard_map/ppermute | solution.py:23
  6.1 5.6 %collective-permute-start.1 = (bf16[64,512]{1,0:T(8,128)(2,1)S(1)}, bf16[64,512]{1,0:T(8,128)(2,1)S(1)}, u32[]{:S(2)}, u32[]{:S(2)}) collective-permute-start(bf16[64,512]{1,0:T(8,128)(2,1)S(1)} %fusion.1), channel_id=1, source_target_pairs={{0,8},{2,10},{4,12},{6,14},{8,0},{10,2},{12,4},{14,6},{1,9},{3,11}... | collective-permute-start | bytes 196616 | tf_op jit(solution)/shard_map/ppermute | solution.py:23
  6.1 5.6 %collective-permute-start = (bf16[64,512]{1,0:T(8,128)(2,1)S(1)}, bf16[64,512]{1,0:T(8,128)(2,1)S(1)}, u32[]{:S(2)}, u32[]{:S(2)}) collective-permute-start(bf16[64,512]{1,0:T(8,128)(2,1)S(1)} %fusion.1), channel_id=1, source_target_pairs={{0,4},{2,6},{4,0},{6,2},{8,12},{10,14},{12,8},{14,10},{1,5},{3,7},... | collective-permute-start | bytes 196616 | tf_op jit(solution)/shard_map/ppermute | solution.py:23
  6.7 0.7 copy-start.2
  7.5 1.2 %copy-start = (f32[2,131072]{1,0:T(2,128)S(1)}, f32[2,131072]{1,0:T(2,128)}, u32[]{:S(2)}) copy-start(f32[2,131072]{1,0:T(2,128)} %param.3) | copy-start | bytes 3145732
  10.0 1.8 %copy-start.1 = (bf16[3,1,2,64,512]{4,3,2,1,0:T(8,128)(2,1)S(1)}, bf16[3,1,2,64,512]{4,3,2,1,0:T(8,128)(2,1)}, u32[]{:S(2)}) copy-start(bf16[3,1,2,64,512]{4,3,2,1,0:T(8,128)(2,1)} %param.4) | copy-start | bytes 1179652
  11.7 3.2 %collective-permute-start.7 = (bf16[256,512]{1,0:T(8,128)(2,1)S(1)}, bf16[256,512]{1,0:T(8,128)(2,1)S(1)}, u32[]{:S(2)}, u32[]{:S(2)}) collective-permute-start(bf16[256,512]{1,0:T(8,128)(2,1)S(1)} %pad_maximum_fusion.1.refs_0_), channel_id=1, source_target_pairs={{0,1},{1,0},{2,3},{3,2},{4,5},{5,4},{6,7},{7,6},{8,9},{9,8},{10,11... | collective-permute-start | bytes 786440 | tf_op jit(solution)/shard_map/ppermute | solution.py:23
  11.8 8.8 %collective-permute-start.3 = (bf16[256,512]{1,0:T(8,128)(2,1)S(1)}, bf16[256,512]{1,0:T(8,128)(2,1)S(1)}, u32[]{:S(2)}, u32[]{:S(2)}) collective-permute-start(bf16[256,512]{1,0:T(8,128)(2,1)S(1)} %pad_maximum_fusion.1.refs_0_), channel_id=1, source_target_pairs={{0,2},{2,0},{4,6},{6,4},{8,10},{10,8},{12,14},{14,12},{1,3},{3,1},... | collective-permute-start | bytes 786440 | tf_op jit(solution)/shard_map/ppermute | solution.py:23
  13.4 8.8 %collective-permute-start.4 = (bf16[256,512]{1,0:T(8,128)(2,1)S(1)}, bf16[256,512]{1,0:T(8,128)(2,1)S(1)}, u32[]{:S(2)}, u32[]{:S(2)}) collective-permute-start(bf16[256,512]{1,0:T(8,128)(2,1)S(1)} %pad_maximum_fusion.1.refs_0_), channel_id=1, source_target_pairs={{0,16},{16,0},{1,17},{17,1},{2,18},{18,2},{3,19},{19,3},{4,20},{20... | collective-permute-start | bytes 786440 | tf_op jit(solution)/shard_map/ppermute | solution.py:23
  14.9 8.8 %collective-permute-start.14 = (bf16[2,64,512]{2,1,0:T(8,128)(2,1)S(1)}, bf16[2,64,512]{2,1,0:T(8,128)(2,1)S(1)}, u32[]{:S(2)}, u32[]{:S(2)}) collective-permute-start(bf16[2,64,512]{2,1,0:T(8,128)(2,1)S(1)} %fusion), channel_id=1, source_target_pairs={{0,12},{2,14},{4,8},{6,10},{8,4},{10,6},{12,0},{14,2},{1,13},{3,15... | collective-permute-start | bytes 393224 | tf_op jit(solution)/shard_map/ppermute | solution.py:23
  17.9 11.3 %collective-permute-start.13 = (bf16[2,64,512]{2,1,0:T(8,128)(2,1)S(1)}, bf16[2,64,512]{2,1,0:T(8,128)(2,1)S(1)}, u32[]{:S(2)}, u32[]{:S(2)}) collective-permute-start(bf16[2,64,512]{2,1,0:T(8,128)(2,1)S(1)} %fusion), channel_id=1, source_target_pairs={{0,8},{2,10},{4,12},{6,14},{8,0},{10,2},{12,4},{14,6},{1,9},{3,11}... | collective-permute-start | bytes 393224 | tf_op jit(solution)/shard_map/ppermute | solution.py:23
  17.9 11.3 %collective-permute-start.12 = (bf16[2,64,512]{2,1,0:T(8,128)(2,1)S(1)}, bf16[2,64,512]{2,1,0:T(8,128)(2,1)S(1)}, u32[]{:S(2)}, u32[]{:S(2)}) collective-permute-start(bf16[2,64,512]{2,1,0:T(8,128)(2,1)S(1)} %fusion), channel_id=1, source_target_pairs={{0,4},{2,6},{4,0},{6,2},{8,12},{10,14},{12,8},{14,10},{1,5},{3,7},... | collective-permute-start | bytes 393224 | tf_op jit(solution)/shard_map/ppermute | solution.py:23
  20.6 8.7 %collective-permute-start.5 = (bf16[128,512]{1,0:T(8,128)(2,1)S(1)}, bf16[128,512]{1,0:T(8,128)(2,1)S(1)}, u32[]{:S(2)}, u32[]{:S(2)}) collective-permute-start(bf16[128,512]{1,0:T(8,128)(2,1)S(1)} %slice.34), channel_id=1, source_target_pairs={{0,16},{16,0},{1,17},{17,1},{2,18},{18,2},{3,19},{19,3},{4,20},{20... | collective-permute-start | bytes 393224 | tf_op jit(solution)/shard_map/ppermute | solution.py:23
  22.2 7.7 %collective-permute-start.6 = (bf16[128,512]{1,0:T(8,128)(2,1)S(1)}, bf16[128,512]{1,0:T(8,128)(2,1)S(1)}, u32[]{:S(2)}, u32[]{:S(2)}) collective-permute-start(bf16[128,512]{1,0:T(8,128)(2,1)S(1)} %slice.35), channel_id=1, source_target_pairs={{0,2},{2,0},{4,6},{6,4},{8,10},{10,8},{12,14},{14,12},{1,3},{3,1},... | collective-permute-start | bytes 393224 | tf_op jit(solution)/shard_map/ppermute | solution.py:23
  23.7 6.9 %collective-permute-start.8 = (bf16[256,512]{1,0:T(8,128)(2,1)S(1)}, bf16[256,512]{1,0:T(8,128)(2,1)S(1)}, u32[]{:S(2)}, u32[]{:S(2)}) collective-permute-start(bf16[256,512]{1,0:T(8,128)(2,1)S(1)} %collective-permute-done.3.refs_1_), channel_id=1, source_target_pairs={{0,1},{1,0},{2,3},{3,2},{4,5},{5,4},{6,7},{7,6},{8,9},{9,8},{10,11... | collective-permute-start | bytes 786440 | tf_op jit(solution)/shard_map/ppermute | solution.py:23
  29.2 1.5 %collective-permute-start.9 = (bf16[256,512]{1,0:T(8,128)(2,1)S(1)}, bf16[256,512]{1,0:T(8,128)(2,1)S(1)}, u32[]{:S(2)}, u32[]{:S(2)}) collective-permute-start(bf16[256,512]{1,0:T(8,128)(2,1)S(1)} %collective-permute-done.4.refs_2_), channel_id=1, source_target_pairs={{0,1},{1,0},{2,3},{3,2},{4,5},{5,4},{6,7},{7,6},{8,9},{9,8},{10,11... | collective-permute-start | bytes 786440 | tf_op jit(solution)/shard_map/ppermute | solution.py:23
  29.3 1.7 %collective-permute-start.10 = (bf16[128,512]{1,0:T(8,128)(2,1)S(1)}, bf16[128,512]{1,0:T(8,128)(2,1)S(1)}, u32[]{:S(2)}, u32[]{:S(2)}) collective-permute-start(bf16[128,512]{1,0:T(8,128)(2,1)S(1)} %collective-permute-done.5.refs_3_), channel_id=1, source_target_pairs={{0,1},{1,0},{2,3},{3,2},{4,5},{5,4},{6,7},{7,6},{8,9},{9,8},{10,11... | collective-permute-start | bytes 393224 | tf_op jit(solution)/shard_map/ppermute | solution.py:23
  29.9 1.3 %collective-permute-start.11 = (bf16[128,512]{1,0:T(8,128)(2,1)S(1)}, bf16[128,512]{1,0:T(8,128)(2,1)S(1)}, u32[]{:S(2)}, u32[]{:S(2)}) collective-permute-start(bf16[128,512]{1,0:T(8,128)(2,1)S(1)} %collective-permute-done.6.refs_4_), channel_id=1, source_target_pairs={{0,1},{1,0},{2,3},{3,2},{4,5},{5,4},{6,7},{7,6},{8,9},{9,8},{10,11... | collective-permute-start | bytes 393224 | tf_op jit(solution)/shard_map/ppermute | solution.py:23
  30.0 11.7 %collective-permute-start.15 = (bf16[256,512]{1,0:T(8,128)(2,1)S(1)}, bf16[256,512]{1,0:T(8,128)(2,1)S(1)}, u32[]{:S(2)}, u32[]{:S(2)}) collective-permute-start(bf16[256,512]{1,0:T(8,128)(2,1)S(1)} %get-tuple-element.12.refs_0_), channel_id=1, source_target_pairs={{0,2},{2,0},{4,6},{6,4},{8,10},{10,8},{12,14},{14,12},{1,3},{3,1},... | collective-permute-start | bytes 786440 | tf_op jit(solution)/shard_map/ppermute | solution.py:23
  35.8 29.6 %all-to-all-start = ((bf16[16,64,256]{2,1,0:T(8,128)(2,1)}), bf16[16,64,256]{2,1,0:T(8,128)(2,1)S(1)}, u32[]{:S(2)}, u32[]{:S(2)}) async-start(bf16[16,64,256]{2,1,0:T(8,128)(2,1)} %bitcast.8), calls=%async_computation | async-start | bytes 1048576 | tf_op jit(solution)/shard_map/all_to_all | solution.py:341
  39.5 9.2 %collective-permute-start.16 = (bf16[256,512]{1,0:T(8,128)(2,1)S(1)}, bf16[256,512]{1,0:T(8,128)(2,1)S(1)}, u32[]{:S(2)}, u32[]{:S(2)}) collective-permute-start(bf16[256,512]{1,0:T(8,128)(2,1)S(1)} %get-tuple-element.12.refs_0_), channel_id=1, source_target_pairs={{0,16},{16,0},{1,17},{17,1},{2,18},{18,2},{3,19},{19,3},{4,20},{20... | collective-permute-start | bytes 786440 | tf_op jit(solution)/shard_map/ppermute | solution.py:23
  40.2 8.4 %collective-permute-start.18 = (bf16[256,512]{1,0:T(8,128)(2,1)S(1)}, bf16[256,512]{1,0:T(8,128)(2,1)S(1)}, u32[]{:S(2)}, u32[]{:S(2)}) collective-permute-start(bf16[256,512]{1,0:T(8,128)(2,1)S(1)} %get-tuple-element.12.refs_0_), channel_id=1, source_target_pairs={{0,1},{1,0},{2,3},{3,2},{4,5},{5,4},{6,7},{7,6},{8,9},{9,8},{10,11... | collective-permute-start | bytes 786440 | tf_op jit(solution)/shard_map/ppermute | solution.py:23
  40.3 14.0 %collective-permute-start.23 = (bf16[256,512]{1,0:T(8,128)(2,1)S(1)}, bf16[256,512]{1,0:T(8,128)(2,1)S(1)}, u32[]{:S(2)}, u32[]{:S(2)}) collective-permute-start(bf16[256,512]{1,0:T(8,128)(2,1)S(1)} %get-tuple-element.11.refs_0_), channel_id=1, source_target_pairs={{0,16},{16,0},{1,17},{17,1},{2,18},{18,2},{3,19},{19,3},{4,20},{20... | collective-permute-start | bytes 786440 | tf_op jit(solution)/shard_map/ppermute | solution.py:23
  41.7 17.7 %collective-permute-start.17 = (bf16[256,512]{1,0:T(8,128)(2,1)S(1)}, bf16[256,512]{1,0:T(8,128)(2,1)S(1)}, u32[]{:S(2)}, u32[]{:S(2)}) collective-permute-start(bf16[256,512]{1,0:T(8,128)(2,1)S(1)} %collective-permute-done.15.refs_1_), channel_id=1, source_target_pairs={{0,16},{16,0},{1,17},{17,1},{2,18},{18,2},{3,19},{19,3},{4,20},{20... | collective-permute-start | bytes 786440 | tf_op jit(solution)/shard_map/ppermute | solution.py:23
  42.3 17.0 %collective-permute-start.22 = (bf16[256,512]{1,0:T(8,128)(2,1)S(1)}, bf16[256,512]{1,0:T(8,128)(2,1)S(1)}, u32[]{:S(2)}, u32[]{:S(2)}) collective-permute-start(bf16[256,512]{1,0:T(8,128)(2,1)S(1)} %get-tuple-element.11.refs_0_), channel_id=1, source_target_pairs={{0,2},{2,0},{4,6},{6,4},{8,10},{10,8},{12,14},{14,12},{1,3},{3,1},... | collective-permute-start | bytes 786440 | tf_op jit(solution)/shard_map/ppermute | solution.py:23
  48.7 11.2 %collective-permute-start.19 = (bf16[256,512]{1,0:T(8,128)(2,1)S(1)}, bf16[256,512]{1,0:T(8,128)(2,1)S(1)}, u32[]{:S(2)}, u32[]{:S(2)}) collective-permute-start(bf16[256,512]{1,0:T(8,128)(2,1)S(1)} %collective-permute-done.15.refs_1_), channel_id=1, source_target_pairs={{0,1},{1,0},{2,3},{3,2},{4,5},{5,4},{6,7},{7,6},{8,9},{9,8},{10,11... | collective-permute-start | bytes 786440 | tf_op jit(solution)/shard_map/ppermute | solution.py:23
  48.7 11.3 %collective-permute-start.20 = (bf16[256,512]{1,0:T(8,128)(2,1)S(1)}, bf16[256,512]{1,0:T(8,128)(2,1)S(1)}, u32[]{:S(2)}, u32[]{:S(2)}) collective-permute-start(bf16[256,512]{1,0:T(8,128)(2,1)S(1)} %collective-permute-done.16.refs_2_), channel_id=1, source_target_pairs={{0,1},{1,0},{2,3},{3,2},{4,5},{5,4},{6,7},{7,6},{8,9},{9,8},{10,11... | collective-permute-start | bytes 786440 | tf_op jit(solution)/shard_map/ppermute | solution.py:23
  54.3 7.2 %collective-permute-start.24 = (bf16[256,512]{1,0:T(8,128)(2,1)S(1)}, bf16[256,512]{1,0:T(8,128)(2,1)S(1)}, u32[]{:S(2)}, u32[]{:S(2)}) collective-permute-start(bf16[256,512]{1,0:T(8,128)(2,1)S(1)} %collective-permute-done.23.refs_2_), channel_id=1, source_target_pairs={{0,2},{2,0},{4,6},{6,4},{8,10},{10,8},{12,14},{14,12},{1,3},{3,1},... | collective-permute-start | bytes 786440 | tf_op jit(solution)/shard_map/ppermute | solution.py:23
  59.4 2.1 %collective-permute-start.21 = (bf16[256,512]{1,0:T(8,128)(2,1)S(1)}, bf16[256,512]{1,0:T(8,128)(2,1)S(1)}, u32[]{:S(2)}, u32[]{:S(2)}) collective-permute-start(bf16[256,512]{1,0:T(8,128)(2,1)S(1)} %collective-permute-done.17.refs_3_), channel_id=1, source_target_pairs={{0,1},{1,0},{2,3},{3,2},{4,5},{5,4},{6,7},{7,6},{8,9},{9,8},{10,11... | collective-permute-start | bytes 786440 | tf_op jit(solution)/shard_map/ppermute | solution.py:23
  59.4 4.1 %collective-permute-start.25 = (bf16[256,512]{1,0:T(8,128)(2,1)S(1)}, bf16[256,512]{1,0:T(8,128)(2,1)S(1)}, u32[]{:S(2)}, u32[]{:S(2)}) collective-permute-start(bf16[256,512]{1,0:T(8,128)(2,1)S(1)} %get-tuple-element.11.refs_0_), channel_id=1, source_target_pairs={{0,1},{1,0},{2,3},{3,2},{4,5},{5,4},{6,7},{7,6},{8,9},{9,8},{10,11... | collective-permute-start | bytes 786440 | tf_op jit(solution)/shard_map/ppermute | solution.py:23
  59.9 3.6 %collective-permute-start.27 = (bf16[256,512]{1,0:T(8,128)(2,1)S(1)}, bf16[256,512]{1,0:T(8,128)(2,1)S(1)}, u32[]{:S(2)}, u32[]{:S(2)}) collective-permute-start(bf16[256,512]{1,0:T(8,128)(2,1)S(1)} %collective-permute-done.23.refs_2_), channel_id=1, source_target_pairs={{0,1},{1,0},{2,3},{3,2},{4,5},{5,4},{6,7},{7,6},{8,9},{9,8},{10,11... | collective-permute-start | bytes 786440 | tf_op jit(solution)/shard_map/ppermute | solution.py:23
  59.9 3.5 %collective-permute-start.26 = (bf16[256,512]{1,0:T(8,128)(2,1)S(1)}, bf16[256,512]{1,0:T(8,128)(2,1)S(1)}, u32[]{:S(2)}, u32[]{:S(2)}) collective-permute-start(bf16[256,512]{1,0:T(8,128)(2,1)S(1)} %collective-permute-done.22.refs_1_), channel_id=1, source_target_pairs={{0,1},{1,0},{2,3},{3,2},{4,5},{5,4},{6,7},{7,6},{8,9},{9,8},{10,11... | collective-permute-start | bytes 786440 | tf_op jit(solution)/shard_map/ppermute | solution.py:23
  61.5 2.0 %collective-permute-start.28 = (bf16[256,512]{1,0:T(8,128)(2,1)S(1)}, bf16[256,512]{1,0:T(8,128)(2,1)S(1)}, u32[]{:S(2)}, u32[]{:S(2)}) collective-permute-start(bf16[256,512]{1,0:T(8,128)(2,1)S(1)} %collective-permute-done.24.refs_3_), channel_id=1, source_target_pairs={{0,1},{1,0},{2,3},{3,2},{4,5},{5,4},{6,7},{7,6},{8,9},{9,8},{10,11... | collective-permute-start | bytes 786440 | tf_op jit(solution)/shard_map/ppermute | solution.py:23

commit v3 on v2

--- a/solution.py
+++ b/solution.py
@@ -230,28 +230,23 @@
     )(bits, place, *operands)
 
 
-def widen_kernel(order, place_ref, amplitude_ref, out_ref):
+def widen_kernel(amplitude_ref, out_ref):
     rows = amplitude_ref.shape[0]
-    low = log2(rows) if order is None else order[0]
-    size = 2**low
-    for block in range(rows // size):
-        start = 0 if order is None else incoming(block * size, place_ref, order)
-        values = amplitude_ref[block * size : (block + 1) * size, :].astype(jnp.float32)
-        start = pl.multiple_of(2 * start, 2 * size)
-        out_ref[pl.ds(start, size, stride=2), :] = values[:, :lanes]
-        out_ref[pl.ds(start + 1, size, stride=2), :] = values[:, lanes:]
-
-
-def widen(place, amplitude, order):
+    wide = amplitude_ref[...].astype(jnp.float32)
+    out_ref[pl.ds(0, rows, stride=2), :] = wide[:, :lanes]
+    out_ref[pl.ds(1, rows, stride=2), :] = wide[:, lanes:]
+
+
+def widen(amplitude):
     rows = amplitude.shape[0]
     return pl.pallas_call(
-        functools.partial(widen_kernel, order),
+        widen_kernel,
         out_shape=jax.ShapeDtypeStruct((2 * rows, lanes), jnp.float32),
-        in_specs=[on_smem(), on_vmem()],
+        in_specs=[on_vmem()],
         out_specs=on_vmem(),
         compiler_params=params(),
         name="widen",
-    )(place, amplitude)
+    )(amplitude)
 
 
 def gather_plain(sub_branch):
@@ -299,9 +294,13 @@
     near1, near2 = after(along(after(mine(1, 3), near0_other[0])), x0, y0)
     x1, y2 = exchange(near1, "wide", 1), exchange(near2, "cuts", 1)
     own1 = [near1, x1, exchange(near1, "cuts", 1), exchange(x1, "cuts", 1)]
-    own2 = [near2, exchange(near2, "wide", 1), y2, exchange(y2, "wide", 1)]
-    second = (own1, from_other_core(own1), layout, block_rows)
-    third = (own2, from_other_core(own2), layout, block_rows)
+    own2 = [near2, y2, exchange(near2, "wide", 1), exchange(y2, "wide", 1)]
+    own1 = [jnp.concatenate(own1[:2]), jnp.concatenate(own1[2:])]
+    own2 = [jnp.concatenate(own2[:2]), jnp.concatenate(own2[2:])]
+    layout1 = [layout[0] + layout[1], layout[2] + layout[3]]
+    layout2 = [layout[0] + layout[2], layout[1] + layout[3]]
+    second = (own1, from_other_core(own1), layout1, block_rows)
+    third = (own2, from_other_core(own2), layout2, block_rows)
     return [first, second, third], (x1, y2)
 
 
@@ -380,7 +379,7 @@
         products=5,
         name="rest",
     )
-    amplitude = widen(place, swap(amplitude, orders[1]), orders[1])
+    amplitude = widen(swap(amplitude, orders[1]))
     return amplitude.reshape(rows, 2, lanes).transpose(1, 0, 2).reshape(2, rows * lanes)
 
 

time: 91 us -> 84.9 us (0.933)
  waiting for transfers between devices: 22.9 us -> 19.5 us
  starting transfers between devices: 29.5 us -> 27.9 us
    ppermute x29 -> x25, waiting for transfers between devices: 22.9 us -> 19.5 us  [exchange(): return lax.ppermute(value, axis, pairs)]
    ppermute x29 -> x25, starting transfers between devices: 25.8 us -> 24.3 us  [exchange(): return lax.ppermute(value, axis, pairs)]
    unnamed x6 -> x8, local copies, waits for them, and re-layouts: 1.91 us -> 1.28 us
  transfers between devices with their start and end apart: 30 -> 26, of which waited for: 10 -> 6; matrix products, arithmetic and copies ran while one was open for 0% -> 0% of each run, Pallas kernels for 11% -> 12%
where the time goes in v3:
time: 84.9 us; the launch traced here: 84.6 us
  starting transfers between devices  27.9 us (33%)
  blocking collectives  19.9 us (23%)
  waiting for transfers between devices  19.5 us (23%)
  Pallas kernels  14.5 us (17%)
  local copies, waits for them, and re-layouts  2.3 us (3%)
    ppermute x25, starting transfers between devices, exchange(): return lax.ppermute(value, axis, pairs)  24.3 us
    all_to_all x1, blocking collectives, swap(): blocks = lax.all_to_all(blocks, ('wide', 'narrow'), 0, 0, tiled=True)  19.9 us
    ppermute x25, waiting for transfers between devices, exchange(): return lax.ppermute(value, axis, pairs)  19.5 us
    pallas_call x3, Pallas kernels, contract(): pl.pallas_call(kernel, out_shape=jax.ShapeDtypeStruct(shape, jnp.bfloat16...  7.69 us
    pallas_call x3, Pallas kernels, merge(): pl.pallas_call(functools.partial(merge_kernel, layout, block_rows), out_s...  5.79 us
    all_to_all x1, starting transfers between devices, swap(): blocks = lax.all_to_all(blocks, ('wide', 'narrow'), 0, 0, tiled=True)  3.57 us
  transfers between devices with their start and end apart: 26, of which 6 were waited for; matrix products, arithmetic and copies ran while one was open for 0% of the time, Pallas kernels for 12%

profile of v3, /device:TPU:0, one launch (start us, length us, event | category | flops | bytes accessed | tf_op | source)
XLA Modules:
  0.0 84.6 jit_solution(18121646253900965591)
XLA Ops:
  0.0 0.9 %slice_bitcast_fusion.2 = bf16[1,2,64,512]{3,2,1,0:T(8,128)(2,1)S(1)} fusion(bf16[3,1,2,64,512]{4,3,2,1,0:T(8,128)(2,1)} %param.4), kind=kLoop, calls=%fused_computation.9 | loop fusion | bytes 262144 | tf_op jit(solution)/shard_map/squeeze | solution.py:278
  0.9 0.0 copy-start.2
  1.0 5.1 %collective-permute-start.2 = (bf16[64,512]{1,0:T(8,128)(2,1)S(1)}, bf16[64,512]{1,0:T(8,128)(2,1)S(1)}, u32[]{:S(2)}, u32[]{:S(2)}) collective-permute-start(bf16[64,512]{1,0:T(8,128)(2,1)S(1)} %fusion.1), channel_id=1, source_target_pairs={{0,12},{2,14},{4,8},{6,10},{8,4},{10,6},{12,0},{14,2},{1,13},{3,15... | collective-permute-start | bytes 196616 | tf_op jit(solution)/shard_map/ppermute | solution.py:23
  6.1 0.6 collective-permute-start
  6.7 0.1 pad_add_fusion.place_ref
  6.8 1.2 %copy-done = f32[2,131072]{1,0:T(2,128)S(1)} copy-done((f32[2,131072]{1,0:T(2,128)S(1)}, f32[2,131072]{1,0:T(2,128)}, u32[]{:S(2)}) %copy-start) | copy-done | bytes 1048600
  8.0 1.3 %prepare.1.sorted_ref = bf16[512,512]{1,0:T(8,128)(2,1)S(1)} custom-call(s32[3,9]{1,0:T(4,128)S(1)} %add_select_fusion.bits_ref, s32[3]{0:T(128)S(1)} %pad_add_fusion.place_ref, f32[2048,128]{1,0:T(8,128)S(1)} %bitcast.32), custom_call_target="tpu_custom_call" | custom-call | flops 1073741824 | bytes 1048576 | tf_op jit(solution)/shard_map/prepare/pallas_call | solution.py:219
  9.3 0.0 copy-start.1
  9.3 2.3 %collective-permute-done.1 = bf16[64,512]{1,0:T(8,128)(2,1)S(1)} collective-permute-done((bf16[64,512]{1,0:T(8,128)(2,1)S(1)}, bf16[64,512]{1,0:T(8,128)(2,1)S(1)}, u32[]{:S(2)}, u32[]{:S(2)}) %collective-permute-start.1) | collective-permute-done | bytes 65568 | tf_op jit(solution)/shard_map/ppermute | solution.py:23
  11.7 0.0 collective-permute-done
  11.7 0.1 collective-permute-start.7
  11.8 1.6 %collective-permute-start.3 = (bf16[256,512]{1,0:T(8,128)(2,1)S(1)}, bf16[256,512]{1,0:T(8,128)(2,1)S(1)}, u32[]{:S(2)}, u32[]{:S(2)}) collective-permute-start(bf16[256,512]{1,0:T(8,128)(2,1)S(1)} %pad_maximum_fusion.3.refs_0_), channel_id=1, source_target_pairs={{0,2},{2,0},{4,6},{6,4},{8,10},{10,8},{12,14},{14,12},{1,3},{3,1},... | collective-permute-start | bytes 786440 | tf_op jit(solution)/shard_map/ppermute | solution.py:23
  13.4 1.5 %collective-permute-start.4 = (bf16[256,512]{1,0:T(8,128)(2,1)S(1)}, bf16[256,512]{1,0:T(8,128)(2,1)S(1)}, u32[]{:S(2)}, u32[]{:S(2)}) collective-permute-start(bf16[256,512]{1,0:T(8,128)(2,1)S(1)} %pad_maximum_fusion.3.refs_0_), channel_id=1, source_target_pairs={{0,16},{16,0},{1,17},{17,1},{2,18},{18,2},{3,19},{19,3},{4,20},{20... | collective-permute-start | bytes 786440 | tf_op jit(solution)/shard_map/ppermute | solution.py:23
  14.9 0.0 collective-permute-done.7.refs_5_
  14.9 2.8 %collective-permute-start.14 = (bf16[2,64,512]{2,1,0:T(8,128)(2,1)S(1)}, bf16[2,64,512]{2,1,0:T(8,128)(2,1)S(1)}, u32[]{:S(2)}, u32[]{:S(2)}) collective-permute-start(bf16[2,64,512]{2,1,0:T(8,128)(2,1)S(1)} %fusion), channel_id=1, source_target_pairs={{0,12},{2,14},{4,8},{6,10},{8,4},{10,6},{12,0},{14,2},{1,13},{3,15... | collective-permute-start | bytes 393224 | tf_op jit(solution)/shard_map/ppermute | solution.py:23
  17.7 1.7 %collective-permute-start.12 = (bf16[2,64,512]{2,1,0:T(8,128)(2,1)S(1)}, bf16[2,64,512]{2,1,0:T(8,128)(2,1)S(1)}, u32[]{:S(2)}, u32[]{:S(2)}) collective-permute-start(bf16[2,64,512]{2,1,0:T(8,128)(2,1)S(1)} %fusion), channel_id=1, source_target_pairs={{0,4},{2,6},{4,0},{6,2},{8,12},{10,14},{12,8},{14,10},{1,5},{3,7},... | collective-permute-start | bytes 393224 | tf_op jit(solution)/shard_map/ppermute | solution.py:23
  19.4 1.2 %collective-permute-done.3.refs_1_ = bf16[256,512]{1,0:T(8,128)(2,1)S(1)} collective-permute-done((bf16[256,512]{1,0:T(8,128)(2,1)S(1)}, bf16[256,512]{1,0:T(8,128)(2,1)S(1)}, u32[]{:S(2)}, u32[]{:S(2)}) %collective-permute-start.3) | collective-permute-done | bytes 262176 | tf_op jit(solution)/shard_map/ppermute | solution.py:23
  20.6 1.6 %collective-permute-start.5 = (bf16[128,512]{1,0:T(8,128)(2,1)S(1)}, bf16[128,512]{1,0:T(8,128)(2,1)S(1)}, u32[]{:S(2)}, u32[]{:S(2)}) collective-permute-start(bf16[128,512]{1,0:T(8,128)(2,1)S(1)} %slice.34), channel_id=1, source_target_pairs={{0,16},{16,0},{1,17},{17,1},{2,18},{18,2},{3,19},{19,3},{4,20},{20... | collective-permute-start | bytes 393224 | tf_op jit(solution)/shard_map/ppermute | solution.py:23
  22.2 1.6 %collective-permute-start.6 = (bf16[128,512]{1,0:T(8,128)(2,1)S(1)}, bf16[128,512]{1,0:T(8,128)(2,1)S(1)}, u32[]{:S(2)}, u32[]{:S(2)}) collective-permute-start(bf16[128,512]{1,0:T(8,128)(2,1)S(1)} %slice.35), channel_id=1, source_target_pairs={{0,2},{2,0},{4,6},{6,4},{8,10},{10,8},{12,14},{14,12},{1,3},{3,1},... | collective-permute-start | bytes 393224 | tf_op jit(solution)/shard_map/ppermute | solution.py:23
  23.7 0.0 collective-permute-done.14
  23.8 5.5 %collective-permute-done.13 = bf16[2,64,512]{2,1,0:T(8,128)(2,1)S(1)} collective-permute-done((bf16[2,64,512]{2,1,0:T(8,128)(2,1)S(1)}, bf16[2,64,512]{2,1,0:T(8,128)(2,1)S(1)}, u32[]{:S(2)}, u32[]{:S(2)}) %collective-permute-start.13) | collective-permute-done | bytes 131104 | tf_op jit(solution)/shard_map/ppermute | solution.py:23
  29.3 0.0 collective-permute-start.9
  29.3 0.0 collective-permute-done.12
  29.3 0.0 collective-permute-done.5.refs_3_
  29.3 0.6 collective-permute-start.10
  29.9 0.1 collective-permute-start.11
  30.0 0.6 collective-permute-start.15
  30.6 0.0 collective-permute-done.8.refs_6_
  30.6 1.0 %collective-permute-start.16 = (bf16[256,512]{1,0:T(8,128)(2,1)S(1)}, bf16[256,512]{1,0:T(8,128)(2,1)S(1)}, u32[]{:S(2)}, u32[]{:S(2)}) collective-permute-start(bf16[256,512]{1,0:T(8,128)(2,1)S(1)} %get-tuple-element.12), channel_id=1, source_target_pairs={{0,16},{16,0},{1,17},{17,1},{2,18},{18,2},{3,19},{19,3},{4,20},{20... | collective-permute-start | bytes 786440 | tf_op jit(solution)/shard_map/ppermute | solution.py:23
  31.6 1.0 %collective-permute-start.20 = (bf16[256,512]{1,0:T(8,128)(2,1)S(1)}, bf16[256,512]{1,0:T(8,128)(2,1)S(1)}, u32[]{:S(2)}, u32[]{:S(2)}) collective-permute-start(bf16[256,512]{1,0:T(8,128)(2,1)S(1)} %get-tuple-element.11), channel_id=1, source_target_pairs={{0,16},{16,0},{1,17},{17,1},{2,18},{18,2},{3,19},{19,3},{4,20},{20... | collective-permute-start | bytes 786440 | tf_op jit(solution)/shard_map/ppermute | solution.py:23
  32.6 1.5 %collective-permute-start.21 = (bf16[256,512]{1,0:T(8,128)(2,1)S(1)}, bf16[256,512]{1,0:T(8,128)(2,1)S(1)}, u32[]{:S(2)}, u32[]{:S(2)}) collective-permute-start(bf16[256,512]{1,0:T(8,128)(2,1)S(1)} %get-tuple-element.11), channel_id=1, source_target_pairs={{0,2},{2,0},{4,6},{6,4},{8,10},{10,8},{12,14},{14,12},{1,3},{3,1},... | collective-permute-start | bytes 786440 | tf_op jit(solution)/shard_map/ppermute | solution.py:23
  34.2 1.9 %merge.3.branch_ref = bf16[1024,512]{1,0:T(8,128)(2,1)S(1)} custom-call(s32[3]{0:T(128)S(1)} %pad_add_fusion.place_ref, bf16[256,512]{1,0:T(8,128)(2,1)S(1)} %pad_maximum_fusion.3.refs_0_, bf16[256,512]{1,0:T(8,128)(2,1)S(1)} %collective-permute-done.3.refs_1_, bf16[256,512]{1,0:T(8,128)(2,1)S(1)} %collective-permute-done.4.refs_2_, ...), custom_call_target="tpu_custom_call" | custom-call | flops 1073741824 | bytes 3145728 | tf_op jit(solution)/shard_map/merge/pallas_call | solution.py:71
  36.1 2.7 %first.1 = bf16[1024,256]{1,0:T(8,128)(2,1)} custom-call(s32[3,9]{1,0:T(4,128)S(1)} %add_select_fusion.bits_ref, s32[3]{0:T(128)S(1)} %pad_add_fusion.place_ref, bf16[512,512]{1,0:T(8,128)(2,1)S(1)} %prepare.1.sorted_ref, bf16[1024,512]{1,0:T(8,128)(2,1)S(1)} %merge.3.branch_ref), custom_call_target="tpu_custom_call" | custom-call | flops 2147483648 | bytes 1048576 | tf_op jit(solution)/shard_map/first/pallas_call | solution.py:219
  38.8 3.6 %all-to-all-start = ((bf16[16,64,256]{2,1,0:T(8,128)(2,1)}), bf16[16,64,256]{2,1,0:T(8,128)(2,1)S(1)}, u32[]{:S(2)}, u32[]{:S(2)}) async-start(bf16[16,64,256]{2,1,0:T(8,128)(2,1)} %bitcast.8), calls=%async_computation | async-start | bytes 1048576 | tf_op jit(solution)/shard_map/all_to_all | solution.py:340
  42.4 0.4 collective-permute-start.18
  42.7 0.9 %collective-permute-start.17 = (bf16[256,512]{1,0:T(8,128)(2,1)S(1)}, bf16[256,512]{1,0:T(8,128)(2,1)S(1)}, u32[]{:S(2)}, u32[]{:S(2)}) collective-permute-start(bf16[256,512]{1,0:T(8,128)(2,1)S(1)} %collective-permute-done.15), channel_id=1, source_target_pairs={{0,16},{16,0},{1,17},{17,1},{2,18},{18,2},{3,19},{19,3},{4,20},{20... | collective-permute-start | bytes 786440 | tf_op jit(solution)/shard_map/ppermute | solution.py:23
  43.6 1.0 %collective-permute-done.20 = bf16[256,512]{1,0:T(8,128)(2,1)S(1)} collective-permute-done((bf16[256,512]{1,0:T(8,128)(2,1)S(1)}, bf16[256,512]{1,0:T(8,128)(2,1)S(1)}, u32[]{:S(2)}, u32[]{:S(2)}) %collective-permute-start.20) | collective-permute-done | bytes 262176 | tf_op jit(solution)/shard_map/ppermute | solution.py:23
  44.6 0.1 collective-permute-start.23
  44.7 1.6 %collective-permute-start.22 = (bf16[256,512]{1,0:T(8,128)(2,1)S(1)}, bf16[256,512]{1,0:T(8,128)(2,1)S(1)}, u32[]{:S(2)}, u32[]{:S(2)}) collective-permute-start(bf16[256,512]{1,0:T(8,128)(2,1)S(1)} %collective-permute-done.20), channel_id=1, source_target_pairs={{0,2},{2,0},{4,6},{6,4},{8,10},{10,8},{12,14},{14,12},{1,3},{3,1},... | collective-permute-start | bytes 786440 | tf_op jit(solution)/shard_map/ppermute | solution.py:23
  46.3 4.8 %collective-permute-done.17 = bf16[256,512]{1,0:T(8,128)(2,1)S(1)} collective-permute-done((bf16[256,512]{1,0:T(8,128)(2,1)S(1)}, bf16[256,512]{1,0:T(8,128)(2,1)S(1)}, u32[]{:S(2)}, u32[]{:S(2)}) %collective-permute-start.17) | collective-permute-done | bytes 262176 | tf_op jit(solution)/shard_map/ppermute | solution.py:23
  51.2 0.1 collective-permute-start.19
  51.3 4.6 %collective-permute-done.22 = bf16[256,512]{1,0:T(8,128)(2,1)S(1)} collective-permute-done((bf16[256,512]{1,0:T(8,128)(2,1)S(1)}, bf16[256,512]{1,0:T(8,128)(2,1)S(1)}, u32[]{:S(2)}, u32[]{:S(2)}) %collective-permute-start.22) | collective-permute-done | bytes 262176 | tf_op jit(solution)/shard_map/ppermute | solution.py:23
  55.9 0.1 collective-permute-start.24
  56.0 1.9 %merge.4.branch1_ref = bf16[1024,512]{1,0:T(8,128)(2,1)S(1)} custom-call(s32[3]{0:T(128)S(1)} %pad_add_fusion.place_ref, bf16[512,512]{1,0:T(8,128)(2,1)S(1)} %pad_maximum_fusion.1.refs_0_, bf16[512,512]{1,0:T(8,128)(2,1)S(1)} %constant_dynamic-update-slice_fusion.refs_1_, bf16[512,512]{1,0:T(8,128)(2,1)S(1)} %collective-permute-done.18.refs_2_, ...), custom_call_target="tpu_custom_call" | custom-call | flops 1073741824 | bytes 3145728 | tf_op jit(solution)/shard_map/merge/pallas_call | solution.py:71
  58.0 1.9 %merge.5.branch2_ref = bf16[1024,512]{1,0:T(8,128)(2,1)S(1)} custom-call(s32[3]{0:T(128)S(1)} %pad_add_fusion.place_ref, bf16[512,512]{1,0:T(8,128)(2,1)S(1)} %pad_maximum_fusion.2.refs_0_, bf16[512,512]{1,0:T(8,128)(2,1)S(1)} %constant_dynamic-update-slice_fusion.2.refs_1_, bf16[512,512]{1,0:T(8,128)(2,1)S(1)} %collective-permute-done.23.refs_2_, ...), custom_call_target="tpu_custom_call" | custom-call | flops 1073741824 | bytes 3145728 | tf_op jit(solution)/shard_map/merge/pallas_call | solution.py:71
  60.0 3.7 %rest.1 = bf16[1024,256]{1,0:T(8,128)(2,1)S(1)} custom-call(s32[3,9]{1,0:T(4,128)S(1)} %add_select_fusion.bits_ref, s32[3]{0:T(128)S(1)} %pad_add_fusion.place_ref, bf16[1024,256]{1,0:T(8,128)(2,1)S(1)} %bitcast.30, bf16[1024,512]{1,0:T(8,128)(2,1)S(1)} %merge.4.branch1_ref, bf16[1024,512]{1,0:T(8,128)(2,1)S(1)} %merge.5.branch2_ref), custom_call_target="tpu_custom_call" | custom-call | flops 5368709120 | bytes 1048576 | tf_op jit(solution)/shard_map/rest/pallas_call | solution.py:219
  63.7 19.9 %all_to_all.10 = bf16[16,64,256]{2,1,0:T(8,128)(2,1)S(1)} all-to-all(bf16[16,64,256]{2,1,0:T(8,128)(2,1)S(1)} %bitcast.31), channel_id=1, replica_groups=mesh['cuts'=2,'wide'=8,'narrow'=2] {'wide','narrow'}, dimensions={0} | all-to-all | bytes 1048576 | tf_op jit(solution)/shard_map/all_to_all | solution.py:340
  83.6 1.0 %widen.1 = f32[2048,128]{1,0:T(8,128)} custom-call(bf16[1024,256]{1,0:T(8,128)(2,1)S(1)} %bitcast.29), custom_call_target="tpu_custom_call" | custom-call | tf_op jit(solution)/shard_map/widen/pallas_call | solution.py:242
  (35 shorter events, 0.3 us)
Async XLA Ops:
  0.9 5.8 %copy-start.2 = (s32[3,9]{1,0:T(4,128)S(1)}, s32[3,9]{1,0:T(4,128)}, u32[]{:S(2)}) copy-start(s32[3,9]{1,0:T(4,128)} %param.5) | copy-start | bytes 328
  1.0 8.4 %collective-permute-start.2 = (bf16[64,512]{1,0:T(8,128)(2,1)S(1)}, bf16[64,512]{1,0:T(8,128)(2,1)S(1)}, u32[]{:S(2)}, u32[]{:S(2)}) collective-permute-start(bf16[64,512]{1,0:T(8,128)(2,1)S(1)} %fusion.1), channel_id=1, source_target_pairs={{0,12},{2,14},{4,8},{6,10},{8,4},{10,6},{12,0},{14,2},{1,13},{3,15... | collective-permute-start | bytes 196616 | tf_op jit(solution)/shard_map/ppermute | solution.py:23
  6.1 5.6 %collective-permute-start.1 = (bf16[64,512]{1,0:T(8,128)(2,1)S(1)}, bf16[64,512]{1,0:T(8,128)(2,1)S(1)}, u32[]{:S(2)}, u32[]{:S(2)}) collective-permute-start(bf16[64,512]{1,0:T(8,128)(2,1)S(1)} %fusion.1), channel_id=1, source_target_pairs={{0,8},{2,10},{4,12},{6,14},{8,0},{10,2},{12,4},{14,6},{1,9},{3,11}... | collective-permute-start | bytes 196616 | tf_op jit(solution)/shard_map/ppermute | solution.py:23
  6.1 5.6 %collective-permute-start = (bf16[64,512]{1,0:T(8,128)(2,1)S(1)}, bf16[64,512]{1,0:T(8,128)(2,1)S(1)}, u32[]{:S(2)}, u32[]{:S(2)}) collective-permute-start(bf16[64,512]{1,0:T(8,128)(2,1)S(1)} %fusion.1), channel_id=1, source_target_pairs={{0,4},{2,6},{4,0},{6,2},{8,12},{10,14},{12,8},{14,10},{1,5},{3,7},... | collective-permute-start | bytes 196616 | tf_op jit(solution)/shard_map/ppermute | solution.py:23
  6.8 1.2 %copy-start = (f32[2,131072]{1,0:T(2,128)S(1)}, f32[2,131072]{1,0:T(2,128)}, u32[]{:S(2)}) copy-start(f32[2,131072]{1,0:T(2,128)} %param.3) | copy-start | bytes 3145732
  9.3 2.5 %copy-start.1 = (bf16[3,1,2,64,512]{4,3,2,1,0:T(8,128)(2,1)S(1)}, bf16[3,1,2,64,512]{4,3,2,1,0:T(8,128)(2,1)}, u32[]{:S(2)}) copy-start(bf16[3,1,2,64,512]{4,3,2,1,0:T(8,128)(2,1)} %param.4) | copy-start | bytes 1179652
  11.7 3.2 %collective-permute-start.7 = (bf16[256,512]{1,0:T(8,128)(2,1)S(1)}, bf16[256,512]{1,0:T(8,128)(2,1)S(1)}, u32[]{:S(2)}, u32[]{:S(2)}) collective-permute-start(bf16[256,512]{1,0:T(8,128)(2,1)S(1)} %pad_maximum_fusion.3.refs_0_), channel_id=1, source_target_pairs={{0,1},{1,0},{2,3},{3,2},{4,5},{5,4},{6,7},{7,6},{8,9},{9,8},{10,11... | collective-permute-start | bytes 786440 | tf_op jit(solution)/shard_map/ppermute | solution.py:23
  11.8 8.8 %collective-permute-start.3 = (bf16[256,512]{1,0:T(8,128)(2,1)S(1)}, bf16[256,512]{1,0:T(8,128)(2,1)S(1)}, u32[]{:S(2)}, u32[]{:S(2)}) collective-permute-start(bf16[256,512]{1,0:T(8,128)(2,1)S(1)} %pad_maximum_fusion.3.refs_0_), channel_id=1, source_target_pairs={{0,2},{2,0},{4,6},{6,4},{8,10},{10,8},{12,14},{14,12},{1,3},{3,1},... | collective-permute-start | bytes 786440 | tf_op jit(solution)/shard_map/ppermute | solution.py:23
  13.4 8.8 %collective-permute-start.4 = (bf16[256,512]{1,0:T(8,128)(2,1)S(1)}, bf16[256,512]{1,0:T(8,128)(2,1)S(1)}, u32[]{:S(2)}, u32[]{:S(2)}) collective-permute-start(bf16[256,512]{1,0:T(8,128)(2,1)S(1)} %pad_maximum_fusion.3.refs_0_), channel_id=1, source_target_pairs={{0,16},{16,0},{1,17},{17,1},{2,18},{18,2},{3,19},{19,3},{4,20},{20... | collective-permute-start | bytes 786440 | tf_op jit(solution)/shard_map/ppermute | solution.py:23
  14.9 8.8 %collective-permute-start.14 = (bf16[2,64,512]{2,1,0:T(8,128)(2,1)S(1)}, bf16[2,64,512]{2,1,0:T(8,128)(2,1)S(1)}, u32[]{:S(2)}, u32[]{:S(2)}) collective-permute-start(bf16[2,64,512]{2,1,0:T(8,128)(2,1)S(1)} %fusion), channel_id=1, source_target_pairs={{0,12},{2,14},{4,8},{6,10},{8,4},{10,6},{12,0},{14,2},{1,13},{3,15... | collective-permute-start | bytes 393224 | tf_op jit(solution)/shard_map/ppermute | solution.py:23
  17.7 11.6 %collective-permute-start.13 = (bf16[2,64,512]{2,1,0:T(8,128)(2,1)S(1)}, bf16[2,64,512]{2,1,0:T(8,128)(2,1)S(1)}, u32[]{:S(2)}, u32[]{:S(2)}) collective-permute-start(bf16[2,64,512]{2,1,0:T(8,128)(2,1)S(1)} %fusion), channel_id=1, source_target_pairs={{0,8},{2,10},{4,12},{6,14},{8,0},{10,2},{12,4},{14,6},{1,9},{3,11}... | collective-permute-start | bytes 393224 | tf_op jit(solution)/shard_map/ppermute | solution.py:23
  17.7 11.6 %collective-permute-start.12 = (bf16[2,64,512]{2,1,0:T(8,128)(2,1)S(1)}, bf16[2,64,512]{2,1,0:T(8,128)(2,1)S(1)}, u32[]{:S(2)}, u32[]{:S(2)}) collective-permute-start(bf16[2,64,512]{2,1,0:T(8,128)(2,1)S(1)} %fusion), channel_id=1, source_target_pairs={{0,4},{2,6},{4,0},{6,2},{8,12},{10,14},{12,8},{14,10},{1,5},{3,7},... | collective-permute-start | bytes 393224 | tf_op jit(solution)/shard_map/ppermute | solution.py:23
  20.6 8.7 %collective-permute-start.5 = (bf16[128,512]{1,0:T(8,128)(2,1)S(1)}, bf16[128,512]{1,0:T(8,128)(2,1)S(1)}, u32[]{:S(2)}, u32[]{:S(2)}) collective-permute-start(bf16[128,512]{1,0:T(8,128)(2,1)S(1)} %slice.34), channel_id=1, source_target_pairs={{0,16},{16,0},{1,17},{17,1},{2,18},{18,2},{3,19},{19,3},{4,20},{20... | collective-permute-start | bytes 393224 | tf_op jit(solution)/shard_map/ppermute | solution.py:23
  22.2 7.7 %collective-permute-start.6 = (bf16[128,512]{1,0:T(8,128)(2,1)S(1)}, bf16[128,512]{1,0:T(8,128)(2,1)S(1)}, u32[]{:S(2)}, u32[]{:S(2)}) collective-permute-start(bf16[128,512]{1,0:T(8,128)(2,1)S(1)} %slice.35), channel_id=1, source_target_pairs={{0,2},{2,0},{4,6},{6,4},{8,10},{10,8},{12,14},{14,12},{1,3},{3,1},... | collective-permute-start | bytes 393224 | tf_op jit(solution)/shard_map/ppermute | solution.py:23
  23.7 6.9 %collective-permute-start.8 = (bf16[256,512]{1,0:T(8,128)(2,1)S(1)}, bf16[256,512]{1,0:T(8,128)(2,1)S(1)}, u32[]{:S(2)}, u32[]{:S(2)}) collective-permute-start(bf16[256,512]{1,0:T(8,128)(2,1)S(1)} %collective-permute-done.3.refs_1_), channel_id=1, source_target_pairs={{0,1},{1,0},{2,3},{3,2},{4,5},{5,4},{6,7},{7,6},{8,9},{9,8},{10,11... | collective-permute-start | bytes 786440 | tf_op jit(solution)/shard_map/ppermute | solution.py:23
  29.3 2.4 %collective-permute-start.9 = (bf16[256,512]{1,0:T(8,128)(2,1)S(1)}, bf16[256,512]{1,0:T(8,128)(2,1)S(1)}, u32[]{:S(2)}, u32[]{:S(2)}) collective-permute-start(bf16[256,512]{1,0:T(8,128)(2,1)S(1)} %collective-permute-done.4.refs_2_), channel_id=1, source_target_pairs={{0,1},{1,0},{2,3},{3,2},{4,5},{5,4},{6,7},{7,6},{8,9},{9,8},{10,11... | collective-permute-start | bytes 786440 | tf_op jit(solution)/shard_map/ppermute | solution.py:23
  29.3 3.3 %collective-permute-start.10 = (bf16[128,512]{1,0:T(8,128)(2,1)S(1)}, bf16[128,512]{1,0:T(8,128)(2,1)S(1)}, u32[]{:S(2)}, u32[]{:S(2)}) collective-permute-start(bf16[128,512]{1,0:T(8,128)(2,1)S(1)} %collective-permute-done.5.refs_3_), channel_id=1, source_target_pairs={{0,1},{1,0},{2,3},{3,2},{4,5},{5,4},{6,7},{7,6},{8,9},{9,8},{10,11... | collective-permute-start | bytes 393224 | tf_op jit(solution)/shard_map/ppermute | solution.py:23
  29.9 4.3 %collective-permute-start.11 = (bf16[128,512]{1,0:T(8,128)(2,1)S(1)}, bf16[128,512]{1,0:T(8,128)(2,1)S(1)}, u32[]{:S(2)}, u32[]{:S(2)}) collective-permute-start(bf16[128,512]{1,0:T(8,128)(2,1)S(1)} %collective-permute-done.6.refs_4_), channel_id=1, source_target_pairs={{0,1},{1,0},{2,3},{3,2},{4,5},{5,4},{6,7},{7,6},{8,9},{9,8},{10,11... | collective-permute-start | bytes 393224 | tf_op jit(solution)/shard_map/ppermute | solution.py:23
  30.0 12.3 %collective-permute-start.15 = (bf16[256,512]{1,0:T(8,128)(2,1)S(1)}, bf16[256,512]{1,0:T(8,128)(2,1)S(1)}, u32[]{:S(2)}, u32[]{:S(2)}) collective-permute-start(bf16[256,512]{1,0:T(8,128)(2,1)S(1)} %get-tuple-element.12), channel_id=1, source_target_pairs={{0,2},{2,0},{4,6},{6,4},{8,10},{10,8},{12,14},{14,12},{1,3},{3,1},... | collective-permute-start | bytes 786440 | tf_op jit(solution)/shard_map/ppermute | solution.py:23
  30.6 14.1 %collective-permute-start.16 = (bf16[256,512]{1,0:T(8,128)(2,1)S(1)}, bf16[256,512]{1,0:T(8,128)(2,1)S(1)}, u32[]{:S(2)}, u32[]{:S(2)}) collective-permute-start(bf16[256,512]{1,0:T(8,128)(2,1)S(1)} %get-tuple-element.12), channel_id=1, source_target_pairs={{0,16},{16,0},{1,17},{17,1},{2,18},{18,2},{3,19},{19,3},{4,20},{20... | collective-permute-start | bytes 786440 | tf_op jit(solution)/shard_map/ppermute | solution.py:23
  31.6 13.0 %collective-permute-start.20 = (bf16[256,512]{1,0:T(8,128)(2,1)S(1)}, bf16[256,512]{1,0:T(8,128)(2,1)S(1)}, u32[]{:S(2)}, u32[]{:S(2)}) collective-permute-start(bf16[256,512]{1,0:T(8,128)(2,1)S(1)} %get-tuple-element.11), channel_id=1, source_target_pairs={{0,16},{16,0},{1,17},{17,1},{2,18},{18,2},{3,19},{19,3},{4,20},{20... | collective-permute-start | bytes 786440 | tf_op jit(solution)/shard_map/ppermute | solution.py:23
  32.6 13.7 %collective-permute-start.21 = (bf16[256,512]{1,0:T(8,128)(2,1)S(1)}, bf16[256,512]{1,0:T(8,128)(2,1)S(1)}, u32[]{:S(2)}, u32[]{:S(2)}) collective-permute-start(bf16[256,512]{1,0:T(8,128)(2,1)S(1)} %get-tuple-element.11), channel_id=1, source_target_pairs={{0,2},{2,0},{4,6},{6,4},{8,10},{10,8},{12,14},{14,12},{1,3},{3,1},... | collective-permute-start | bytes 786440 | tf_op jit(solution)/shard_map/ppermute | solution.py:23
  38.8 21.2 %all-to-all-start = ((bf16[16,64,256]{2,1,0:T(8,128)(2,1)}), bf16[16,64,256]{2,1,0:T(8,128)(2,1)S(1)}, u32[]{:S(2)}, u32[]{:S(2)}) async-start(bf16[16,64,256]{2,1,0:T(8,128)(2,1)} %bitcast.8), calls=%async_computation | async-start | bytes 1048576 | tf_op jit(solution)/shard_map/all_to_all | solution.py:340
  42.4 13.6 %collective-permute-start.18 = (bf16[512,512]{1,0:T(8,128)(2,1)S(1)}, bf16[512,512]{1,0:T(8,128)(2,1)S(1)}, u32[]{:S(2)}, u32[]{:S(2)}) collective-permute-start(bf16[512,512]{1,0:T(8,128)(2,1)S(1)} %pad_maximum_fusion.1.refs_0_), channel_id=1, source_target_pairs={{0,1},{1,0},{2,3},{3,2},{4,5},{5,4},{6,7},{7,6},{8,9},{9,8},{10,11... | collective-permute-start | bytes 1572872 | tf_op jit(solution)/shard_map/ppermute | solution.py:23
  42.7 8.4 %collective-permute-start.17 = (bf16[256,512]{1,0:T(8,128)(2,1)S(1)}, bf16[256,512]{1,0:T(8,128)(2,1)S(1)}, u32[]{:S(2)}, u32[]{:S(2)}) collective-permute-start(bf16[256,512]{1,0:T(8,128)(2,1)S(1)} %collective-permute-done.15), channel_id=1, source_target_pairs={{0,16},{16,0},{1,17},{17,1},{2,18},{18,2},{3,19},{19,3},{4,20},{20... | collective-permute-start | bytes 786440 | tf_op jit(solution)/shard_map/ppermute | solution.py:23
  44.6 13.3 %collective-permute-start.23 = (bf16[512,512]{1,0:T(8,128)(2,1)S(1)}, bf16[512,512]{1,0:T(8,128)(2,1)S(1)}, u32[]{:S(2)}, u32[]{:S(2)}) collective-permute-start(bf16[512,512]{1,0:T(8,128)(2,1)S(1)} %pad_maximum_fusion.2.refs_0_), channel_id=1, source_target_pairs={{0,1},{1,0},{2,3},{3,2},{4,5},{5,4},{6,7},{7,6},{8,9},{9,8},{10,11... | collective-permute-start | bytes 1572872 | tf_op jit(solution)/shard_map/ppermute | solution.py:23
  44.7 11.2 %collective-permute-start.22 = (bf16[256,512]{1,0:T(8,128)(2,1)S(1)}, bf16[256,512]{1,0:T(8,128)(2,1)S(1)}, u32[]{:S(2)}, u32[]{:S(2)}) collective-permute-start(bf16[256,512]{1,0:T(8,128)(2,1)S(1)} %collective-permute-done.20), channel_id=1, source_target_pairs={{0,2},{2,0},{4,6},{6,4},{8,10},{10,8},{12,14},{14,12},{1,3},{3,1},... | collective-permute-start | bytes 786440 | tf_op jit(solution)/shard_map/ppermute | solution.py:23
  51.2 4.8 %collective-permute-start.19 = (bf16[512,512]{1,0:T(8,128)(2,1)S(1)}, bf16[512,512]{1,0:T(8,128)(2,1)S(1)}, u32[]{:S(2)}, u32[]{:S(2)}) collective-permute-start(bf16[512,512]{1,0:T(8,128)(2,1)S(1)} %constant_dynamic-update-slice_fusion.refs_1_), channel_id=1, source_target_pairs={{0,1},{1,0},{2,3},{3,2},{4,5},{5,4},{6,7},{7,6},{8,9},{9,8},{10,11... | collective-permute-start | bytes 1572872 | tf_op jit(solution)/shard_map/ppermute | solution.py:23
  55.9 2.1 %collective-permute-start.24 = (bf16[512,512]{1,0:T(8,128)(2,1)S(1)}, bf16[512,512]{1,0:T(8,128)(2,1)S(1)}, u32[]{:S(2)}, u32[]{:S(2)}) collective-permute-start(bf16[512,512]{1,0:T(8,128)(2,1)S(1)} %constant_dynamic-update-slice_fusion.2.refs_1_), channel_id=1, source_target_pairs={{0,1},{1,0},{2,3},{3,2},{4,5},{5,4},{6,7},{7,6},{8,9},{9,8},{10,11... | collective-permute-start | bytes 1572872 | tf_op jit(solution)/shard_map/ppermute | solution.py:23

commit v4 on v3

--- a/solution.py
+++ b/solution.py
@@ -10,7 +10,6 @@
 lane_bits = 7
 lanes = 2**lane_bits
 vmem_budget = 24 * 2**20
-permute_swaps = (False, False)
 
 
 def log2(size):
@@ -115,24 +114,6 @@
 branch_rows = 256
 
 
-def outgoing(plain, place_ref, order):
-    if order is None:
-        return plain
-    low, cores = order
-    block = jnp.bitwise_xor(jnp.right_shift(plain, low), place_ref[0] * cores + place_ref[2])
-    blocks = plain.shape[1] >> low
-    core, wide = jnp.bitwise_and(block, cores - 1), jnp.right_shift(block, log2(cores))
-    position = core * (blocks // cores) + wide
-    return jnp.left_shift(position, low) + jnp.bitwise_and(plain, 2**low - 1)
-
-
-def incoming(number, place_ref, order):
-    if order is None:
-        return number
-    low, cores = order
-    return jnp.bitwise_xor(number, jnp.left_shift(place_ref[0] * cores + place_ref[2], low))
-
-
 def order_of(bits_ref, which):
     count = bits_ref.shape[1]
     chosen = [bits_ref[which, k] for k in range(count)]
@@ -173,7 +154,7 @@
         ).astype(jnp.bfloat16)
 
 
-def prepare_kernel(bits_ref, place_ref, stem_ref, sorted_ref):
+def prepare_kernel(bits_ref, stem_ref, sorted_ref):
     rows = stem_ref.shape[0] // 2
     stem = jnp.concatenate(
         [stem_ref[pl.ds(part, rows, stride=2), :].astype(jnp.bfloat16) for part in range(2)],
@@ -182,36 +163,26 @@
     permute_into(sorted_ref, to_sorted(row_numbers(rows), *order_of(bits_ref, 0)), stem)
 
 
-def first_kernel(order, bits_ref, place_ref, sorted_ref, branch_ref, result_ref, product_ref):
+def first_kernel(bits_ref, sorted_ref, branch_ref, result_ref, product_ref):
     multiply_into(product_ref, branch_ref, sorted_ref)
     target = to_plain(row_numbers(result_ref.shape[0]), *order_of(bits_ref, 0))
-    restore_into(result_ref, outgoing(target, place_ref, order), product_ref)
+    restore_into(result_ref, target, product_ref)
 
 
 def rest_kernel(
-    orders,
-    bits_ref,
-    place_ref,
-    amplitude_ref,
-    branch1_ref,
-    branch2_ref,
-    result_ref,
-    sorted_ref,
-    product_ref,
+    bits_ref, amplitude_ref, branch1_ref, branch2_ref, result_ref, sorted_ref, product_ref
 ):
     numbers = row_numbers(result_ref.shape[0])
     second, third = order_of(bits_ref, 1), order_of(bits_ref, 2)
-    target = to_sorted(incoming(numbers, place_ref, orders[0]), *second)
-    permute_into(sorted_ref, target, amplitude_ref[...])
+    permute_into(sorted_ref, to_sorted(numbers, *second), amplitude_ref[...])
     multiply_into(product_ref, branch1_ref, sorted_ref)
     between = to_sorted(to_plain(numbers, *second), *third)
     permute_into(sorted_ref, between, product_ref[...])
     multiply_into(product_ref, branch2_ref, sorted_ref)
-    target = outgoing(to_plain(numbers, *third), place_ref, orders[1])
-    restore_into(result_ref, target, product_ref)
-
-
-def contract(kernel, bits, place, operands, rows, shape, scratch, products, name):
+    restore_into(result_ref, to_plain(numbers, *third), product_ref)
+
+
+def contract(kernel, bits, operands, rows, shape, scratch, products, name):
     shapes = [
         pltpu.VMEM((rows // 2, 4 * lanes), jnp.bfloat16),
         pltpu.VMEM((rows, 2 * lanes), jnp.bfloat16),
@@ -219,7 +190,7 @@
     return pl.pallas_call(
         kernel,
         out_shape=jax.ShapeDtypeStruct(shape, jnp.bfloat16),
-        in_specs=[on_smem()] * 2 + [on_vmem()] * len(operands),
+        in_specs=[on_smem()] + [on_vmem()] * len(operands),
         out_specs=on_vmem(),
         scratch_shapes=shapes[2 - scratch :],
         compiler_params=params(),
@@ -227,7 +198,7 @@
             flops=4 * products * rows * rows * 2 * lanes, bytes_accessed=2**20, transcendentals=0
         ),
         name=name,
-    )(bits, place, *operands)
+    )(bits, *operands)
 
 
 def widen_kernel(amplitude_ref, out_ref):
@@ -301,7 +272,7 @@
     layout2 = [layout[0] + layout[2], layout[1] + layout[3]]
     second = (own1, from_other_core(own1), layout1, block_rows)
     third = (own2, from_other_core(own2), layout2, block_rows)
-    return [first, second, third], (x1, y2)
+    return [first, second, third]
 
 
 def gather_factors(sub_branches, ready):
@@ -314,7 +285,7 @@
     if shared:
         return gather_shared(sub_branches, ready)
     count = sub_branches.shape[0]
-    return [gather_plain(sub_branches[which, 0]) for which in range(count)], ()
+    return [gather_plain(sub_branches[which, 0]) for which in range(count)]
 
 
 def shards(stem_tensor, sub_branches, branch_bits):
@@ -330,28 +301,16 @@
         branch_bits < local_bits, branch_bits - lane_bits, branch_bits - local_bits + low_bits
     )
 
-    small = rows // devices >= 16 and wide_count <= 8 and narrow_count == 2
-    permuted = (low_bits, narrow_count)
-    orders = [permuted if small and use else None for use in permute_swaps]
-
-    def swap(amplitude, order):
-        if order is None:
-            blocks = amplitude.reshape(devices, rows // devices, 2 * lanes)
-            blocks = lax.all_to_all(blocks, ("wide", "narrow"), 0, 0, tiled=True)
-            return blocks.reshape(rows, 2 * lanes)
-        size, half = 2**low_bits, rows // 2
-        other = exchange(amplitude[half:], "narrow", 1)
-        pairs = [
-            jnp.concatenate([amplitude[at : at + size], other[at : at + size]])
-            for at in range(0, half, size)
-        ]
-        pairs = [pair if mask == 0 else exchange(pair, "wide", mask) for mask, pair in enumerate(pairs)]
-        return jnp.concatenate(pairs)
+
+    def swap(amplitude):
+        blocks = amplitude.reshape(devices, rows // devices, 2 * lanes)
+        blocks = lax.all_to_all(blocks, ("wide", "narrow"), 0, 0, tiled=True)
+        return blocks.reshape(rows, 2 * lanes)
 
     stem = stem_tensor.reshape(2, rows, lanes).transpose(1, 0, 2).reshape(2 * rows, lanes)
     width = sub_branches.shape[-1]
     plain = (rows, 2 * lanes)
-    run = functools.partial(contract, bits=positions, place=place, rows=rows)
+    run = functools.partial(contract, bits=positions, rows=rows)
     ordered = run(
         prepare_kernel,
         operands=[stem],
@@ -360,26 +319,26 @@
         products=1,
         name="prepare",
     )
-    factors, sent = gather_factors(sub_branches, ordered)
+    factors = gather_factors(sub_branches, ordered)
     branch0, branch1, branch2 = [merge(place, *each) for each in factors]
     amplitude = run(
-        functools.partial(first_kernel, orders[0]),
+        first_kernel,
         operands=[ordered, branch0],
         shape=plain,
         scratch=1,
         products=2,
         name="first",
     )
-    amplitude = swap(amplitude, orders[0])
+    amplitude = swap(amplitude)
     amplitude = run(
-        functools.partial(rest_kernel, orders),
+        rest_kernel,
         operands=[amplitude, branch1, branch2],
         shape=plain,
         scratch=2,
         products=5,
         name="rest",
     )
-    amplitude = widen(swap(amplitude, orders[1]))
+    amplitude = widen(swap(amplitude))
     return amplitude.reshape(rows, 2, lanes).transpose(1, 0, 2).reshape(2, rows * lanes)
 
 

time: 84.9 us -> 86.3 us (1.016)
  waiting for transfers between devices: 19.5 us -> 22.5 us
  starting transfers between devices: 27.9 us -> 26.5 us
    ppermute x25, waiting for transfers between devices: 19.5 us -> 22.5 us  [exchange(): return lax.ppermute(value, axis, pairs)]
    ppermute x25, starting transfers between devices: 24.3 us -> 22.9 us  [exchange(): return lax.ppermute(value, axis, pairs)]
  transfers between devices with their start and end apart: 26 -> 26, of which waited for: 6 -> 7; matrix products, arithmetic and copies ran while one was open for 0% -> 0% of each run, Pallas kernels for 12% -> 11%
where the time goes in v4:
time: 86.3 us; the launch traced here: 86 us
  starting transfers between devices  26.5 us (31%)
  waiting for transfers between devices  22.5 us (26%)
  blocking collectives  19.7 us (23%)
  Pallas kernels  14.5 us (17%)
  local copies, waits for them, and re-layouts  2.29 us (3%)
    ppermute x25, starting transfers between devices, exchange(): return lax.ppermute(value, axis, pairs)  22.9 us
    ppermute x25, waiting for transfers between devices, exchange(): return lax.ppermute(value, axis, pairs)  22.5 us
    all_to_all x1, blocking collectives, swap(): blocks = lax.all_to_all(blocks, ('wide', 'narrow'), 0, 0, tiled=True)  19.7 us
    pallas_call x3, Pallas kernels, contract(): pl.pallas_call(kernel, out_shape=jax.ShapeDtypeStruct(shape, jnp.bfloat16...  7.69 us
    pallas_call x3, Pallas kernels, merge(): pl.pallas_call(functools.partial(merge_kernel, layout, block_rows), out_s...  5.79 us
    all_to_all x1, starting transfers between devices, swap(): blocks = lax.all_to_all(blocks, ('wide', 'narrow'), 0, 0, tiled=True)  3.57 us
  transfers between devices with their start and end apart: 26, of which 7 were waited for; matrix products, arithmetic and copies ran while one was open for 0% of the time, Pallas kernels for 11%

profile of v4, /device:TPU:0, one launch (start us, length us, event | category | flops | bytes accessed | tf_op | source)
XLA Modules:
  0.0 86.0 jit_solution(4135873455721290994)
XLA Ops:
  0.0 0.9 %slice_bitcast_fusion.2 = bf16[1,2,64,512]{3,2,1,0:T(8,128)(2,1)S(1)} fusion(bf16[3,1,2,64,512]{4,3,2,1,0:T(8,128)(2,1)} %param.4), kind=kLoop, calls=%fused_computation.9 | loop fusion | bytes 262144 | tf_op jit(solution)/shard_map/squeeze | solution.py:249
  0.9 0.0 copy-start.2
  1.0 5.1 %collective-permute-start.2 = (bf16[64,512]{1,0:T(8,128)(2,1)S(1)}, bf16[64,512]{1,0:T(8,128)(2,1)S(1)}, u32[]{:S(2)}, u32[]{:S(2)}) collective-permute-start(bf16[64,512]{1,0:T(8,128)(2,1)S(1)} %fusion.1), channel_id=1, source_target_pairs={{0,12},{2,14},{4,8},{6,10},{8,4},{10,6},{12,0},{14,2},{1,13},{3,15... | collective-permute-start | bytes 196616 | tf_op jit(solution)/shard_map/ppermute | solution.py:22
  6.1 0.6 collective-permute-start
  6.7 1.2 %copy-done = f32[2,131072]{1,0:T(2,128)S(1)} copy-done((f32[2,131072]{1,0:T(2,128)S(1)}, f32[2,131072]{1,0:T(2,128)}, u32[]{:S(2)}) %copy-start) | copy-done | bytes 1048600
  7.9 1.3 %prepare.1.sorted_ref = bf16[512,512]{1,0:T(8,128)(2,1)S(1)} custom-call(s32[3,9]{1,0:T(4,128)S(1)} %add_select_fusion.bits_ref, f32[2048,128]{1,0:T(8,128)S(1)} %bitcast.32), custom_call_target="tpu_custom_call" | custom-call | flops 1073741824 | bytes 1048576 | tf_op jit(solution)/shard_map/prepare/pallas_call | solution.py:190
  9.2 0.0 copy-start.1
  9.3 2.4 %collective-permute-done.1 = bf16[64,512]{1,0:T(8,128)(2,1)S(1)} collective-permute-done((bf16[64,512]{1,0:T(8,128)(2,1)S(1)}, bf16[64,512]{1,0:T(8,128)(2,1)S(1)}, u32[]{:S(2)}, u32[]{:S(2)}) %collective-permute-start.1) | collective-permute-done | bytes 65568 | tf_op jit(solution)/shard_map/ppermute | solution.py:22
  11.7 0.0 collective-permute-done
  11.7 1.6 %collective-permute-start.3 = (bf16[256,512]{1,0:T(8,128)(2,1)S(1)}, bf16[256,512]{1,0:T(8,128)(2,1)S(1)}, u32[]{:S(2)}, u32[]{:S(2)}) collective-permute-start(bf16[256,512]{1,0:T(8,128)(2,1)S(1)} %pad_maximum_fusion.3.refs_0_), channel_id=1, source_target_pairs={{0,2},{2,0},{4,6},{6,4},{8,10},{10,8},{12,14},{14,12},{1,3},{3,1},... | collective-permute-start | bytes 786440 | tf_op jit(solution)/shard_map/ppermute | solution.py:22
  13.3 1.5 %collective-permute-start.4 = (bf16[256,512]{1,0:T(8,128)(2,1)S(1)}, bf16[256,512]{1,0:T(8,128)(2,1)S(1)}, u32[]{:S(2)}, u32[]{:S(2)}) collective-permute-start(bf16[256,512]{1,0:T(8,128)(2,1)S(1)} %pad_maximum_fusion.3.refs_0_), channel_id=1, source_target_pairs={{0,16},{16,0},{1,17},{17,1},{2,18},{18,2},{3,19},{19,3},{4,20},{20... | collective-permute-start | bytes 786440 | tf_op jit(solution)/shard_map/ppermute | solution.py:22
  14.8 1.5 %collective-permute-done.7.refs_5_ = bf16[256,512]{1,0:T(8,128)(2,1)S(1)} collective-permute-done((bf16[256,512]{1,0:T(8,128)(2,1)S(1)}, bf16[256,512]{1,0:T(8,128)(2,1)S(1)}, u32[]{:S(2)}, u32[]{:S(2)}) %collective-permute-start.7) | collective-permute-done | bytes 262176 | tf_op jit(solution)/shard_map/ppermute | solution.py:22
  16.3 2.7 %collective-permute-start.14 = (bf16[2,64,512]{2,1,0:T(8,128)(2,1)S(1)}, bf16[2,64,512]{2,1,0:T(8,128)(2,1)S(1)}, u32[]{:S(2)}, u32[]{:S(2)}) collective-permute-start(bf16[2,64,512]{2,1,0:T(8,128)(2,1)S(1)} %fusion), channel_id=1, source_target_pairs={{0,12},{2,14},{4,8},{6,10},{8,4},{10,6},{12,0},{14,2},{1,13},{3,15... | collective-permute-start | bytes 393224 | tf_op jit(solution)/shard_map/ppermute | solution.py:22
  19.0 1.7 %collective-permute-start.12 = (bf16[2,64,512]{2,1,0:T(8,128)(2,1)S(1)}, bf16[2,64,512]{2,1,0:T(8,128)(2,1)S(1)}, u32[]{:S(2)}, u32[]{:S(2)}) collective-permute-start(bf16[2,64,512]{2,1,0:T(8,128)(2,1)S(1)} %fusion), channel_id=1, source_target_pairs={{0,4},{2,6},{4,0},{6,2},{8,12},{10,14},{12,8},{14,10},{1,5},{3,7},... | collective-permute-start | bytes 393224 | tf_op jit(solution)/shard_map/ppermute | solution.py:22
  20.7 0.7 collective-permute-start.5
  21.4 1.6 %collective-permute-start.6 = (bf16[128,512]{1,0:T(8,128)(2,1)S(1)}, bf16[128,512]{1,0:T(8,128)(2,1)S(1)}, u32[]{:S(2)}, u32[]{:S(2)}) collective-permute-start(bf16[128,512]{1,0:T(8,128)(2,1)S(1)} %slice.35), channel_id=1, source_target_pairs={{0,2},{2,0},{4,6},{6,4},{8,10},{10,8},{12,14},{14,12},{1,3},{3,1},... | collective-permute-start | bytes 393224 | tf_op jit(solution)/shard_map/ppermute | solution.py:22
  23.0 0.1 pad_add_fusion.place_ref
  23.1 1.5 %collective-permute-done.14 = bf16[2,64,512]{2,1,0:T(8,128)(2,1)S(1)} collective-permute-done((bf16[2,64,512]{2,1,0:T(8,128)(2,1)S(1)}, bf16[2,64,512]{2,1,0:T(8,128)(2,1)S(1)}, u32[]{:S(2)}, u32[]{:S(2)}) %collective-permute-start.14) | collective-permute-done | bytes 131104 | tf_op jit(solution)/shard_map/ppermute | solution.py:22
  24.6 6.2 %collective-permute-done.13 = bf16[2,64,512]{2,1,0:T(8,128)(2,1)S(1)} collective-permute-done((bf16[2,64,512]{2,1,0:T(8,128)(2,1)S(1)}, bf16[2,64,512]{2,1,0:T(8,128)(2,1)S(1)}, u32[]{:S(2)}, u32[]{:S(2)}) %collective-permute-start.13) | collective-permute-done | bytes 131104 | tf_op jit(solution)/shard_map/ppermute | solution.py:22
  30.8 0.6 collective-permute-start.10
  31.4 0.0 collective-permute-done.6.refs_4_
  31.4 0.1 collective-permute-start.11
  31.5 0.6 collective-permute-start.15
  32.2 0.5 collective-permute-start.16
  32.7 0.0 collective-permute-done.9.refs_7_
  32.7 1.5 %collective-permute-start.20 = (bf16[256,512]{1,0:T(8,128)(2,1)S(1)}, bf16[256,512]{1,0:T(8,128)(2,1)S(1)}, u32[]{:S(2)}, u32[]{:S(2)}) collective-permute-start(bf16[256,512]{1,0:T(8,128)(2,1)S(1)} %get-tuple-element.11), channel_id=1, source_target_pairs={{0,16},{16,0},{1,17},{17,1},{2,18},{18,2},{3,19},{19,3},{4,20},{20... | collective-permute-start | bytes 786440 | tf_op jit(solution)/shard_map/ppermute | solution.py:22
  34.2 0.0 collective-permute-done.10.refs_8_
  34.2 1.5 %collective-permute-start.21 = (bf16[256,512]{1,0:T(8,128)(2,1)S(1)}, bf16[256,512]{1,0:T(8,128)(2,1)S(1)}, u32[]{:S(2)}, u32[]{:S(2)}) collective-permute-start(bf16[256,512]{1,0:T(8,128)(2,1)S(1)} %get-tuple-element.11), channel_id=1, source_target_pairs={{0,2},{2,0},{4,6},{6,4},{8,10},{10,8},{12,14},{14,12},{1,3},{3,1},... | collective-permute-start | bytes 786440 | tf_op jit(solution)/shard_map/ppermute | solution.py:22
  35.7 0.0 collective-permute-done.11.refs_9_
  35.7 1.9 %merge.3.branch_ref = bf16[1024,512]{1,0:T(8,128)(2,1)S(1)} custom-call(s32[3]{0:T(128)S(1)} %pad_add_fusion.place_ref, bf16[256,512]{1,0:T(8,128)(2,1)S(1)} %pad_maximum_fusion.3.refs_0_, bf16[256,512]{1,0:T(8,128)(2,1)S(1)} %collective-permute-done.3.refs_1_, bf16[256,512]{1,0:T(8,128)(2,1)S(1)} %collective-permute-done.4.refs_2_, ...), custom_call_target="tpu_custom_call" | custom-call | flops 1073741824 | bytes 3145728 | tf_op jit(solution)/shard_map/merge/pallas_call | solution.py:70
  37.6 2.6 %first.1 = bf16[1024,256]{1,0:T(8,128)(2,1)} custom-call(s32[3,9]{1,0:T(4,128)S(1)} %add_select_fusion.bits_ref, bf16[512,512]{1,0:T(8,128)(2,1)S(1)} %prepare.1.sorted_ref, bf16[1024,512]{1,0:T(8,128)(2,1)S(1)} %merge.3.branch_ref), custom_call_target="tpu_custom_call" | custom-call | flops 2147483648 | bytes 1048576 | tf_op jit(solution)/shard_map/first/pallas_call | solution.py:190
  40.3 3.6 %all-to-all-start = ((bf16[16,64,256]{2,1,0:T(8,128)(2,1)}), bf16[16,64,256]{2,1,0:T(8,128)(2,1)S(1)}, u32[]{:S(2)}, u32[]{:S(2)}) async-start(bf16[16,64,256]{2,1,0:T(8,128)(2,1)} %bitcast.8), calls=%async_computation | async-start | bytes 1048576 | tf_op jit(solution)/shard_map/all_to_all | solution.py:307
  43.9 0.0 collective-permute-done.15
  43.9 0.4 collective-permute-start.18
  44.3 0.5 collective-permute-start.17
  44.8 1.4 %collective-permute-done.20 = bf16[256,512]{1,0:T(8,128)(2,1)S(1)} collective-permute-done((bf16[256,512]{1,0:T(8,128)(2,1)S(1)}, bf16[256,512]{1,0:T(8,128)(2,1)S(1)}, u32[]{:S(2)}, u32[]{:S(2)}) %collective-permute-start.20) | collective-permute-done | bytes 262176 | tf_op jit(solution)/shard_map/ppermute | solution.py:22
  46.2 0.1 collective-permute-start.23
  46.3 1.6 %collective-permute-start.22 = (bf16[256,512]{1,0:T(8,128)(2,1)S(1)}, bf16[256,512]{1,0:T(8,128)(2,1)S(1)}, u32[]{:S(2)}, u32[]{:S(2)}) collective-permute-start(bf16[256,512]{1,0:T(8,128)(2,1)S(1)} %collective-permute-done.20), channel_id=1, source_target_pairs={{0,2},{2,0},{4,6},{6,4},{8,10},{10,8},{12,14},{14,12},{1,3},{3,1},... | collective-permute-start | bytes 786440 | tf_op jit(solution)/shard_map/ppermute | solution.py:22
  47.9 4.8 %collective-permute-done.17 = bf16[256,512]{1,0:T(8,128)(2,1)S(1)} collective-permute-done((bf16[256,512]{1,0:T(8,128)(2,1)S(1)}, bf16[256,512]{1,0:T(8,128)(2,1)S(1)}, u32[]{:S(2)}, u32[]{:S(2)}) %collective-permute-start.17) | collective-permute-done | bytes 262176 | tf_op jit(solution)/shard_map/ppermute | solution.py:22
  52.7 0.1 collective-permute-start.19
  52.8 4.6 %collective-permute-done.22 = bf16[256,512]{1,0:T(8,128)(2,1)S(1)} collective-permute-done((bf16[256,512]{1,0:T(8,128)(2,1)S(1)}, bf16[256,512]{1,0:T(8,128)(2,1)S(1)}, u32[]{:S(2)}, u32[]{:S(2)}) %collective-permute-start.22) | collective-permute-done | bytes 262176 | tf_op jit(solution)/shard_map/ppermute | solution.py:22
  57.5 0.1 collective-permute-start.24
  57.6 0.0 collective-permute-done.18.refs_2_
  57.6 1.9 %merge.4.branch1_ref = bf16[1024,512]{1,0:T(8,128)(2,1)S(1)} custom-call(s32[3]{0:T(128)S(1)} %pad_add_fusion.place_ref, bf16[512,512]{1,0:T(8,128)(2,1)S(1)} %pad_maximum_fusion.1.refs_0_, bf16[512,512]{1,0:T(8,128)(2,1)S(1)} %constant_dynamic-update-slice_fusion.refs_1_, bf16[512,512]{1,0:T(8,128)(2,1)S(1)} %collective-permute-done.18.refs_2_, ...), custom_call_target="tpu_custom_call" | custom-call | flops 1073741824 | bytes 3145728 | tf_op jit(solution)/shard_map/merge/pallas_call | solution.py:70
  59.5 1.9 %merge.5.branch2_ref = bf16[1024,512]{1,0:T(8,128)(2,1)S(1)} custom-call(s32[3]{0:T(128)S(1)} %pad_add_fusion.place_ref, bf16[512,512]{1,0:T(8,128)(2,1)S(1)} %pad_maximum_fusion.2.refs_0_, bf16[512,512]{1,0:T(8,128)(2,1)S(1)} %constant_dynamic-update-slice_fusion.2.refs_1_, bf16[512,512]{1,0:T(8,128)(2,1)S(1)} %collective-permute-done.23.refs_2_, ...), custom_call_target="tpu_custom_call" | custom-call | flops 1073741824 | bytes 3145728 | tf_op jit(solution)/shard_map/merge/pallas_call | solution.py:70
  61.5 3.7 %rest.1 = bf16[1024,256]{1,0:T(8,128)(2,1)S(1)} custom-call(s32[3,9]{1,0:T(4,128)S(1)} %add_select_fusion.bits_ref, bf16[1024,256]{1,0:T(8,128)(2,1)S(1)} %bitcast.30, bf16[1024,512]{1,0:T(8,128)(2,1)S(1)} %merge.4.branch1_ref, bf16[1024,512]{1,0:T(8,128)(2,1)S(1)} %merge.5.branch2_ref), custom_call_target="tpu_custom_call" | custom-call | flops 5368709120 | bytes 1048576 | tf_op jit(solution)/shard_map/rest/pallas_call | solution.py:190
  65.2 19.7 %all_to_all.10 = bf16[16,64,256]{2,1,0:T(8,128)(2,1)S(1)} all-to-all(bf16[16,64,256]{2,1,0:T(8,128)(2,1)S(1)} %bitcast.31), channel_id=1, replica_groups=mesh['cuts'=2,'wide'=8,'narrow'=2] {'wide','narrow'}, dimensions={0} | all-to-all | bytes 1048576 | tf_op jit(solution)/shard_map/all_to_all | solution.py:307
  85.0 1.0 %widen.1 = f32[2048,128]{1,0:T(8,128)} custom-call(bf16[1024,256]{1,0:T(8,128)(2,1)S(1)} %bitcast.29), custom_call_target="tpu_custom_call" | custom-call | tf_op jit(solution)/shard_map/widen/pallas_call | solution.py:213
  (35 shorter events, 0.3 us)
Async XLA Ops:
  0.9 5.8 %copy-start.2 = (s32[3,9]{1,0:T(4,128)S(1)}, s32[3,9]{1,0:T(4,128)}, u32[]{:S(2)}) copy-start(s32[3,9]{1,0:T(4,128)} %param.5) | copy-start | bytes 328
  1.0 8.3 %collective-permute-start.2 = (bf16[64,512]{1,0:T(8,128)(2,1)S(1)}, bf16[64,512]{1,0:T(8,128)(2,1)S(1)}, u32[]{:S(2)}, u32[]{:S(2)}) collective-permute-start(bf16[64,512]{1,0:T(8,128)(2,1)S(1)} %fusion.1), channel_id=1, source_target_pairs={{0,12},{2,14},{4,8},{6,10},{8,4},{10,6},{12,0},{14,2},{1,13},{3,15... | collective-permute-start | bytes 196616 | tf_op jit(solution)/shard_map/ppermute | solution.py:22
  6.1 5.6 %collective-permute-start.1 = (bf16[64,512]{1,0:T(8,128)(2,1)S(1)}, bf16[64,512]{1,0:T(8,128)(2,1)S(1)}, u32[]{:S(2)}, u32[]{:S(2)}) collective-permute-start(bf16[64,512]{1,0:T(8,128)(2,1)S(1)} %fusion.1), channel_id=1, source_target_pairs={{0,8},{2,10},{4,12},{6,14},{8,0},{10,2},{12,4},{14,6},{1,9},{3,11}... | collective-permute-start | bytes 196616 | tf_op jit(solution)/shard_map/ppermute | solution.py:22
  6.1 5.6 %collective-permute-start = (bf16[64,512]{1,0:T(8,128)(2,1)S(1)}, bf16[64,512]{1,0:T(8,128)(2,1)S(1)}, u32[]{:S(2)}, u32[]{:S(2)}) collective-permute-start(bf16[64,512]{1,0:T(8,128)(2,1)S(1)} %fusion.1), channel_id=1, source_target_pairs={{0,4},{2,6},{4,0},{6,2},{8,12},{10,14},{12,8},{14,10},{1,5},{3,7},... | collective-permute-start | bytes 196616 | tf_op jit(solution)/shard_map/ppermute | solution.py:22
  6.7 1.2 %copy-start = (f32[2,131072]{1,0:T(2,128)S(1)}, f32[2,131072]{1,0:T(2,128)}, u32[]{:S(2)}) copy-start(f32[2,131072]{1,0:T(2,128)} %param.3) | copy-start | bytes 3145732
  9.2 5.5 %copy-start.1 = (bf16[3,1,2,64,512]{4,3,2,1,0:T(8,128)(2,1)S(1)}, bf16[3,1,2,64,512]{4,3,2,1,0:T(8,128)(2,1)}, u32[]{:S(2)}) copy-start(bf16[3,1,2,64,512]{4,3,2,1,0:T(8,128)(2,1)} %param.4) | copy-start | bytes 1179652
  11.7 9.0 %collective-permute-start.3 = (bf16[256,512]{1,0:T(8,128)(2,1)S(1)}, bf16[256,512]{1,0:T(8,128)(2,1)S(1)}, u32[]{:S(2)}, u32[]{:S(2)}) collective-permute-start(bf16[256,512]{1,0:T(8,128)(2,1)S(1)} %pad_maximum_fusion.3.refs_0_), channel_id=1, source_target_pairs={{0,2},{2,0},{4,6},{6,4},{8,10},{10,8},{12,14},{14,12},{1,3},{3,1},... | collective-permute-start | bytes 786440 | tf_op jit(solution)/shard_map/ppermute | solution.py:22
  13.3 8.2 %collective-permute-start.4 = (bf16[256,512]{1,0:T(8,128)(2,1)S(1)}, bf16[256,512]{1,0:T(8,128)(2,1)S(1)}, u32[]{:S(2)}, u32[]{:S(2)}) collective-permute-start(bf16[256,512]{1,0:T(8,128)(2,1)S(1)} %pad_maximum_fusion.3.refs_0_), channel_id=1, source_target_pairs={{0,16},{16,0},{1,17},{17,1},{2,18},{18,2},{3,19},{19,3},{4,20},{20... | collective-permute-start | bytes 786440 | tf_op jit(solution)/shard_map/ppermute | solution.py:22
  14.8 1.5 %collective-permute-start.7 = (bf16[256,512]{1,0:T(8,128)(2,1)S(1)}, bf16[256,512]{1,0:T(8,128)(2,1)S(1)}, u32[]{:S(2)}, u32[]{:S(2)}) collective-permute-start(bf16[256,512]{1,0:T(8,128)(2,1)S(1)} %pad_maximum_fusion.3.refs_0_), channel_id=1, source_target_pairs={{0,1},{1,0},{2,3},{3,2},{4,5},{5,4},{6,7},{7,6},{8,9},{9,8},{10,11... | collective-permute-start | bytes 786440 | tf_op jit(solution)/shard_map/ppermute | solution.py:22
  16.3 8.2 %collective-permute-start.14 = (bf16[2,64,512]{2,1,0:T(8,128)(2,1)S(1)}, bf16[2,64,512]{2,1,0:T(8,128)(2,1)S(1)}, u32[]{:S(2)}, u32[]{:S(2)}) collective-permute-start(bf16[2,64,512]{2,1,0:T(8,128)(2,1)S(1)} %fusion), channel_id=1, source_target_pairs={{0,12},{2,14},{4,8},{6,10},{8,4},{10,6},{12,0},{14,2},{1,13},{3,15... | collective-permute-start | bytes 393224 | tf_op jit(solution)/shard_map/ppermute | solution.py:22
  19.0 11.8 %collective-permute-start.13 = (bf16[2,64,512]{2,1,0:T(8,128)(2,1)S(1)}, bf16[2,64,512]{2,1,0:T(8,128)(2,1)S(1)}, u32[]{:S(2)}, u32[]{:S(2)}) collective-permute-start(bf16[2,64,512]{2,1,0:T(8,128)(2,1)S(1)} %fusion), channel_id=1, source_target_pairs={{0,8},{2,10},{4,12},{6,14},{8,0},{10,2},{12,4},{14,6},{1,9},{3,11}... | collective-permute-start | bytes 393224 | tf_op jit(solution)/shard_map/ppermute | solution.py:22
  19.0 11.8 %collective-permute-start.12 = (bf16[2,64,512]{2,1,0:T(8,128)(2,1)S(1)}, bf16[2,64,512]{2,1,0:T(8,128)(2,1)S(1)}, u32[]{:S(2)}, u32[]{:S(2)}) collective-permute-start(bf16[2,64,512]{2,1,0:T(8,128)(2,1)S(1)} %fusion), channel_id=1, source_target_pairs={{0,4},{2,6},{4,0},{6,2},{8,12},{10,14},{12,8},{14,10},{1,5},{3,7},... | collective-permute-start | bytes 393224 | tf_op jit(solution)/shard_map/ppermute | solution.py:22
  20.7 10.1 %collective-permute-start.5 = (bf16[128,512]{1,0:T(8,128)(2,1)S(1)}, bf16[128,512]{1,0:T(8,128)(2,1)S(1)}, u32[]{:S(2)}, u32[]{:S(2)}) collective-permute-start(bf16[128,512]{1,0:T(8,128)(2,1)S(1)} %slice.34), channel_id=1, source_target_pairs={{0,16},{16,0},{1,17},{17,1},{2,18},{18,2},{3,19},{19,3},{4,20},{20... | collective-permute-start | bytes 393224 | tf_op jit(solution)/shard_map/ppermute | solution.py:22
  21.4 10.0 %collective-permute-start.6 = (bf16[128,512]{1,0:T(8,128)(2,1)S(1)}, bf16[128,512]{1,0:T(8,128)(2,1)S(1)}, u32[]{:S(2)}, u32[]{:S(2)}) collective-permute-start(bf16[128,512]{1,0:T(8,128)(2,1)S(1)} %slice.35), channel_id=1, source_target_pairs={{0,2},{2,0},{4,6},{6,4},{8,10},{10,8},{12,14},{14,12},{1,3},{3,1},... | collective-permute-start | bytes 393224 | tf_op jit(solution)/shard_map/ppermute | solution.py:22
  24.5 7.6 %collective-permute-start.8 = (bf16[256,512]{1,0:T(8,128)(2,1)S(1)}, bf16[256,512]{1,0:T(8,128)(2,1)S(1)}, u32[]{:S(2)}, u32[]{:S(2)}) collective-permute-start(bf16[256,512]{1,0:T(8,128)(2,1)S(1)} %collective-permute-done.3.refs_1_), channel_id=1, source_target_pairs={{0,1},{1,0},{2,3},{3,2},{4,5},{5,4},{6,7},{7,6},{8,9},{9,8},{10,11... | collective-permute-start | bytes 786440 | tf_op jit(solution)/shard_map/ppermute | solution.py:22
  30.8 1.9 %collective-permute-start.9 = (bf16[256,512]{1,0:T(8,128)(2,1)S(1)}, bf16[256,512]{1,0:T(8,128)(2,1)S(1)}, u32[]{:S(2)}, u32[]{:S(2)}) collective-permute-start(bf16[256,512]{1,0:T(8,128)(2,1)S(1)} %collective-permute-done.4.refs_2_), channel_id=1, source_target_pairs={{0,1},{1,0},{2,3},{3,2},{4,5},{5,4},{6,7},{7,6},{8,9},{9,8},{10,11... | collective-permute-start | bytes 786440 | tf_op jit(solution)/shard_map/ppermute | solution.py:22
  30.8 3.4 %collective-permute-start.10 = (bf16[128,512]{1,0:T(8,128)(2,1)S(1)}, bf16[128,512]{1,0:T(8,128)(2,1)S(1)}, u32[]{:S(2)}, u32[]{:S(2)}) collective-permute-start(bf16[128,512]{1,0:T(8,128)(2,1)S(1)} %collective-permute-done.5.refs_3_), channel_id=1, source_target_pairs={{0,1},{1,0},{2,3},{3,2},{4,5},{5,4},{6,7},{7,6},{8,9},{9,8},{10,11... | collective-permute-start | bytes 393224 | tf_op jit(solution)/shard_map/ppermute | solution.py:22
  31.4 4.3 %collective-permute-start.11 = (bf16[128,512]{1,0:T(8,128)(2,1)S(1)}, bf16[128,512]{1,0:T(8,128)(2,1)S(1)}, u32[]{:S(2)}, u32[]{:S(2)}) collective-permute-start(bf16[128,512]{1,0:T(8,128)(2,1)S(1)} %collective-permute-done.6.refs_4_), channel_id=1, source_target_pairs={{0,1},{1,0},{2,3},{3,2},{4,5},{5,4},{6,7},{7,6},{8,9},{9,8},{10,11... | collective-permute-start | bytes 393224 | tf_op jit(solution)/shard_map/ppermute | solution.py:22
  31.5 12.3 %collective-permute-start.15 = (bf16[256,512]{1,0:T(8,128)(2,1)S(1)}, bf16[256,512]{1,0:T(8,128)(2,1)S(1)}, u32[]{:S(2)}, u32[]{:S(2)}) collective-permute-start(bf16[256,512]{1,0:T(8,128)(2,1)S(1)} %get-tuple-element.12), channel_id=1, source_target_pairs={{0,2},{2,0},{4,6},{6,4},{8,10},{10,8},{12,14},{14,12},{1,3},{3,1},... | collective-permute-start | bytes 786440 | tf_op jit(solution)/shard_map/ppermute | solution.py:22
  32.2 14.1 %collective-permute-start.16 = (bf16[256,512]{1,0:T(8,128)(2,1)S(1)}, bf16[256,512]{1,0:T(8,128)(2,1)S(1)}, u32[]{:S(2)}, u32[]{:S(2)}) collective-permute-start(bf16[256,512]{1,0:T(8,128)(2,1)S(1)} %get-tuple-element.12), channel_id=1, source_target_pairs={{0,16},{16,0},{1,17},{17,1},{2,18},{18,2},{3,19},{19,3},{4,20},{20... | collective-permute-start | bytes 786440 | tf_op jit(solution)/shard_map/ppermute | solution.py:22
  32.7 13.5 %collective-permute-start.20 = (bf16[256,512]{1,0:T(8,128)(2,1)S(1)}, bf16[256,512]{1,0:T(8,128)(2,1)S(1)}, u32[]{:S(2)}, u32[]{:S(2)}) collective-permute-start(bf16[256,512]{1,0:T(8,128)(2,1)S(1)} %get-tuple-element.11), channel_id=1, source_target_pairs={{0,16},{16,0},{1,17},{17,1},{2,18},{18,2},{3,19},{19,3},{4,20},{20... | collective-permute-start | bytes 786440 | tf_op jit(solution)/shard_map/ppermute | solution.py:22
  34.2 13.6 %collective-permute-start.21 = (bf16[256,512]{1,0:T(8,128)(2,1)S(1)}, bf16[256,512]{1,0:T(8,128)(2,1)S(1)}, u32[]{:S(2)}, u32[]{:S(2)}) collective-permute-start(bf16[256,512]{1,0:T(8,128)(2,1)S(1)} %get-tuple-element.11), channel_id=1, source_target_pairs={{0,2},{2,0},{4,6},{6,4},{8,10},{10,8},{12,14},{14,12},{1,3},{3,1},... | collective-permute-start | bytes 786440 | tf_op jit(solution)/shard_map/ppermute | solution.py:22
  40.3 21.2 %all-to-all-start = ((bf16[16,64,256]{2,1,0:T(8,128)(2,1)}), bf16[16,64,256]{2,1,0:T(8,128)(2,1)S(1)}, u32[]{:S(2)}, u32[]{:S(2)}) async-start(bf16[16,64,256]{2,1,0:T(8,128)(2,1)} %bitcast.8), calls=%async_computation | async-start | bytes 1048576 | tf_op jit(solution)/shard_map/all_to_all | solution.py:307
  43.9 13.6 %collective-permute-start.18 = (bf16[512,512]{1,0:T(8,128)(2,1)S(1)}, bf16[512,512]{1,0:T(8,128)(2,1)S(1)}, u32[]{:S(2)}, u32[]{:S(2)}) collective-permute-start(bf16[512,512]{1,0:T(8,128)(2,1)S(1)} %pad_maximum_fusion.1.refs_0_), channel_id=1, source_target_pairs={{0,1},{1,0},{2,3},{3,2},{4,5},{5,4},{6,7},{7,6},{8,9},{9,8},{10,11... | collective-permute-start | bytes 1572872 | tf_op jit(solution)/shard_map/ppermute | solution.py:22
  44.3 8.4 %collective-permute-start.17 = (bf16[256,512]{1,0:T(8,128)(2,1)S(1)}, bf16[256,512]{1,0:T(8,128)(2,1)S(1)}, u32[]{:S(2)}, u32[]{:S(2)}) collective-permute-start(bf16[256,512]{1,0:T(8,128)(2,1)S(1)} %collective-permute-done.15), channel_id=1, source_target_pairs={{0,16},{16,0},{1,17},{17,1},{2,18},{18,2},{3,19},{19,3},{4,20},{20... | collective-permute-start | bytes 786440 | tf_op jit(solution)/shard_map/ppermute | solution.py:22
  46.2 13.3 %collective-permute-start.23 = (bf16[512,512]{1,0:T(8,128)(2,1)S(1)}, bf16[512,512]{1,0:T(8,128)(2,1)S(1)}, u32[]{:S(2)}, u32[]{:S(2)}) collective-permute-start(bf16[512,512]{1,0:T(8,128)(2,1)S(1)} %pad_maximum_fusion.2.refs_0_), channel_id=1, source_target_pairs={{0,1},{1,0},{2,3},{3,2},{4,5},{5,4},{6,7},{7,6},{8,9},{9,8},{10,11... | collective-permute-start | bytes 1572872 | tf_op jit(solution)/shard_map/ppermute | solution.py:22
  46.3 11.2 %collective-permute-start.22 = (bf16[256,512]{1,0:T(8,128)(2,1)S(1)}, bf16[256,512]{1,0:T(8,128)(2,1)S(1)}, u32[]{:S(2)}, u32[]{:S(2)}) collective-permute-start(bf16[256,512]{1,0:T(8,128)(2,1)S(1)} %collective-permute-done.20), channel_id=1, source_target_pairs={{0,2},{2,0},{4,6},{6,4},{8,10},{10,8},{12,14},{14,12},{1,3},{3,1},... | collective-permute-start | bytes 786440 | tf_op jit(solution)/shard_map/ppermute | solution.py:22
  52.7 4.8 %collective-permute-start.19 = (bf16[512,512]{1,0:T(8,128)(2,1)S(1)}, bf16[512,512]{1,0:T(8,128)(2,1)S(1)}, u32[]{:S(2)}, u32[]{:S(2)}) collective-permute-start(bf16[512,512]{1,0:T(8,128)(2,1)S(1)} %constant_dynamic-update-slice_fusion.refs_1_), channel_id=1, source_target_pairs={{0,1},{1,0},{2,3},{3,2},{4,5},{5,4},{6,7},{7,6},{8,9},{9,8},{10,11... | collective-permute-start | bytes 1572872 | tf_op jit(solution)/shard_map/ppermute | solution.py:22
  57.5 2.1 %collective-permute-start.24 = (bf16[512,512]{1,0:T(8,128)(2,1)S(1)}, bf16[512,512]{1,0:T(8,128)(2,1)S(1)}, u32[]{:S(2)}, u32[]{:S(2)}) collective-permute-start(bf16[512,512]{1,0:T(8,128)(2,1)S(1)} %constant_dynamic-update-slice_fusion.2.refs_1_), channel_id=1, source_target_pairs={{0,1},{1,0},{2,3},{3,2},{4,5},{5,4},{6,7},{7,6},{8,9},{9,8},{10,11... | collective-permute-start | bytes 1572872 | tf_op jit(solution)/shard_map/ppermute | solution.py:22

commit v5 on v3

--- a/solution.py
+++ b/solution.py
@@ -276,6 +276,8 @@
 
     def mine(first, last):
         own = sub_branches[first:last, 0]
+        if first == 0:
+            return lax.dynamic_index_in_dim(own, part, axis=1, keepdims=False)
         return jnp.where(part == 0, own[:, 0], own[:, 1])
 
     def blocks(masks, wide_mask, part_mask):
@@ -283,7 +285,7 @@
 
     sides = [(0, 0), (1, 0), (0, 1), (1, 1)]
     layout = [blocks(even, *side) for side in sides]
-    near0 = after(along(mine(0, 1)[0]), ready)
+    near0 = along(mine(0, 1)[0])
     near0_other = from_other_core([near0])
     x0, y0 = exchange(near0, "wide", 1), exchange(near0, "cuts", 1)
     half = near0.shape[0] // 2

time: 84.9 us -> 84.9 us (level)
    unnamed x8 -> x6, local copies, waits for them, and re-layouts: 1.28 us -> 0.05 us
    slice x0 -> x2, local copies, waits for them, and re-layouts: none -> 0.9 us  [mine(): own = sub_branches[first:last, 0]]
  transfers between devices with their start and end apart: 26 -> 26, of which waited for: 6 -> 7; matrix products, arithmetic and copies ran while one was open for 0% -> 2% of each run, Pallas kernels for 12% -> 12%
where the time goes in v5:
time: 84.9 us; the launch traced here: 84.6 us
  starting transfers between devices  27.9 us (33%)
  blocking collectives  19.9 us (23%)
  waiting for transfers between devices  19.7 us (23%)
  Pallas kernels  14.5 us (17%)
  local copies, waits for them, and re-layouts  2.01 us (2%)
    ppermute x25, starting transfers between devices, exchange(): return lax.ppermute(value, axis, pairs)  24.4 us
    all_to_all x1, blocking collectives, swap(): blocks = lax.all_to_all(blocks, ('wide', 'narrow'), 0, 0, tiled=True)  19.9 us
    ppermute x25, waiting for transfers between devices, exchange(): return lax.ppermute(value, axis, pairs)  19.7 us
    pallas_call x3, Pallas kernels, contract(): pl.pallas_call(kernel, out_shape=jax.ShapeDtypeStruct(shape, jnp.bfloat16...  7.69 us
    pallas_call x3, Pallas kernels, merge(): pl.pallas_call(functools.partial(merge_kernel, layout, block_rows), out_s...  5.79 us
    all_to_all x1, starting transfers between devices, swap(): blocks = lax.all_to_all(blocks, ('wide', 'narrow'), 0, 0, tiled=True)  3.57 us
  transfers between devices with their start and end apart: 26, of which 7 were waited for; matrix products, arithmetic and copies ran while one was open for 2% of the time, Pallas kernels for 12%

profile of v5, /device:TPU:0, one launch (start us, length us, event | category | flops | bytes accessed | tf_op | source)
XLA Modules:
  0.0 84.6 jit_solution(10349795596582572051)
XLA Ops:
  0.0 0.9 %slice-done = bf16[1,1,2,64,512]{4,3,2,1,0:T(8,128)(2,1)S(1)} async-done(((bf16[3,1,2,64,512]{4,3,2,1,0:T(8,128)(2,1)}), bf16[1,1,2,64,512]{4,3,2,1,0:T(8,128)(2,1)S(1)}, s32[]{:S(2)}) %slice-start) | async-done | bytes 131096 | tf_op jit(solution)/shard_map/slice | solution.py:278
  0.9 5.1 %collective-permute-start.2 = (bf16[64,512]{1,0:T(8,128)(2,1)S(1)}, bf16[64,512]{1,0:T(8,128)(2,1)S(1)}, u32[]{:S(2)}, u32[]{:S(2)}) collective-permute-start(bf16[64,512]{1,0:T(8,128)(2,1)S(1)} %dynamic-slice_bitcast_fusion), channel_id=1, source_target_pairs={{0,12},{2,14},{4,8},{6,10},{8,4},{10,6},{12,0},{14,2},{1,13},{3,15... | collective-permute-start | bytes 196616 | tf_op jit(solution)/shard_map/ppermute | solution.py:23
  6.0 0.0 collective-permute-start.1
  6.0 0.6 collective-permute-start
  6.7 1.0 %copy_bitcast_fusion = bf16[2,2,64,512]{3,2,0,1:T(8,128)(2,1)S(1)} fusion(bf16[3,1,2,64,512]{4,3,2,1,0:T(8,128)(2,1)} %param.4), kind=kLoop, calls=%fused_computation.4 | loop fusion | bytes 524288 | tf_op jit(solution)/shard_map/squeeze | solution.py:278
  7.6 1.0 %collective-permute-done.2 = bf16[64,512]{1,0:T(8,128)(2,1)S(1)} collective-permute-done((bf16[64,512]{1,0:T(8,128)(2,1)S(1)}, bf16[64,512]{1,0:T(8,128)(2,1)S(1)}, u32[]{:S(2)}, u32[]{:S(2)}) %collective-permute-start.2) | collective-permute-done | bytes 65568 | tf_op jit(solution)/shard_map/ppermute | solution.py:23
  8.6 3.0 %collective-permute-done.1 = bf16[64,512]{1,0:T(8,128)(2,1)S(1)} collective-permute-done((bf16[64,512]{1,0:T(8,128)(2,1)S(1)}, bf16[64,512]{1,0:T(8,128)(2,1)S(1)}, u32[]{:S(2)}, u32[]{:S(2)}) %collective-permute-start.1) | collective-permute-done | bytes 65568 | tf_op jit(solution)/shard_map/ppermute | solution.py:23
  11.7 0.1 collective-permute-start.7
  11.8 0.0 copy-start.1
  11.8 1.6 %collective-permute-start.3 = (bf16[256,512]{1,0:T(8,128)(2,1)S(1)}, bf16[256,512]{1,0:T(8,128)(2,1)S(1)}, u32[]{:S(2)}, u32[]{:S(2)}) collective-permute-start(bf16[256,512]{1,0:T(8,128)(2,1)S(1)} %pad_maximum_fusion.3.refs_0_), channel_id=1, source_target_pairs={{0,2},{2,0},{4,6},{6,4},{8,10},{10,8},{12,14},{14,12},{1,3},{3,1},... | collective-permute-start | bytes 786440 | tf_op jit(solution)/shard_map/ppermute | solution.py:23
  13.3 1.5 %collective-permute-start.4 = (bf16[256,512]{1,0:T(8,128)(2,1)S(1)}, bf16[256,512]{1,0:T(8,128)(2,1)S(1)}, u32[]{:S(2)}, u32[]{:S(2)}) collective-permute-start(bf16[256,512]{1,0:T(8,128)(2,1)S(1)} %pad_maximum_fusion.3.refs_0_), channel_id=1, source_target_pairs={{0,16},{16,0},{1,17},{17,1},{2,18},{18,2},{3,19},{19,3},{4,20},{20... | collective-permute-start | bytes 786440 | tf_op jit(solution)/shard_map/ppermute | solution.py:23
  14.9 0.0 collective-permute-done.7.refs_5_
  14.9 2.8 %collective-permute-start.14 = (bf16[2,64,512]{2,1,0:T(8,128)(2,1)S(1)}, bf16[2,64,512]{2,1,0:T(8,128)(2,1)S(1)}, u32[]{:S(2)}, u32[]{:S(2)}) collective-permute-start(bf16[2,64,512]{2,1,0:T(8,128)(2,1)S(1)} %fusion), channel_id=1, source_target_pairs={{0,12},{2,14},{4,8},{6,10},{8,4},{10,6},{12,0},{14,2},{1,13},{3,15... | collective-permute-start | bytes 393224 | tf_op jit(solution)/shard_map/ppermute | solution.py:23
  17.6 1.7 %collective-permute-start.12 = (bf16[2,64,512]{2,1,0:T(8,128)(2,1)S(1)}, bf16[2,64,512]{2,1,0:T(8,128)(2,1)S(1)}, u32[]{:S(2)}, u32[]{:S(2)}) collective-permute-start(bf16[2,64,512]{2,1,0:T(8,128)(2,1)S(1)} %fusion), channel_id=1, source_target_pairs={{0,4},{2,6},{4,0},{6,2},{8,12},{10,14},{12,8},{14,10},{1,5},{3,7},... | collective-permute-start | bytes 393224 | tf_op jit(solution)/shard_map/ppermute | solution.py:23
  19.3 0.1 pad_add_fusion.place_ref
  19.4 1.1 %collective-permute-done.3.refs_1_ = bf16[256,512]{1,0:T(8,128)(2,1)S(1)} collective-permute-done((bf16[256,512]{1,0:T(8,128)(2,1)S(1)}, bf16[256,512]{1,0:T(8,128)(2,1)S(1)}, u32[]{:S(2)}, u32[]{:S(2)}) %collective-permute-start.3) | collective-permute-done | bytes 262176 | tf_op jit(solution)/shard_map/ppermute | solution.py:23
  20.6 1.6 %collective-permute-start.5 = (bf16[128,512]{1,0:T(8,128)(2,1)S(1)}, bf16[128,512]{1,0:T(8,128)(2,1)S(1)}, u32[]{:S(2)}, u32[]{:S(2)}) collective-permute-start(bf16[128,512]{1,0:T(8,128)(2,1)S(1)} %slice.24), channel_id=1, source_target_pairs={{0,16},{16,0},{1,17},{17,1},{2,18},{18,2},{3,19},{19,3},{4,20},{20... | collective-permute-start | bytes 393224 | tf_op jit(solution)/shard_map/ppermute | solution.py:23
  22.2 1.6 %collective-permute-start.6 = (bf16[128,512]{1,0:T(8,128)(2,1)S(1)}, bf16[128,512]{1,0:T(8,128)(2,1)S(1)}, u32[]{:S(2)}, u32[]{:S(2)}) collective-permute-start(bf16[128,512]{1,0:T(8,128)(2,1)S(1)} %slice.25), channel_id=1, source_target_pairs={{0,2},{2,0},{4,6},{6,4},{8,10},{10,8},{12,14},{14,12},{1,3},{3,1},... | collective-permute-start | bytes 393224 | tf_op jit(solution)/shard_map/ppermute | solution.py:23
  23.7 1.3 %prepare.1.sorted_ref = bf16[512,512]{1,0:T(8,128)(2,1)S(1)} custom-call(s32[3,9]{1,0:T(4,128)S(1)} %add_select_fusion.bits_ref, s32[3]{0:T(128)S(1)} %pad_add_fusion.place_ref, f32[2048,128]{1,0:T(8,128)S(1)} %bitcast.30), custom_call_target="tpu_custom_call" | custom-call | flops 1073741824 | bytes 1048576 | tf_op jit(solution)/shard_map/prepare/pallas_call | solution.py:219
  25.0 0.0 collective-permute-done.14
  25.0 0.1 collective-permute-start.8
  25.1 4.1 %collective-permute-done.13 = bf16[2,64,512]{2,1,0:T(8,128)(2,1)S(1)} collective-permute-done((bf16[2,64,512]{2,1,0:T(8,128)(2,1)S(1)}, bf16[2,64,512]{2,1,0:T(8,128)(2,1)S(1)}, u32[]{:S(2)}, u32[]{:S(2)}) %collective-permute-start.13) | collective-permute-done | bytes 131104 | tf_op jit(solution)/shard_map/ppermute | solution.py:23
  29.2 0.0 collective-permute-start.9
  29.3 0.6 collective-permute-start.10
  29.8 0.0 collective-permute-done.6.refs_4_
  29.8 0.1 collective-permute-start.11
  30.0 0.6 collective-permute-start.15
  30.6 0.0 collective-permute-done.8.refs_6_
  30.6 1.0 %collective-permute-start.16 = (bf16[256,512]{1,0:T(8,128)(2,1)S(1)}, bf16[256,512]{1,0:T(8,128)(2,1)S(1)}, u32[]{:S(2)}, u32[]{:S(2)}) collective-permute-start(bf16[256,512]{1,0:T(8,128)(2,1)S(1)} %get-tuple-element.10), channel_id=1, source_target_pairs={{0,16},{16,0},{1,17},{17,1},{2,18},{18,2},{3,19},{19,3},{4,20},{20... | collective-permute-start | bytes 786440 | tf_op jit(solution)/shard_map/ppermute | solution.py:23
  31.6 1.0 %collective-permute-start.20 = (bf16[256,512]{1,0:T(8,128)(2,1)S(1)}, bf16[256,512]{1,0:T(8,128)(2,1)S(1)}, u32[]{:S(2)}, u32[]{:S(2)}) collective-permute-start(bf16[256,512]{1,0:T(8,128)(2,1)S(1)} %get-tuple-element.9), channel_id=1, source_target_pairs={{0,16},{16,0},{1,17},{17,1},{2,18},{18,2},{3,19},{19,3},{4,20},{20... | collective-permute-start | bytes 786440 | tf_op jit(solution)/shard_map/ppermute | solution.py:23
  32.6 1.5 %collective-permute-start.21 = (bf16[256,512]{1,0:T(8,128)(2,1)S(1)}, bf16[256,512]{1,0:T(8,128)(2,1)S(1)}, u32[]{:S(2)}, u32[]{:S(2)}) collective-permute-start(bf16[256,512]{1,0:T(8,128)(2,1)S(1)} %get-tuple-element.9), channel_id=1, source_target_pairs={{0,2},{2,0},{4,6},{6,4},{8,10},{10,8},{12,14},{14,12},{1,3},{3,1},... | collective-permute-start | bytes 786440 | tf_op jit(solution)/shard_map/ppermute | solution.py:23
  34.1 1.9 %merge.3.branch_ref = bf16[1024,512]{1,0:T(8,128)(2,1)S(1)} custom-call(s32[3]{0:T(128)S(1)} %pad_add_fusion.place_ref, bf16[256,512]{1,0:T(8,128)(2,1)S(1)} %pad_maximum_fusion.3.refs_0_, bf16[256,512]{1,0:T(8,128)(2,1)S(1)} %collective-permute-done.3.refs_1_, bf16[256,512]{1,0:T(8,128)(2,1)S(1)} %collective-permute-done.4.refs_2_, ...), custom_call_target="tpu_custom_call" | custom-call | flops 1073741824 | bytes 3145728 | tf_op jit(solution)/shard_map/merge/pallas_call | solution.py:71
  36.1 2.7 %first.1 = bf16[1024,256]{1,0:T(8,128)(2,1)} custom-call(s32[3,9]{1,0:T(4,128)S(1)} %add_select_fusion.bits_ref, s32[3]{0:T(128)S(1)} %pad_add_fusion.place_ref, bf16[512,512]{1,0:T(8,128)(2,1)S(1)} %prepare.1.sorted_ref, bf16[1024,512]{1,0:T(8,128)(2,1)S(1)} %merge.3.branch_ref), custom_call_target="tpu_custom_call" | custom-call | flops 2147483648 | bytes 1048576 | tf_op jit(solution)/shard_map/first/pallas_call | solution.py:219
  38.7 3.6 %all-to-all-start = ((bf16[16,64,256]{2,1,0:T(8,128)(2,1)}), bf16[16,64,256]{2,1,0:T(8,128)(2,1)S(1)}, u32[]{:S(2)}, u32[]{:S(2)}) async-start(bf16[16,64,256]{2,1,0:T(8,128)(2,1)} %bitcast.7), calls=%async_computation | async-start | bytes 1048576 | tf_op jit(solution)/shard_map/all_to_all | solution.py:342
  42.3 0.4 collective-permute-start.18
  42.7 0.9 %collective-permute-start.17 = (bf16[256,512]{1,0:T(8,128)(2,1)S(1)}, bf16[256,512]{1,0:T(8,128)(2,1)S(1)}, u32[]{:S(2)}, u32[]{:S(2)}) collective-permute-start(bf16[256,512]{1,0:T(8,128)(2,1)S(1)} %collective-permute-done.15), channel_id=1, source_target_pairs={{0,16},{16,0},{1,17},{17,1},{2,18},{18,2},{3,19},{19,3},{4,20},{20... | collective-permute-start | bytes 786440 | tf_op jit(solution)/shard_map/ppermute | solution.py:23
  43.6 1.0 %collective-permute-done.20 = bf16[256,512]{1,0:T(8,128)(2,1)S(1)} collective-permute-done((bf16[256,512]{1,0:T(8,128)(2,1)S(1)}, bf16[256,512]{1,0:T(8,128)(2,1)S(1)}, u32[]{:S(2)}, u32[]{:S(2)}) %collective-permute-start.20) | collective-permute-done | bytes 262176 | tf_op jit(solution)/shard_map/ppermute | solution.py:23
  44.6 0.1 collective-permute-start.23
  44.7 1.6 %collective-permute-start.22 = (bf16[256,512]{1,0:T(8,128)(2,1)S(1)}, bf16[256,512]{1,0:T(8,128)(2,1)S(1)}, u32[]{:S(2)}, u32[]{:S(2)}) collective-permute-start(bf16[256,512]{1,0:T(8,128)(2,1)S(1)} %collective-permute-done.20), channel_id=1, source_target_pairs={{0,2},{2,0},{4,6},{6,4},{8,10},{10,8},{12,14},{14,12},{1,3},{3,1},... | collective-permute-start | bytes 786440 | tf_op jit(solution)/shard_map/ppermute | solution.py:23
  46.3 4.8 %collective-permute-done.17 = bf16[256,512]{1,0:T(8,128)(2,1)S(1)} collective-permute-done((bf16[256,512]{1,0:T(8,128)(2,1)S(1)}, bf16[256,512]{1,0:T(8,128)(2,1)S(1)}, u32[]{:S(2)}, u32[]{:S(2)}) %collective-permute-start.17) | collective-permute-done | bytes 262176 | tf_op jit(solution)/shard_map/ppermute | solution.py:23
  51.2 0.1 collective-permute-start.19
  51.2 4.6 %collective-permute-done.22 = bf16[256,512]{1,0:T(8,128)(2,1)S(1)} collective-permute-done((bf16[256,512]{1,0:T(8,128)(2,1)S(1)}, bf16[256,512]{1,0:T(8,128)(2,1)S(1)}, u32[]{:S(2)}, u32[]{:S(2)}) %collective-permute-start.22) | collective-permute-done | bytes 262176 | tf_op jit(solution)/shard_map/ppermute | solution.py:23
  55.9 0.1 collective-permute-start.24
  56.0 1.9 %merge.4.branch1_ref = bf16[1024,512]{1,0:T(8,128)(2,1)S(1)} custom-call(s32[3]{0:T(128)S(1)} %pad_add_fusion.place_ref, bf16[512,512]{1,0:T(8,128)(2,1)S(1)} %pad_maximum_fusion.1.refs_0_, bf16[512,512]{1,0:T(8,128)(2,1)S(1)} %constant_dynamic-update-slice_fusion.refs_1_, bf16[512,512]{1,0:T(8,128)(2,1)S(1)} %collective-permute-done.18.refs_2_, ...), custom_call_target="tpu_custom_call" | custom-call | flops 1073741824 | bytes 3145728 | tf_op jit(solution)/shard_map/merge/pallas_call | solution.py:71
  58.0 1.9 %merge.5.branch2_ref = bf16[1024,512]{1,0:T(8,128)(2,1)S(1)} custom-call(s32[3]{0:T(128)S(1)} %pad_add_fusion.place_ref, bf16[512,512]{1,0:T(8,128)(2,1)S(1)} %pad_maximum_fusion.2.refs_0_, bf16[512,512]{1,0:T(8,128)(2,1)S(1)} %constant_dynamic-update-slice_fusion.2.refs_1_, bf16[512,512]{1,0:T(8,128)(2,1)S(1)} %collective-permute-done.23.refs_2_, ...), custom_call_target="tpu_custom_call" | custom-call | flops 1073741824 | bytes 3145728 | tf_op jit(solution)/shard_map/merge/pallas_call | solution.py:71
  59.9 3.7 %rest.1 = bf16[1024,256]{1,0:T(8,128)(2,1)S(1)} custom-call(s32[3,9]{1,0:T(4,128)S(1)} %add_select_fusion.bits_ref, s32[3]{0:T(128)S(1)} %pad_add_fusion.place_ref, bf16[1024,256]{1,0:T(8,128)(2,1)S(1)} %bitcast.28, bf16[1024,512]{1,0:T(8,128)(2,1)S(1)} %merge.4.branch1_ref, bf16[1024,512]{1,0:T(8,128)(2,1)S(1)} %merge.5.branch2_ref), custom_call_target="tpu_custom_call" | custom-call | flops 5368709120 | bytes 1048576 | tf_op jit(solution)/shard_map/rest/pallas_call | solution.py:219
  63.6 19.9 %all_to_all.10 = bf16[16,64,256]{2,1,0:T(8,128)(2,1)S(1)} all-to-all(bf16[16,64,256]{2,1,0:T(8,128)(2,1)S(1)} %bitcast.29), channel_id=1, replica_groups=mesh['cuts'=2,'wide'=8,'narrow'=2] {'wide','narrow'}, dimensions={0} | all-to-all | bytes 1048576 | tf_op jit(solution)/shard_map/all_to_all | solution.py:342
  83.5 1.0 %widen.1 = f32[2048,128]{1,0:T(8,128)} custom-call(bf16[1024,256]{1,0:T(8,128)(2,1)S(1)} %bitcast.27), custom_call_target="tpu_custom_call" | custom-call | tf_op jit(solution)/shard_map/widen/pallas_call | solution.py:242
  (34 shorter events, 0.3 us)
Async XLA Ops:
  0.0 0.9 %slice-start = ((bf16[3,1,2,64,512]{4,3,2,1,0:T(8,128)(2,1)}), bf16[1,1,2,64,512]{4,3,2,1,0:T(8,128)(2,1)S(1)}, s32[]{:S(2)}) async-start(bf16[3,1,2,64,512]{4,3,2,1,0:T(8,128)(2,1)} %param.4), calls=%async_computation.2 | async-start | bytes 262144 | tf_op jit(solution)/shard_map/slice | solution.py:278
  0.9 22.8 %copy-start = (f32[2,131072]{1,0:T(2,128)S(1)}, f32[2,131072]{1,0:T(2,128)}, u32[]{:S(2)}) copy-start(f32[2,131072]{1,0:T(2,128)} %param.3) | copy-start | bytes 3145732
  0.9 7.7 %collective-permute-start.2 = (bf16[64,512]{1,0:T(8,128)(2,1)S(1)}, bf16[64,512]{1,0:T(8,128)(2,1)S(1)}, u32[]{:S(2)}, u32[]{:S(2)}) collective-permute-start(bf16[64,512]{1,0:T(8,128)(2,1)S(1)} %dynamic-slice_bitcast_fusion), channel_id=1, source_target_pairs={{0,12},{2,14},{4,8},{6,10},{8,4},{10,6},{12,0},{14,2},{1,13},{3,15... | collective-permute-start | bytes 196616 | tf_op jit(solution)/shard_map/ppermute | solution.py:23
  6.0 5.6 %collective-permute-start.1 = (bf16[64,512]{1,0:T(8,128)(2,1)S(1)}, bf16[64,512]{1,0:T(8,128)(2,1)S(1)}, u32[]{:S(2)}, u32[]{:S(2)}) collective-permute-start(bf16[64,512]{1,0:T(8,128)(2,1)S(1)} %dynamic-slice_bitcast_fusion), channel_id=1, source_target_pairs={{0,8},{2,10},{4,12},{6,14},{8,0},{10,2},{12,4},{14,6},{1,9},{3,11}... | collective-permute-start | bytes 196616 | tf_op jit(solution)/shard_map/ppermute | solution.py:23
  6.0 5.6 %collective-permute-start = (bf16[64,512]{1,0:T(8,128)(2,1)S(1)}, bf16[64,512]{1,0:T(8,128)(2,1)S(1)}, u32[]{:S(2)}, u32[]{:S(2)}) collective-permute-start(bf16[64,512]{1,0:T(8,128)(2,1)S(1)} %dynamic-slice_bitcast_fusion), channel_id=1, source_target_pairs={{0,4},{2,6},{4,0},{6,2},{8,12},{10,14},{12,8},{14,10},{1,5},{3,7},... | collective-permute-start | bytes 196616 | tf_op jit(solution)/shard_map/ppermute | solution.py:23
  11.7 3.2 %collective-permute-start.7 = (bf16[256,512]{1,0:T(8,128)(2,1)S(1)}, bf16[256,512]{1,0:T(8,128)(2,1)S(1)}, u32[]{:S(2)}, u32[]{:S(2)}) collective-permute-start(bf16[256,512]{1,0:T(8,128)(2,1)S(1)} %pad_maximum_fusion.3.refs_0_), channel_id=1, source_target_pairs={{0,1},{1,0},{2,3},{3,2},{4,5},{5,4},{6,7},{7,6},{8,9},{9,8},{10,11... | collective-permute-start | bytes 786440 | tf_op jit(solution)/shard_map/ppermute | solution.py:23
  11.8 3.1 %copy-start.1 = (s32[3,9]{1,0:T(4,128)S(1)}, s32[3,9]{1,0:T(4,128)}, u32[]{:S(2)}) copy-start(s32[3,9]{1,0:T(4,128)} %param.5) | copy-start | bytes 328
  11.8 8.8 %collective-permute-start.3 = (bf16[256,512]{1,0:T(8,128)(2,1)S(1)}, bf16[256,512]{1,0:T(8,128)(2,1)S(1)}, u32[]{:S(2)}, u32[]{:S(2)}) collective-permute-start(bf16[256,512]{1,0:T(8,128)(2,1)S(1)} %pad_maximum_fusion.3.refs_0_), channel_id=1, source_target_pairs={{0,2},{2,0},{4,6},{6,4},{8,10},{10,8},{12,14},{14,12},{1,3},{3,1},... | collective-permute-start | bytes 786440 | tf_op jit(solution)/shard_map/ppermute | solution.py:23
  13.3 8.8 %collective-permute-start.4 = (bf16[256,512]{1,0:T(8,128)(2,1)S(1)}, bf16[256,512]{1,0:T(8,128)(2,1)S(1)}, u32[]{:S(2)}, u32[]{:S(2)}) collective-permute-start(bf16[256,512]{1,0:T(8,128)(2,1)S(1)} %pad_maximum_fusion.3.refs_0_), channel_id=1, source_target_pairs={{0,16},{16,0},{1,17},{17,1},{2,18},{18,2},{3,19},{19,3},{4,20},{20... | collective-permute-start | bytes 786440 | tf_op jit(solution)/shard_map/ppermute | solution.py:23
  14.9 10.2 %collective-permute-start.14 = (bf16[2,64,512]{2,1,0:T(8,128)(2,1)S(1)}, bf16[2,64,512]{2,1,0:T(8,128)(2,1)S(1)}, u32[]{:S(2)}, u32[]{:S(2)}) collective-permute-start(bf16[2,64,512]{2,1,0:T(8,128)(2,1)S(1)} %fusion), channel_id=1, source_target_pairs={{0,12},{2,14},{4,8},{6,10},{8,4},{10,6},{12,0},{14,2},{1,13},{3,15... | collective-permute-start | bytes 393224 | tf_op jit(solution)/shard_map/ppermute | solution.py:23
  17.6 11.6 %collective-permute-start.13 = (bf16[2,64,512]{2,1,0:T(8,128)(2,1)S(1)}, bf16[2,64,512]{2,1,0:T(8,128)(2,1)S(1)}, u32[]{:S(2)}, u32[]{:S(2)}) collective-permute-start(bf16[2,64,512]{2,1,0:T(8,128)(2,1)S(1)} %fusion), channel_id=1, source_target_pairs={{0,8},{2,10},{4,12},{6,14},{8,0},{10,2},{12,4},{14,6},{1,9},{3,11}... | collective-permute-start | bytes 393224 | tf_op jit(solution)/shard_map/ppermute | solution.py:23
  17.6 11.6 %collective-permute-start.12 = (bf16[2,64,512]{2,1,0:T(8,128)(2,1)S(1)}, bf16[2,64,512]{2,1,0:T(8,128)(2,1)S(1)}, u32[]{:S(2)}, u32[]{:S(2)}) collective-permute-start(bf16[2,64,512]{2,1,0:T(8,128)(2,1)S(1)} %fusion), channel_id=1, source_target_pairs={{0,4},{2,6},{4,0},{6,2},{8,12},{10,14},{12,8},{14,10},{1,5},{3,7},... | collective-permute-start | bytes 393224 | tf_op jit(solution)/shard_map/ppermute | solution.py:23
  20.6 8.7 %collective-permute-start.5 = (bf16[128,512]{1,0:T(8,128)(2,1)S(1)}, bf16[128,512]{1,0:T(8,128)(2,1)S(1)}, u32[]{:S(2)}, u32[]{:S(2)}) collective-permute-start(bf16[128,512]{1,0:T(8,128)(2,1)S(1)} %slice.24), channel_id=1, source_target_pairs={{0,16},{16,0},{1,17},{17,1},{2,18},{18,2},{3,19},{19,3},{4,20},{20... | collective-permute-start | bytes 393224 | tf_op jit(solution)/shard_map/ppermute | solution.py:23
  22.2 7.7 %collective-permute-start.6 = (bf16[128,512]{1,0:T(8,128)(2,1)S(1)}, bf16[128,512]{1,0:T(8,128)(2,1)S(1)}, u32[]{:S(2)}, u32[]{:S(2)}) collective-permute-start(bf16[128,512]{1,0:T(8,128)(2,1)S(1)} %slice.25), channel_id=1, source_target_pairs={{0,2},{2,0},{4,6},{6,4},{8,10},{10,8},{12,14},{14,12},{1,3},{3,1},... | collective-permute-start | bytes 393224 | tf_op jit(solution)/shard_map/ppermute | solution.py:23
  25.0 5.5 %collective-permute-start.8 = (bf16[256,512]{1,0:T(8,128)(2,1)S(1)}, bf16[256,512]{1,0:T(8,128)(2,1)S(1)}, u32[]{:S(2)}, u32[]{:S(2)}) collective-permute-start(bf16[256,512]{1,0:T(8,128)(2,1)S(1)} %collective-permute-done.3.refs_1_), channel_id=1, source_target_pairs={{0,1},{1,0},{2,3},{3,2},{4,5},{5,4},{6,7},{7,6},{8,9},{9,8},{10,11... | collective-permute-start | bytes 786440 | tf_op jit(solution)/shard_map/ppermute | solution.py:23
  29.2 2.4 %collective-permute-start.9 = (bf16[256,512]{1,0:T(8,128)(2,1)S(1)}, bf16[256,512]{1,0:T(8,128)(2,1)S(1)}, u32[]{:S(2)}, u32[]{:S(2)}) collective-permute-start(bf16[256,512]{1,0:T(8,128)(2,1)S(1)} %collective-permute-done.4.refs_2_), channel_id=1, source_target_pairs={{0,1},{1,0},{2,3},{3,2},{4,5},{5,4},{6,7},{7,6},{8,9},{9,8},{10,11... | collective-permute-start | bytes 786440 | tf_op jit(solution)/shard_map/ppermute | solution.py:23
  29.3 3.3 %collective-permute-start.10 = (bf16[128,512]{1,0:T(8,128)(2,1)S(1)}, bf16[128,512]{1,0:T(8,128)(2,1)S(1)}, u32[]{:S(2)}, u32[]{:S(2)}) collective-permute-start(bf16[128,512]{1,0:T(8,128)(2,1)S(1)} %collective-permute-done.5.refs_3_), channel_id=1, source_target_pairs={{0,1},{1,0},{2,3},{3,2},{4,5},{5,4},{6,7},{7,6},{8,9},{9,8},{10,11... | collective-permute-start | bytes 393224 | tf_op jit(solution)/shard_map/ppermute | solution.py:23
  29.8 4.3 %collective-permute-start.11 = (bf16[128,512]{1,0:T(8,128)(2,1)S(1)}, bf16[128,512]{1,0:T(8,128)(2,1)S(1)}, u32[]{:S(2)}, u32[]{:S(2)}) collective-permute-start(bf16[128,512]{1,0:T(8,128)(2,1)S(1)} %collective-permute-done.6.refs_4_), channel_id=1, source_target_pairs={{0,1},{1,0},{2,3},{3,2},{4,5},{5,4},{6,7},{7,6},{8,9},{9,8},{10,11... | collective-permute-start | bytes 393224 | tf_op jit(solution)/shard_map/ppermute | solution.py:23
  30.0 12.3 %collective-permute-start.15 = (bf16[256,512]{1,0:T(8,128)(2,1)S(1)}, bf16[256,512]{1,0:T(8,128)(2,1)S(1)}, u32[]{:S(2)}, u32[]{:S(2)}) collective-permute-start(bf16[256,512]{1,0:T(8,128)(2,1)S(1)} %get-tuple-element.10), channel_id=1, source_target_pairs={{0,2},{2,0},{4,6},{6,4},{8,10},{10,8},{12,14},{14,12},{1,3},{3,1},... | collective-permute-start | bytes 786440 | tf_op jit(solution)/shard_map/ppermute | solution.py:23
  30.6 14.1 %collective-permute-start.16 = (bf16[256,512]{1,0:T(8,128)(2,1)S(1)}, bf16[256,512]{1,0:T(8,128)(2,1)S(1)}, u32[]{:S(2)}, u32[]{:S(2)}) collective-permute-start(bf16[256,512]{1,0:T(8,128)(2,1)S(1)} %get-tuple-element.10), channel_id=1, source_target_pairs={{0,16},{16,0},{1,17},{17,1},{2,18},{18,2},{3,19},{19,3},{4,20},{20... | collective-permute-start | bytes 786440 | tf_op jit(solution)/shard_map/ppermute | solution.py:23
  31.6 13.0 %collective-permute-start.20 = (bf16[256,512]{1,0:T(8,128)(2,1)S(1)}, bf16[256,512]{1,0:T(8,128)(2,1)S(1)}, u32[]{:S(2)}, u32[]{:S(2)}) collective-permute-start(bf16[256,512]{1,0:T(8,128)(2,1)S(1)} %get-tuple-element.9), channel_id=1, source_target_pairs={{0,16},{16,0},{1,17},{17,1},{2,18},{18,2},{3,19},{19,3},{4,20},{20... | collective-permute-start | bytes 786440 | tf_op jit(solution)/shard_map/ppermute | solution.py:23
  32.6 13.7 %collective-permute-start.21 = (bf16[256,512]{1,0:T(8,128)(2,1)S(1)}, bf16[256,512]{1,0:T(8,128)(2,1)S(1)}, u32[]{:S(2)}, u32[]{:S(2)}) collective-permute-start(bf16[256,512]{1,0:T(8,128)(2,1)S(1)} %get-tuple-element.9), channel_id=1, source_target_pairs={{0,2},{2,0},{4,6},{6,4},{8,10},{10,8},{12,14},{14,12},{1,3},{3,1},... | collective-permute-start | bytes 786440 | tf_op jit(solution)/shard_map/ppermute | solution.py:23
  38.7 21.2 %all-to-all-start = ((bf16[16,64,256]{2,1,0:T(8,128)(2,1)}), bf16[16,64,256]{2,1,0:T(8,128)(2,1)S(1)}, u32[]{:S(2)}, u32[]{:S(2)}) async-start(bf16[16,64,256]{2,1,0:T(8,128)(2,1)} %bitcast.7), calls=%async_computation | async-start | bytes 1048576 | tf_op jit(solution)/shard_map/all_to_all | solution.py:342
  42.3 13.6 %collective-permute-start.18 = (bf16[512,512]{1,0:T(8,128)(2,1)S(1)}, bf16[512,512]{1,0:T(8,128)(2,1)S(1)}, u32[]{:S(2)}, u32[]{:S(2)}) collective-permute-start(bf16[512,512]{1,0:T(8,128)(2,1)S(1)} %pad_maximum_fusion.1.refs_0_), channel_id=1, source_target_pairs={{0,1},{1,0},{2,3},{3,2},{4,5},{5,4},{6,7},{7,6},{8,9},{9,8},{10,11... | collective-permute-start | bytes 1572872 | tf_op jit(solution)/shard_map/ppermute | solution.py:23
  42.7 8.4 %collective-permute-start.17 = (bf16[256,512]{1,0:T(8,128)(2,1)S(1)}, bf16[256,512]{1,0:T(8,128)(2,1)S(1)}, u32[]{:S(2)}, u32[]{:S(2)}) collective-permute-start(bf16[256,512]{1,0:T(8,128)(2,1)S(1)} %collective-permute-done.15), channel_id=1, source_target_pairs={{0,16},{16,0},{1,17},{17,1},{2,18},{18,2},{3,19},{19,3},{4,20},{20... | collective-permute-start | bytes 786440 | tf_op jit(solution)/shard_map/ppermute | solution.py:23
  44.6 13.3 %collective-permute-start.23 = (bf16[512,512]{1,0:T(8,128)(2,1)S(1)}, bf16[512,512]{1,0:T(8,128)(2,1)S(1)}, u32[]{:S(2)}, u32[]{:S(2)}) collective-permute-start(bf16[512,512]{1,0:T(8,128)(2,1)S(1)} %pad_maximum_fusion.2.refs_0_), channel_id=1, source_target_pairs={{0,1},{1,0},{2,3},{3,2},{4,5},{5,4},{6,7},{7,6},{8,9},{9,8},{10,11... | collective-permute-start | bytes 1572872 | tf_op jit(solution)/shard_map/ppermute | solution.py:23
  44.7 11.2 %collective-permute-start.22 = (bf16[256,512]{1,0:T(8,128)(2,1)S(1)}, bf16[256,512]{1,0:T(8,128)(2,1)S(1)}, u32[]{:S(2)}, u32[]{:S(2)}) collective-permute-start(bf16[256,512]{1,0:T(8,128)(2,1)S(1)} %collective-permute-done.20), channel_id=1, source_target_pairs={{0,2},{2,0},{4,6},{6,4},{8,10},{10,8},{12,14},{14,12},{1,3},{3,1},... | collective-permute-start | bytes 786440 | tf_op jit(solution)/shard_map/ppermute | solution.py:23
  51.2 4.8 %collective-permute-start.19 = (bf16[512,512]{1,0:T(8,128)(2,1)S(1)}, bf16[512,512]{1,0:T(8,128)(2,1)S(1)}, u32[]{:S(2)}, u32[]{:S(2)}) collective-permute-start(bf16[512,512]{1,0:T(8,128)(2,1)S(1)} %constant_dynamic-update-slice_fusion.refs_1_), channel_id=1, source_target_pairs={{0,1},{1,0},{2,3},{3,2},{4,5},{5,4},{6,7},{7,6},{8,9},{9,8},{10,11... | collective-permute-start | bytes 1572872 | tf_op jit(solution)/shard_map/ppermute | solution.py:23
  55.9 2.1 %collective-permute-start.24 = (bf16[512,512]{1,0:T(8,128)(2,1)S(1)}, bf16[512,512]{1,0:T(8,128)(2,1)S(1)}, u32[]{:S(2)}, u32[]{:S(2)}) collective-permute-start(bf16[512,512]{1,0:T(8,128)(2,1)S(1)} %constant_dynamic-update-slice_fusion.2.refs_1_), channel_id=1, source_target_pairs={{0,1},{1,0},{2,3},{3,2},{4,5},{5,4},{6,7},{7,6},{8,9},{9,8},{10,11... | collective-permute-start | bytes 1572872 | tf_op jit(solution)/shard_map/ppermute | solution.py:23
